TPU v7x, 32 devices: a whole 2x2x4 slice. The times are simulated.
32 devices in a mesh: row: 4 (over z), col: 8 (over y, x, core).
Axes of the slice: x: 2, y: 2, z: 4, core: 2. Of those that a mesh axis runs over, the one named last changes fastest.
Arguments:
- object_field: float32 [2, 1024, 2048], P(None, 'row', 'col'), may hold values from -4 to 4
- probe_field: float32 [2, 256, 256], replicated, may hold values from -6 to 6
- measured: float32 [16, 2048, 256], P('row', 'col'), may hold values from 0.1 to 4
- positions: int32 [16, 16], P('row', 'col'), may hold values from 0 to 160
Outputs:
- new_object: float32 [2, 1024, 2048], P(None, 'row', 'col')
- new_probe: float32 [2, 256, 256], replicated
Inputs may be any that keep to these rules, and one draw needn't show every extreme that they name: `positions`: each entry is a pixel offset of a window's top-left corner within its device's tile.
All inputs are finite; a program needn't handle non-finite values.
Results may differ from a plain program's by a relative error of at most 0.0003.
Values sent between devices are 32-bit elements; how exact they have to be, the bound alone decides.
No kernel may reach another device: no remote copies, remote signals or barrier semaphores. Data moves between devices by JAX's collectives and lax.ppermute only.
A program may use at most 64 MiB of HBM per device.

v0:
```python
import math

import jax
import jax.numpy as jnp
import numpy as np
from jax import lax
from jax.experimental import pallas as pl
from jax.experimental.pallas import tpu as pltpu
from jax.sharding import PartitionSpec as P

HALO = 160
VMEM = pl.BlockSpec(memory_space=pltpu.VMEM)
SMEM = pl.BlockSpec(memory_space=pltpu.SMEM)
PARAMS = pltpu.CompilerParams(vmem_limit_bytes=24 * 1024 * 1024)
BF16 = jnp.bfloat16


def shifted(value, axis, steps):
    count = lax.axis_size(axis)
    initial, last = (max(0, -steps), min(count, count - steps))
    return lax.ppermute(value, axis, [(source, source + steps) for source in range(initial, last)])


def f32(*shape):
    return jax.ShapeDtypeStruct(shape, jnp.float32)


def cost(flops, moved):
    return pl.CostEstimate(flops=flops, bytes_accessed=moved, transcendentals=0)


def tables(side):
    half = side // 2
    index = np.arange(half)
    angle = 2.0 * math.pi / half * (np.outer(index, index) % half)
    cos = np.cos(angle) / math.sqrt(side)
    sin = -np.sin(angle) / math.sqrt(side)
    matrix = np.block([[cos, sin], [-sin, cos]])
    high = matrix.astype(BF16)
    low = (matrix - high.astype(np.float64)).astype(BF16)
    turn = -2.0 * math.pi / side * index
    twiddle = np.stack([np.cos(turn), np.sin(turn)]).astype(np.float32)
    lanes = np.ascontiguousarray(np.broadcast_to(twiddle[:, None, :], (2, 8, half)))
    rows = np.ascontiguousarray(np.broadcast_to(twiddle[:, :, None], (2, half, half)))
    pick = np.concatenate([np.arange(0, side, 2), np.arange(1, side, 2)])
    sort = np.zeros((side, side), np.float32)
    sort[pick, np.arange(side)] = 1.0
    return (
        np.concatenate([high, high, low], 0),
        np.concatenate([high.T, high.T, low.T], 1),
        np.concatenate([high.T, high.T, low.T], 0),
        np.concatenate([high, high, low], 1),
        lanes,
        rows,
        np.stack([sort, sort.T]).astype(BF16),
    )


def dot(left, right):
    return jnp.dot(left, right, preferred_element_type=jnp.float32)


def halves(value):
    high = value.astype(BF16)
    low = (value - high.astype(jnp.float32)).astype(BF16)
    return high, low


def pack_extra(rows, extra, width):
    per = width // extra
    for group in range(rows // 8):
        yield group * 8, group // per * 8, group % per * extra


def pack_kernel(tile_ref, near_ref, far_ref, right_ref):
    margin = far_ref.shape[1]
    side = tile_ref.shape[1]
    half = far_ref.shape[2]
    extra = margin - half
    near_ref[:, 0:margin, :] = tile_ref[:, 0:margin, 0:half]
    far_ref[...] = tile_ref[:, 0:margin, half:]
    right_ref[:, 0:side, :] = tile_ref[:, :, 0:half]
    for row, packed, lane in pack_extra(side, extra, half):
        piece = tile_ref[:, row : row + 8, half:margin]
        right_ref[:, side + packed : side + packed + 8, lane : lane + extra] = piece
        if row < margin:
            near_ref[:, margin + packed : margin + packed + 8, lane : lane + extra] = piece


def turned(load, steps, half, lanes):
    within = lax.rem(steps, half)
    first = lax.rem(lax.div(steps, half), 2)
    back = lax.rem(half - within, half)
    one = pltpu.roll(load(first), back, 1)
    two = pltpu.roll(load(1 - first), back, 1)
    stay = lanes < half - within
    return jnp.where(stay, one, two), jnp.where(stay, two, one)


def prepare_kernel(pos_ref, probe_ref, meas_ref, sort_ref, prot_ref, sorted_ref, twice):
    frames, side = meas_ref.shape[0], meas_ref.shape[1]
    half = side // 2
    for part in range(2):
        for tile in range(2):
            piece = probe_ref[part, :, tile * half : (tile + 1) * half]
            twice[part, tile, 0:side] = piece
            twice[part, tile, side : 2 * side] = piece
    step = 64
    lanes = lax.broadcasted_iota(jnp.int32, (step, half), 1)

    @pl.loop(0, frames)
    def _(frame):
        dy = pos_ref[0, frame]
        dx = pos_ref[1, frame]
        for part in range(2):
            for row in range(0, side, step):
                one, two = turned(
                    lambda tile: twice[part, tile, pl.ds(side - dy + row, step), :], side - dx, half, lanes
                )
                prot_ref[frame, part, row : row + step, 0:half] = one
                prot_ref[frame, part, row : row + step, half:side] = two
        value = meas_ref[frame]
        total = None
        for _ in range(3):
            piece = value.astype(BF16)
            value = value - piece.astype(jnp.float32)
            term = dot(dot(sort_ref[1], piece).astype(BF16), sort_ref[0])
            total = term if total is None else total + term
        sorted_ref[frame] = total


def frame_kernel(
    pos_ref, tile_ref, right_ref, near_ref, far_ref, corner_ref, prot_ref, meas_ref,
    fwd_right, fwd_left, inv_right, inv_left, lane_ref, row_ref,
    gt_ref, gr_ref, gz_ref, qs_ref, max_ref,
    right_extra, corner_extra, obj_ref, left_in, right_in, mid, twice,
):
    frames, side = meas_ref.shape[0], meas_ref.shape[1]
    half = side // 2
    margin = far_ref.shape[1]
    extra = margin - half
    for row, packed, lane in pack_extra(side, extra, half):
        right_extra[:, row : row + 8, 0:extra] = right_ref[:, side + packed : side + packed + 8, lane : lane + extra]
        if row < margin:
            corner_extra[:, row : row + 8, 0:extra] = corner_ref[
                :, margin + packed : margin + packed + 8, lane : lane + extra
            ]
    lane_cos, lane_sin = lane_ref[0, 0:1], lane_ref[1, 0:1]

    def store_left(where, rows, tile, value):
        high, low = halves(value)
        lane = tile * half
        left_in[where, rows, lane : lane + half] = high
        left_in[where, rows, side + lane : side + lane + half] = low
        left_in[where, rows, 2 * side + lane : 2 * side + lane + half] = high

    def store_right(where, row, count, columns, value):
        high, low = halves(value)
        right_in[where, row : row + count, columns] = high
        right_in[where, side + row : side + row + count, columns] = low
        right_in[where, 2 * side + row : 2 * side + row + count, columns] = high

    step = 32
    lanes = lax.broadcasted_iota(jnp.int32, (step, half), 1)
    row_in = lax.broadcasted_iota(jnp.int32, (step, half), 0)
    largest = jnp.zeros((step, half), jnp.float32)
    for frame in range(frames):
        dy = pos_ref[0, frame]
        dx = pos_ref[1, frame]
        own_col = (lanes >= dx, lanes + half >= dx)
        for row in range(0, side, step):
            rows = slice(row, row + step)
            own_row = row_in + row >= dy
            wave = []
            for tile in range(2):
                columns = slice(tile * half, (tile + 1) * half)
                obj = []
                for part in range(2):
                    right = right_extra[part, rows] if tile else right_ref[part, rows]
                    value = jnp.where(own_col[tile], tile_ref[part, rows, columns], right)
                    if row < margin:
                        below = far_ref[part, rows] if tile else near_ref[part, rows]
                        corner = corner_extra[part, rows] if tile else corner_ref[part, rows]
                        value = jnp.where(own_row, value, jnp.where(own_col[tile], below, corner))
                    obj_ref[frame, part, rows, columns] = value
                    obj.append(value)
                pro_re = prot_ref[frame, 0, rows, columns]
                pro_im = prot_ref[frame, 1, rows, columns]
                if frame == 0:
                    largest = jnp.maximum(largest, pro_re * pro_re + pro_im * pro_im)
                wave.append((pro_re * obj[0] - pro_im * obj[1], pro_re * obj[1] + pro_im * obj[0]))
            (re0, im0), (re1, im1) = wave
            store_left(2 * frame, rows, 0, re0 + re1)
            store_left(2 * frame, rows, 1, im0 + im1)
            re, im = re0 - re1, im0 - im1
            store_left(2 * frame + 1, rows, 0, re * lane_cos - im * lane_sin)
            store_left(2 * frame + 1, rows, 1, re * lane_sin + im * lane_cos)
        for which in range(2):
            mid[2 * frame + which] = dot(left_in[2 * frame + which], fwd_right[...])
    max_ref[0, 0] = jnp.max(largest)

    for frame in range(frames):
        for row in range(0, half, step):
            top, low = slice(row, row + step), slice(half + row, half + row + step)
            row_cos, row_sin = row_ref[0, top], row_ref[1, top]
            for which in range(2):
                columns = slice(which * half, (which + 1) * half)
                top_re, top_im = mid[2 * frame + which, top, 0:half], mid[2 * frame + which, top, half:side]
                low_re, low_im = mid[2 * frame + which, low, 0:half], mid[2 * frame + which, low, half:side]
                store_right(2 * frame, row, step, columns, top_re + low_re)
                store_right(2 * frame, half + row, step, columns, top_im + low_im)
                re, im = top_re - low_re, top_im - low_im
                store_right(2 * frame + 1, row, step, columns, re * row_cos - im * row_sin)
                store_right(2 * frame + 1, half + row, step, columns, re * row_sin + im * row_cos)
        for which in range(2):
            mid[2 * frame + which] = dot(fwd_left[...], right_in[2 * frame + which])

    for frame in range(frames):
        for which in range(2):
            for row in range(0, half, step):
                re = mid[2 * frame + which, row : row + step]
                im = mid[2 * frame + which, half + row : half + row + step]
                ampl = meas_ref[frame, which * half + row : which * half + row + step]
                factor = ampl * lax.rsqrt(jnp.maximum(re * re + im * im, 0.25)) - 1.0
                store_right(2 * frame + which, row, step, slice(0, side), factor * re)
                store_right(2 * frame + which, half + row, step, slice(0, side), factor * im)
            mid[2 * frame + which] = dot(inv_left[...], right_in[2 * frame + which])

    for frame in range(frames):
        for row in range(0, half, step):
            top, low = slice(row, row + step), slice(half + row, half + row + step)
            row_cos, row_sin = row_ref[0, top], row_ref[1, top]
            for which in range(2):
                columns = slice(which * half, (which + 1) * half)
                even_re, even_im = mid[2 * frame, top, columns], mid[2 * frame, low, columns]
                odd_re, odd_im = mid[2 * frame + 1, top, columns], mid[2 * frame + 1, low, columns]
                re = odd_re * row_cos + odd_im * row_sin
                im = odd_im * row_cos - odd_re * row_sin
                store_left(2 * frame + which, top, 0, even_re + re)
                store_left(2 * frame + which, top, 1, even_im + im)
                store_left(2 * frame + which, low, 0, even_re - re)
                store_left(2 * frame + which, low, 1, even_im - im)
        for which in range(2):
            mid[2 * frame + which] = dot(left_in[2 * frame + which], inv_right[...])

    step = 8
    lanes = lax.broadcasted_iota(jnp.int32, (step, half), 1)
    row_in = lax.broadcasted_iota(jnp.int32, (step, half), 0)
    places = {row: (packed, lane) for row, packed, lane in pack_extra(side, extra, half)}
    for row in range(0, side, step):
        rows = slice(row, row + step)
        total = {}
        for frame in range(frames):
            dy = pos_ref[0, frame]
            dx = pos_ref[1, frame]
            own_row = row_in + row >= dy
            even_re, even_im = mid[2 * frame, rows, 0:half], mid[2 * frame, rows, half:side]
            odd_re, odd_im = mid[2 * frame + 1, rows, 0:half], mid[2 * frame + 1, rows, half:side]
            re = odd_re * lane_cos + odd_im * lane_sin
            im = odd_im * lane_cos - odd_re * lane_sin
            for tile in range(2):
                columns = slice(tile * half, (tile + 1) * half)
                chi_re = even_re - re if tile else even_re + re
                chi_im = even_im - im if tile else even_im + im
                own_col = lanes + tile * half >= dx
                pro_re = prot_ref[frame, 0, rows, columns]
                pro_im = prot_ref[frame, 1, rows, columns]
                obj_re = obj_ref[frame, 0, rows, columns]
                obj_im = obj_ref[frame, 1, rows, columns]
                for part, value in enumerate(
                    (pro_re * chi_re + pro_im * chi_im, pro_re * chi_im - pro_im * chi_re)
                ):
                    own = value
                    pieces = []
                    if row < margin:
                        own = jnp.where(own_row, value, 0.0)
                        other = jnp.where(own_row, 0.0, value)
                        pieces.append(("b", jnp.where(own_col, other, 0.0)))
                        pieces.append(("c", jnp.where(own_col, 0.0, other)))
                    pieces.append(("t", jnp.where(own_col, own, 0.0)))
                    pieces.append(("r", jnp.where(own_col, 0.0, own)))
                    for name, piece in pieces:
                        key = (name, part, tile)
                        total[key] = piece if frame == 0 else total[key] + piece
                for index, value in enumerate(
                    (
                        obj_re * chi_re + obj_im * chi_im,
                        obj_re * chi_im - obj_im * chi_re,
                        obj_re * obj_re + obj_im * obj_im,
                    )
                ):
                    twice[frame, index, tile, row : row + step] = value
                    twice[frame, index, tile, side + row : side + row + step] = value
        packed, lane = places[row]
        for part in range(2):
            gt_ref[part, rows, 0:half] = total["t", part, 0]
            gt_ref[part, rows, half:side] = total["t", part, 1]
            gr_ref[part, rows] = total["r", part, 0]
            gr_ref[part, side + packed : side + packed + 8, lane : lane + extra] = total["r", part, 1][:, 0:extra]
            if row < margin:
                gz_ref[part, rows] = total["b", part, 0]
                gz_ref[part, margin + row : margin + row + step] = total["b", part, 1]
                base = 2 * margin
                gz_ref[part, base + row : base + row + step] = total["c", part, 0]
                base = 3 * margin + packed
                gz_ref[part, base : base + 8, lane : lane + extra] = total["c", part, 1][:, 0:extra]

    depth = qs_ref.shape[2]
    step = min(32, depth)
    lanes = lax.broadcasted_iota(jnp.int32, (step, half), 1)
    for row in range(0, side, step):
        for index in range(3):
            sums = None
            for frame in range(frames):
                dy = pos_ref[0, frame]
                dx = pos_ref[1, frame]
                pair = turned(
                    lambda tile: twice[frame, index, tile, pl.ds(dy + row, step), :], dx, half, lanes
                )
                sums = pair if sums is None else (sums[0] + pair[0], sums[1] + pair[1])
            place = slice(row % depth, row % depth + step)
            qs_ref[row // depth, index, place, 0:half] = sums[0]
            qs_ref[row // depth, index, place, half:side] = sums[1]


def finish_kernel(max_ref, tile_ref, grad_ref, right_ref, down_ref, out_ref):
    side = tile_ref.shape[1]
    half = side // 2
    rows = right_ref.shape[1]
    extra = (rows - side) * half // side
    margin = half + extra
    scale = 1.0 / max_ref[0, 0]
    step = 8
    for row, packed, lane in pack_extra(side, extra, half):
        place = slice(row, row + step)
        for part in range(2):
            one = grad_ref[part, place, 0:half] + right_ref[part, place]
            two = grad_ref[part, place, half:side]
            if row < margin:
                one = one + down_ref[part, place]
                two = two + down_ref[part, margin + row : margin + row + step]
            out_ref[part, place, 0:half] = tile_ref[part, place, 0:half] + one * scale
            out_ref[part, place, half:side] = tile_ref[part, place, half:side] + two * scale
            piece = right_ref[part, side + packed : side + packed + 8, lane : lane + extra]
            out_ref[part, place, half:margin] += piece * scale


def body(object_field, probe_field, measured, positions):
    side = probe_field.shape[1]
    half = side // 2
    margin = HALO
    extra = margin - half
    frames = measured.shape[0]
    n_row, n_col = lax.axis_size("row"), lax.axis_size("col")
    fwd_right, fwd_left, inv_right, inv_left, lane_tw, row_tw, sort = tables(side)
    wide = side + side * extra // half
    tall = margin + margin * extra // half

    near, far, right = pl.pallas_call(
        pack_kernel,
        out_shape=(f32(2, tall, half), f32(2, margin, half), f32(2, wide, half)),
        in_specs=[VMEM],
        out_specs=(VMEM,) * 3,
        cost_estimate=cost(10**6, 2 * 10**6),
        compiler_params=PARAMS,
    )(object_field)
    near = shifted(near, "row", -1)
    far = shifted(far, "row", -1)
    right = shifted(right, "col", -1)
    corner = shifted(near, "col", -1)
    places = positions.T
    prot, ampl = pl.pallas_call(
        prepare_kernel,
        out_shape=(f32(frames, 2, side, side), f32(frames, side, side)),
        in_specs=[SMEM, VMEM, VMEM, VMEM],
        out_specs=(VMEM, VMEM),
        scratch_shapes=[pltpu.VMEM((2, 2, 2 * side, half), jnp.float32)],
        cost_estimate=cost(3 * 10**9, 6 * 10**6),
        compiler_params=PARAMS,
    )(places, probe_field, measured, sort)
    depth = side // n_col
    g_tile, g_right, g_down, sums, largest = pl.pallas_call(
        frame_kernel,
        out_shape=(
            f32(2, side, side),
            f32(2, wide, half),
            f32(2, 2 * margin + tall, half),
            f32(n_col, 3, depth, side),
            f32(1, 1),
        ),
        in_specs=[SMEM] + [VMEM] * 13,
        out_specs=(VMEM,) * 4 + (SMEM,),
        scratch_shapes=[
            pltpu.VMEM((2, side, half), jnp.float32),
            pltpu.VMEM((2, margin, half), jnp.float32),
            pltpu.VMEM((frames, 2, side, side), jnp.float32),
            pltpu.VMEM((2 * frames, side, 3 * side), BF16),
            pltpu.VMEM((2 * frames, 3 * side, side), BF16),
            pltpu.VMEM((2 * frames, side, side), jnp.float32),
            pltpu.VMEM((frames, 3, 2, 2 * side, half), jnp.float32),
        ],
        cost_estimate=cost(6 * 10**9, 12 * 10**6),
        compiler_params=PARAMS,
    )(
        places, object_field, right, near, far, corner, prot, ampl,
        fwd_right, fwd_left, inv_right, inv_left, lane_tw, row_tw,
    )

    from_above = shifted(g_down, "row", 1)
    part = jnp.sum(lax.all_to_all(sums, "col", 0, 0), 0)
    g_corner = from_above[:, 2 * margin :]
    g_right, part, g_corner = lax.optimization_barrier((g_right, part, g_corner))
    g_right = jnp.concatenate(
        [
            g_right[:, :margin] + g_corner[:, :margin],
            g_right[:, margin:side],
            g_right[:, side : side + tall - margin] + g_corner[:, margin:],
            g_right[:, side + tall - margin :],
        ],
        1,
    )
    from_left = shifted(g_right, "col", 1)
    if depth % n_row == 0:
        thin = depth // n_row
        part = part.reshape(3, n_row, thin, side).transpose(1, 0, 2, 3)
        part = jnp.sum(lax.all_to_all(part, "row", 0, 0), 0)
        start = (lax.axis_index("col") * n_row + lax.axis_index("row")) * thin
        old = lax.dynamic_slice_in_dim(probe_field, start, thin, 1)
        new = old + part[:2] / (part[2] + 1.0)
        new = lax.all_to_all(jnp.broadcast_to(new, (n_row,) + new.shape), "row", 0, 0)
    else:
        part = lax.psum(part, "row")
        old = lax.dynamic_slice_in_dim(probe_field, lax.axis_index("col") * depth, depth, 1)
        new = (old + part[:2] / (part[2] + 1.0))[None]
    new = lax.all_to_all(jnp.broadcast_to(new, (n_col,) + new.shape), "col", 0, 0)
    new_probe = new.transpose(2, 0, 1, 3, 4).reshape(2, side, side)
    new_object = pl.pallas_call(
        finish_kernel,
        out_shape=f32(2, side, side),
        in_specs=[SMEM] + [VMEM] * 4,
        out_specs=VMEM,
        cost_estimate=cost(10**6, 4 * 10**6),
        compiler_params=PARAMS,
    )(largest, object_field, g_tile, from_left, from_above)
    return (new_object, new_probe)


def solution(mesh):
    in_specs = (P(None, "row", "col"), P(), P("row", "col", None), P("row", "col"))
    out_specs = (P(None, "row", "col"), P())
    return jax.shard_map(body, mesh=mesh, in_specs=in_specs, out_specs=out_specs, check_vma=False)
```

profile of v0, /device:TPU:4, one launch (start us, length us, event | category | flops | bytes accessed | tf_op | source)
XLA Modules:
  0.0 88.0 jit_solution(7053860859622658367)
XLA Ops:
  0.6 0.0 copy-start
  0.6 1.0 %copy-done = f32[2,256,256]{2,1,0:T(8,128)S(1)} copy-done((f32[2,256,256]{2,1,0:T(8,128)S(1)}, f32[2,256,256]{2,1,0:T(8,128)}, u32[]{:S(2)}) %copy-start) | copy-done | bytes 524312
  1.7 0.1 shard_map.122
  1.8 1.3 %collective-permute-start.1 = (f32[2,200,128]{2,1,0:T(8,128)S(1)}, f32[2,200,128]{2,1,0:T(8,128)S(1)}, u32[]{:S(2)}, u32[]{:S(2)}) collective-permute-start(f32[2,200,128]{2,1,0:T(8,128)S(1)} %get-tuple-element.16), channel_id=1, source_target_pairs={{8,0},{16,8},{24,16},{9,1},{17,9},{25,17},{10,2},{18,10},{26,18},{... | collective-permute-start | bytes 614408 | tf_op jit(solution)/shard_map/ppermute | solution.py:21
  3.1 2.8 %collective-permute-start = (f32[2,320,128]{2,1,0:T(8,128)S(1)}, f32[2,320,128]{2,1,0:T(8,128)S(1)}, u32[]{:S(2)}, u32[]{:S(2)}) collective-permute-start(f32[2,320,128]{2,1,0:T(8,128)S(1)} %get-tuple-element.15), channel_id=1, source_target_pairs={{1,0},{2,1},{3,2},{4,3},{5,4},{6,5},{7,6},{9,8},{10,9},{11,10},{12... | collective-permute-start | bytes 983048 | tf_op jit(solution)/shard_map/ppermute | solution.py:21
  5.9 1.3 %collective-permute-start.2 = (f32[2,160,128]{2,1,0:T(8,128)S(1)}, f32[2,160,128]{2,1,0:T(8,128)S(1)}, u32[]{:S(2)}, u32[]{:S(2)}) collective-permute-start(f32[2,160,128]{2,1,0:T(8,128)S(1)} %get-tuple-element.17), channel_id=1, source_target_pairs={{8,0},{16,8},{24,16},{9,1},{17,9},{25,17},{10,2},{18,10},{26,18},{... | collective-permute-start | bytes 491528 | tf_op jit(solution)/shard_map/ppermute | solution.py:21
  7.2 3.3 %collective-permute-done.1.near_ref = f32[2,200,128]{2,1,0:T(8,128)S(1)} collective-permute-done((f32[2,200,128]{2,1,0:T(8,128)S(1)}, f32[2,200,128]{2,1,0:T(8,128)S(1)}, u32[]{:S(2)}, u32[]{:S(2)}) %collective-permute-start.1) | collective-permute-done | bytes 204832 | tf_op jit(solution)/shard_map/ppermute | solution.py:21
  10.5 1.9 %collective-permute-start.3 = (f32[2,200,128]{2,1,0:T(8,128)S(1)}, f32[2,200,128]{2,1,0:T(8,128)S(1)}, u32[]{:S(2)}, u32[]{:S(2)}) collective-permute-start(f32[2,200,128]{2,1,0:T(8,128)S(1)} %collective-permute-done.1.near_ref), channel_id=1, source_target_pairs={{1,0},{2,1},{3,2},{4,3},{5,4},{6,5},{7,6},{9,8},{10,9},{11,10},{12... | collective-permute-start | bytes 614408 | tf_op jit(solution)/shard_map/ppermute | solution.py:21
  12.4 0.0 copy-start.2
  12.4 1.0 %copy-done.2 = f32[2,256,256]{2,1,0:T(8,128)S(1)} copy-done((f32[2,256,256]{2,1,0:T(8,128)S(1)}, f32[2,256,256]{2,1,0:T(8,128)}, u32[]{:S(2)}) %copy-start.2) | copy-done | bytes 524312
  13.5 0.0 copy-start.3
  13.5 1.2 %copy-done.3 = f32[4,256,256]{2,1,0:T(8,128)S(1)} copy-done((f32[4,256,256]{2,1,0:T(8,128)S(1)}, f32[4,256,256]{2,1,0:T(8,128)}, u32[]{:S(2)}) %copy-start.3) | copy-done | bytes 1048600
  14.7 0.0 copy-start.4
  14.7 0.7 copy-done.4
  15.4 0.0 copy-start.9
  15.4 0.9 %copy-done.9 = bf16[2,256,256]{2,1,0:T(8,128)(2,1)S(1)} copy-done((bf16[2,256,256]{2,1,0:T(8,128)(2,1)S(1)}, bf16[2,256,256]{2,1,0:T(8,128)(2,1)}, u32[]{:S(2)}) %copy-start.9) | copy-done | bytes 262168
  16.3 0.0 copy-start.1
  16.3 0.0 copy-start.5
  16.3 0.0 copy-start.6
  16.3 0.0 copy-start.7
  16.3 0.0 copy-start.8
  16.3 0.0 copy-start.10
  16.4 0.0 copy-start.11
  16.4 2.8 %shard_map.123 = (f32[4,2,256,256]{3,2,1,0:T(8,128)S(1)}, f32[4,256,256]{2,1,0:T(8,128)S(1)}) custom-call(s32[2,4]{1,0:T(2,128)S(1)} %bitcast.9, f32[2,256,256]{2,1,0:T(8,128)S(1)} %copy-done.2, f32[4,256,256]{2,1,0:T(8,128)S(1)} %copy-done.3, bf16[2,256,256]{2,1,0:T(8,128)(2,1)S(1)} %copy-done.9), custom_call_target="tpu_custom_call" | custom-call | flops 3000000000 | bytes 6000000 | tf_op jit(solution)/shard_map/pallas_call | solution.py:372
  19.2 0.0 collective-permute-done.2.far_ref
  19.2 0.0 collective-permute-done.right_ref
  19.2 0.0 collective-permute-done.3.corner_ref
  19.2 0.0 copy-done.1
  19.2 0.0 copy-done.5
  19.2 0.0 copy-done.6
  19.2 0.0 copy-done.7
  19.2 0.0 copy-done.8
  19.3 0.0 copy-done.10
  19.3 0.0 copy-done.11
  19.3 8.2 %shard_map.124 = (f32[2,256,256]{2,1,0:T(8,128)S(1)}, f32[2,320,128]{2,1,0:T(8,128)S(1)}, f32[2,520,128]{2,1,0:T(8,128)S(1)}, f32[8,3,32,256]{3,2,1,0:T(8,128)}, f32[1,1]{1,0:T(1,128)}) custom-call(s32[2,4]{1,0:T(2,128)S(1)} %bitcast.10, f32[2,256,256]{2,1,0:T(8,128)S(1)} %copy-done.1, f32[2,320,128]{2,1,0:T(8,128)S(1)} %collective-permute-done.right_ref, ...), custom_call_target="tpu_custom_call" | custom-call | flops 6000000000 | bytes 12000000 | tf_op jit(solution)/shard_map/pallas_call | solution.py:382
  27.5 4.3 %all-to-all-start = ((f32[8,3,32,256]{3,2,1,0:T(8,128)}), f32[8,3,32,256]{3,2,1,0:T(8,128)S(1)}, u32[]{:S(2)}, u32[]{:S(2)}) async-start(f32[8,3,32,256]{3,2,1,0:T(8,128)} %get-tuple-element.23), calls=%async_computation | async-start | bytes 1572864 | tf_op jit(solution)/shard_map/all_to_all | solution.py:410
  31.8 3.5 %collective-permute-start.4 = (f32[2,520,128]{2,1,0:T(8,128)S(1)}, f32[2,520,128]{2,1,0:T(8,128)S(1)}, u32[]{:S(2)}, u32[]{:S(2)}) collective-permute-start(f32[2,520,128]{2,1,0:T(8,128)S(1)} %get-tuple-element.24), channel_id=1, source_target_pairs={{0,8},{8,16},{16,24},{1,9},{9,17},{17,25},{2,10},{10,18},{18,26},{... | collective-permute-start | bytes 1597448 | tf_op jit(solution)/shard_map/ppermute | solution.py:21
  35.3 11.6 %collective-permute-done.4.down_ref = f32[2,520,128]{2,1,0:T(8,128)S(1)} collective-permute-done((f32[2,520,128]{2,1,0:T(8,128)S(1)}, f32[2,520,128]{2,1,0:T(8,128)S(1)}, u32[]{:S(2)}, u32[]{:S(2)}) %collective-permute-start.4) | collective-permute-done | bytes 532512 | tf_op jit(solution)/shard_map/ppermute | solution.py:21
  47.0 0.0 all-to-all-done
  47.0 0.1 reduce_sum.18
  47.0 0.6 copy.14
  47.7 4.8 %all-to-all-start.1 = ((f32[4,3,8,256]{3,2,1,0:T(8,128)}), f32[4,3,8,256]{3,2,1,0:T(8,128)S(1)}, u32[]{:S(2)}, u32[]{:S(2)}) async-start(f32[4,3,8,256]{3,2,1,0:T(8,128)} %copy.14), calls=%async_computation.1 | async-start | bytes 196608 | tf_op jit(solution)/shard_map/all_to_all | solution.py:426
  52.4 5.8 %all-to-all-done.1 = f32[4,3,8,256]{3,2,1,0:T(8,128)S(1)} async-done(((f32[4,3,8,256]{3,2,1,0:T(8,128)}), f32[4,3,8,256]{3,2,1,0:T(8,128)S(1)}, u32[]{:S(2)}, u32[]{:S(2)}) %all-to-all-start.1) | async-done | bytes 98336 | tf_op jit(solution)/shard_map/all_to_all | solution.py:426
  58.3 0.7 fusion
  59.0 0.6 broadcast_in_dim.7
  59.7 3.3 %all-to-all-start.2 = ((f32[4,2,8,256]{3,2,1,0:T(8,128)}), f32[4,2,8,256]{3,2,1,0:T(8,128)S(1)}, u32[]{:S(2)}, u32[]{:S(2)}) async-start(f32[4,2,8,256]{3,2,1,0:T(8,128)} %broadcast_in_dim.7), calls=%async_computation.2 | async-start | bytes 131072 | tf_op jit(solution)/shard_map/all_to_all | solution.py:430
  63.0 5.7 %all-to-all-done.2 = f32[4,2,8,256]{3,2,1,0:T(8,128)S(1)} async-done(((f32[4,2,8,256]{3,2,1,0:T(8,128)}), f32[4,2,8,256]{3,2,1,0:T(8,128)S(1)}, u32[]{:S(2)}, u32[]{:S(2)}) %all-to-all-start.2) | async-done | bytes 65568 | tf_op jit(solution)/shard_map/all_to_all | solution.py:430
  68.7 0.8 broadcast_in_dim.8
  69.5 4.2 %all-to-all-start.3 = ((f32[8,4,2,8,256]{4,3,1,2,0:T(8,128)}), f32[8,4,2,8,256]{4,3,1,2,0:T(8,128)S(1)}, u32[]{:S(2)}, u32[]{:S(2)}) async-start(f32[8,4,2,8,256]{4,3,1,2,0:T(8,128)} %broadcast_in_dim.8), calls=%async_computation.3 | async-start | bytes 1048576 | tf_op jit(solution)/shard_map/all_to_all | solution.py:435
  73.8 2.1 %collective-permute-start.5 = (f32[2,320,128]{2,1,0:T(8,128)S(1)}, f32[2,320,128]{2,1,0:T(8,128)S(1)}, u32[]{:S(2)}, u32[]{:S(2)}) collective-permute-start(f32[2,320,128]{2,1,0:T(8,128)S(1)} %pad_maximum_fusion), channel_id=1, source_target_pairs={{0,1},{1,2},{2,3},{3,4},{4,5},{5,6},{6,7},{8,9},{9,10},{10,11},{11... | collective-permute-start | bytes 983048 | tf_op jit(solution)/shard_map/ppermute | solution.py:21
  75.9 9.7 %collective-permute-done.5.right_ref = f32[2,320,128]{2,1,0:T(8,128)S(1)} collective-permute-done((f32[2,320,128]{2,1,0:T(8,128)S(1)}, f32[2,320,128]{2,1,0:T(8,128)S(1)}, u32[]{:S(2)}, u32[]{:S(2)}) %collective-permute-start.5) | collective-permute-done | bytes 327712 | tf_op jit(solution)/shard_map/ppermute | solution.py:21
  85.5 1.6 %shard_map.125 = f32[2,256,256]{2,1,0:T(8,128)} custom-call(f32[1,1]{1,0:T(1,128)} %get-tuple-element.20.max_ref, f32[2,256,256]{2,1,0:T(8,128)S(1)} %copy-done.1, f32[2,256,256]{2,1,0:T(8,128)S(1)} %get-tuple-element.21.grad_ref, f32[2,320,128]{2,1,0:T(8,128)S(1)} %collective-permute-done.5.right_ref, f32[2,520,128]{2,1,0:T(8,128)S(1)} %collective-permute-done.4.down_ref), custom_call_target="tpu_custom_call" | custom-call | flops 1000000 | bytes 4000000 | tf_op jit(solution)/shard_map/pallas_call | solution.py:437
  87.1 0.0 all-to-all-done.3
  87.1 0.8 copy.16
  (9 shorter events, 0.1 us)
Async XLA Ops:
  0.6 1.0 %copy-start = (f32[2,256,256]{2,1,0:T(8,128)S(1)}, f32[2,256,256]{2,1,0:T(8,128)}, u32[]{:S(2)}) copy-start(f32[2,256,256]{2,1,0:T(8,128)} %tile_ref.5) | copy-start | bytes 1572868
  1.8 8.7 %collective-permute-start.1 = (f32[2,200,128]{2,1,0:T(8,128)S(1)}, f32[2,200,128]{2,1,0:T(8,128)S(1)}, u32[]{:S(2)}, u32[]{:S(2)}) collective-permute-start(f32[2,200,128]{2,1,0:T(8,128)S(1)} %get-tuple-element.16), channel_id=1, source_target_pairs={{8,0},{16,8},{24,16},{9,1},{17,9},{25,17},{10,2},{18,10},{26,18},{... | collective-permute-start | bytes 614408 | tf_op jit(solution)/shard_map/ppermute | solution.py:21
  3.1 16.1 %collective-permute-start = (f32[2,320,128]{2,1,0:T(8,128)S(1)}, f32[2,320,128]{2,1,0:T(8,128)S(1)}, u32[]{:S(2)}, u32[]{:S(2)}) collective-permute-start(f32[2,320,128]{2,1,0:T(8,128)S(1)} %get-tuple-element.15), channel_id=1, source_target_pairs={{1,0},{2,1},{3,2},{4,3},{5,4},{6,5},{7,6},{9,8},{10,9},{11,10},{12... | collective-permute-start | bytes 983048 | tf_op jit(solution)/shard_map/ppermute | solution.py:21
  5.9 13.3 %collective-permute-start.2 = (f32[2,160,128]{2,1,0:T(8,128)S(1)}, f32[2,160,128]{2,1,0:T(8,128)S(1)}, u32[]{:S(2)}, u32[]{:S(2)}) collective-permute-start(f32[2,160,128]{2,1,0:T(8,128)S(1)} %get-tuple-element.17), channel_id=1, source_target_pairs={{8,0},{16,8},{24,16},{9,1},{17,9},{25,17},{10,2},{18,10},{26,18},{... | collective-permute-start | bytes 491528 | tf_op jit(solution)/shard_map/ppermute | solution.py:21
  10.5 8.7 %collective-permute-start.3 = (f32[2,200,128]{2,1,0:T(8,128)S(1)}, f32[2,200,128]{2,1,0:T(8,128)S(1)}, u32[]{:S(2)}, u32[]{:S(2)}) collective-permute-start(f32[2,200,128]{2,1,0:T(8,128)S(1)} %collective-permute-done.1.near_ref), channel_id=1, source_target_pairs={{1,0},{2,1},{3,2},{4,3},{5,4},{6,5},{7,6},{9,8},{10,9},{11,10},{12... | collective-permute-start | bytes 614408 | tf_op jit(solution)/shard_map/ppermute | solution.py:21
  12.4 1.0 %copy-start.2 = (f32[2,256,256]{2,1,0:T(8,128)S(1)}, f32[2,256,256]{2,1,0:T(8,128)}, u32[]{:S(2)}) copy-start(f32[2,256,256]{2,1,0:T(8,128)} %probe_ref.1) | copy-start | bytes 1572868
  13.5 1.2 %copy-start.3 = (f32[4,256,256]{2,1,0:T(8,128)S(1)}, f32[4,256,256]{2,1,0:T(8,128)}, u32[]{:S(2)}) copy-start(f32[4,256,256]{2,1,0:T(8,128)} %meas_ref.1) | copy-start | bytes 3145732
  14.7 0.7 copy-start.4
  15.4 0.9 %copy-start.9 = (bf16[2,256,256]{2,1,0:T(8,128)(2,1)S(1)}, bf16[2,256,256]{2,1,0:T(8,128)(2,1)}, u32[]{:S(2)}) copy-start(bf16[2,256,256]{2,1,0:T(8,128)(2,1)} %constant.34.clone.sort_ref) | copy-start | bytes 786436
  16.3 2.9 %copy-start.1 = (f32[2,256,256]{2,1,0:T(8,128)S(1)}, f32[2,256,256]{2,1,0:T(8,128)}, u32[]{:S(2)}) copy-start(f32[2,256,256]{2,1,0:T(8,128)} %tile_ref.5) | copy-start | bytes 1572868
  16.3 2.9 %copy-start.5 = (bf16[768,256]{1,0:T(8,128)(2,1)S(1)}, bf16[768,256]{1,0:T(8,128)(2,1)}, u32[]{:S(2)}) copy-start(bf16[768,256]{1,0:T(8,128)(2,1)} %constant.35.clone.fwd_right) | copy-start | bytes 1179652
  16.3 2.9 %copy-start.6 = (bf16[256,768]{1,0:T(8,128)(2,1)S(1)}, bf16[256,768]{1,0:T(8,128)(2,1)}, u32[]{:S(2)}) copy-start(bf16[256,768]{1,0:T(8,128)(2,1)} %constant.36.clone.fwd_left) | copy-start | bytes 1179652
  16.3 2.9 %copy-start.7 = (bf16[768,256]{1,0:T(8,128)(2,1)S(1)}, bf16[768,256]{1,0:T(8,128)(2,1)}, u32[]{:S(2)}) copy-start(bf16[768,256]{1,0:T(8,128)(2,1)} %constant.37.clone.inv_right) | copy-start | bytes 1179652
  16.3 2.9 %copy-start.8 = (bf16[256,768]{1,0:T(8,128)(2,1)S(1)}, bf16[256,768]{1,0:T(8,128)(2,1)}, u32[]{:S(2)}) copy-start(bf16[256,768]{1,0:T(8,128)(2,1)} %constant.38.clone.inv_left) | copy-start | bytes 1179652
  16.3 2.9 %copy-start.10 = (f32[2,128,128]{2,1,0:T(8,128)S(1)}, f32[2,128,128]{2,1,0:T(8,128)}, u32[]{:S(2)}) copy-start(f32[2,128,128]{2,1,0:T(8,128)} %constant.40.clone.row_ref) | copy-start | bytes 393220
  16.4 2.9 %copy-start.11 = (f32[2,8,128]{2,1,0:T(8,128)S(1)}, f32[2,8,128]{2,1,0:T(8,128)}, u32[]{:S(2)}) copy-start(f32[2,8,128]{2,1,0:T(8,128)} %constant.39.clone.lane_ref) | copy-start | bytes 24580
  27.5 19.5 %all-to-all-start = ((f32[8,3,32,256]{3,2,1,0:T(8,128)}), f32[8,3,32,256]{3,2,1,0:T(8,128)S(1)}, u32[]{:S(2)}, u32[]{:S(2)}) async-start(f32[8,3,32,256]{3,2,1,0:T(8,128)} %get-tuple-element.23), calls=%async_computation | async-start | bytes 1572864 | tf_op jit(solution)/shard_map/all_to_all | solution.py:410
  31.8 15.1 %collective-permute-start.4 = (f32[2,520,128]{2,1,0:T(8,128)S(1)}, f32[2,520,128]{2,1,0:T(8,128)S(1)}, u32[]{:S(2)}, u32[]{:S(2)}) collective-permute-start(f32[2,520,128]{2,1,0:T(8,128)S(1)} %get-tuple-element.24), channel_id=1, source_target_pairs={{0,8},{8,16},{16,24},{1,9},{9,17},{17,25},{2,10},{10,18},{18,26},{... | collective-permute-start | bytes 1597448 | tf_op jit(solution)/shard_map/ppermute | solution.py:21
  47.7 10.6 %all-to-all-start.1 = ((f32[4,3,8,256]{3,2,1,0:T(8,128)}), f32[4,3,8,256]{3,2,1,0:T(8,128)S(1)}, u32[]{:S(2)}, u32[]{:S(2)}) async-start(f32[4,3,8,256]{3,2,1,0:T(8,128)} %copy.14), calls=%async_computation.1 | async-start | bytes 196608 | tf_op jit(solution)/shard_map/all_to_all | solution.py:426
  59.7 9.0 %all-to-all-start.2 = ((f32[4,2,8,256]{3,2,1,0:T(8,128)}), f32[4,2,8,256]{3,2,1,0:T(8,128)S(1)}, u32[]{:S(2)}, u32[]{:S(2)}) async-start(f32[4,2,8,256]{3,2,1,0:T(8,128)} %broadcast_in_dim.7), calls=%async_computation.2 | async-start | bytes 131072 | tf_op jit(solution)/shard_map/all_to_all | solution.py:430
  69.5 17.6 %all-to-all-start.3 = ((f32[8,4,2,8,256]{4,3,1,2,0:T(8,128)}), f32[8,4,2,8,256]{4,3,1,2,0:T(8,128)S(1)}, u32[]{:S(2)}, u32[]{:S(2)}) async-start(f32[8,4,2,8,256]{4,3,1,2,0:T(8,128)} %broadcast_in_dim.8), calls=%async_computation.3 | async-start | bytes 1048576 | tf_op jit(solution)/shard_map/all_to_all | solution.py:435
  73.8 11.7 %collective-permute-start.5 = (f32[2,320,128]{2,1,0:T(8,128)S(1)}, f32[2,320,128]{2,1,0:T(8,128)S(1)}, u32[]{:S(2)}, u32[]{:S(2)}) collective-permute-start(f32[2,320,128]{2,1,0:T(8,128)S(1)} %pad_maximum_fusion), channel_id=1, source_target_pairs={{0,1},{1,2},{2,3},{3,4},{4,5},{5,6},{6,7},{8,9},{9,10},{10,11},{11... | collective-permute-start | bytes 983048 | tf_op jit(solution)/shard_map/ppermute | solution.py:21
where the time goes:
time: 88.8 us; the launch traced here: 88 us
  waiting for transfers between devices  36.1 us (41%)
  starting transfers between devices  29.4 us (33%)
  Pallas kernels  12.7 us (14%)
  local copies, waits for them, and re-layouts  7.97 us (9%)
  between operations  0.89 us (1%)
    ppermute x6, waiting for transfers between devices, shifted(): lax.ppermute(value, axis, [(source, source + steps) for source in range(i...  24.6 us
    ppermute x6, starting transfers between devices, shifted(): lax.ppermute(value, axis, [(source, source + steps) for source in range(i...  12.8 us
    pallas_call x1, Pallas kernels, body(): pl.pallas_call(frame_kernel, out_shape=(f32(2, side, side), f32(2, wide,...  8.19 us
    all_to_all x1, waiting for transfers between devices, body(): part = jnp.sum(lax.all_to_all(part, 'row', 0, 0), 0)  5.83 us
    all_to_all x1, waiting for transfers between devices, body(): lax.all_to_all(jnp.broadcast_to(new, (n_row,) + new.shape), 'row', 0, 0)  5.68 us
    unnamed x24, local copies, waits for them, and re-layouts  4.96 us
    all_to_all x1, starting transfers between devices, body(): part = jnp.sum(lax.all_to_all(part, 'row', 0, 0), 0)  4.75 us
    all_to_all x1, starting transfers between devices, body(): part = jnp.sum(lax.all_to_all(sums, 'col', 0, 0), 0)  4.35 us
  transfers between devices with their start and end apart: 10, of which 5 were waited for; matrix products, arithmetic and copies ran while one was open for 0% of the time, Pallas kernels for 5%

commit v1 on v0

--- a/solution.py
+++ b/solution.py
@@ -10,6 +10,7 @@
 
 HALO = 160
 VMEM = pl.BlockSpec(memory_space=pltpu.VMEM)
+HBM = pl.BlockSpec(memory_space=pltpu.HBM)
 SMEM = pl.BlockSpec(memory_space=pltpu.SMEM)
 PARAMS = pltpu.CompilerParams(vmem_limit_bytes=24 * 1024 * 1024)
 BF16 = jnp.bfloat16
@@ -97,9 +98,16 @@
     return jnp.where(stay, one, two), jnp.where(stay, two, one)
 
 
-def prepare_kernel(pos_ref, probe_ref, meas_ref, sort_ref, prot_ref, sorted_ref, twice):
+def prepare_kernel(
+    pos_ref, probe_hbm, meas_hbm, sort_hbm, prot_ref, sorted_ref, probe_ref, meas_ref, sort_ref, twice, sems
+):
     frames, side = meas_ref.shape[0], meas_ref.shape[1]
     half = side // 2
+    pairs = ((probe_hbm, probe_ref), (sort_hbm, sort_ref), (meas_hbm, meas_ref))
+    copies = [pltpu.make_async_copy(source, target, sems.at[index]) for index, (source, target) in enumerate(pairs)]
+    for copy in copies:
+        copy.start()
+    copies[0].wait()
     for part in range(2):
         for tile in range(2):
             piece = probe_ref[part, :, tile * half : (tile + 1) * half]
@@ -119,6 +127,12 @@
                 )
                 prot_ref[frame, part, row : row + step, 0:half] = one
                 prot_ref[frame, part, row : row + step, half:side] = two
+
+    copies[1].wait()
+    copies[2].wait()
+
+    @pl.loop(0, frames)
+    def _(frame):
         value = meas_ref[frame]
         total = None
         for _ in range(3):
@@ -138,6 +152,7 @@
     frames, side = meas_ref.shape[0], meas_ref.shape[1]
     half = side // 2
     margin = far_ref.shape[1]
+    wide = right_ref.shape[1]
     extra = margin - half
     for row, packed, lane in pack_extra(side, extra, half):
         right_extra[:, row : row + 8, 0:extra] = right_ref[:, side + packed : side + packed + 8, lane : lane + extra]
@@ -300,10 +315,9 @@
             if row < margin:
                 gz_ref[part, rows] = total["b", part, 0]
                 gz_ref[part, margin + row : margin + row + step] = total["b", part, 1]
-                base = 2 * margin
-                gz_ref[part, base + row : base + row + step] = total["c", part, 0]
-                base = 3 * margin + packed
-                gz_ref[part, base : base + 8, lane : lane + extra] = total["c", part, 1][:, 0:extra]
+                gr_ref[part, wide + row : wide + row + step] = total["c", part, 0]
+                base = wide + margin + packed
+                gr_ref[part, base : base + 8, lane : lane + extra] = total["c", part, 1][:, 0:extra]
 
     depth = qs_ref.shape[2]
     step = min(32, depth)
@@ -323,12 +337,11 @@
             qs_ref[row // depth, index, place, half:side] = sums[1]
 
 
-def finish_kernel(max_ref, tile_ref, grad_ref, right_ref, down_ref, out_ref):
+def finish_kernel(max_ref, tile_ref, grad_ref, right_ref, down_ref, corner_ref, out_ref):
     side = tile_ref.shape[1]
     half = side // 2
-    rows = right_ref.shape[1]
-    extra = (rows - side) * half // side
-    margin = half + extra
+    margin = down_ref.shape[1] // 2
+    extra = margin - half
     scale = 1.0 / max_ref[0, 0]
     step = 8
     for row, packed, lane in pack_extra(side, extra, half):
@@ -336,12 +349,13 @@
         for part in range(2):
             one = grad_ref[part, place, 0:half] + right_ref[part, place]
             two = grad_ref[part, place, half:side]
+            piece = right_ref[part, side + packed : side + packed + 8, lane : lane + extra]
             if row < margin:
-                one = one + down_ref[part, place]
+                one = one + down_ref[part, place] + corner_ref[part, place]
                 two = two + down_ref[part, margin + row : margin + row + step]
+                piece = piece + corner_ref[part, margin + packed : margin + packed + 8, lane : lane + extra]
             out_ref[part, place, 0:half] = tile_ref[part, place, 0:half] + one * scale
             out_ref[part, place, half:side] = tile_ref[part, place, half:side] + two * scale
-            piece = right_ref[part, side + packed : side + packed + 8, lane : lane + extra]
             out_ref[part, place, half:margin] += piece * scale
 
 
@@ -367,24 +381,31 @@
     near = shifted(near, "row", -1)
     far = shifted(far, "row", -1)
     right = shifted(right, "col", -1)
-    corner = shifted(near, "col", -1)
     places = positions.T
     prot, ampl = pl.pallas_call(
         prepare_kernel,
         out_shape=(f32(frames, 2, side, side), f32(frames, side, side)),
-        in_specs=[SMEM, VMEM, VMEM, VMEM],
+        in_specs=[SMEM, HBM, HBM, HBM],
         out_specs=(VMEM, VMEM),
-        scratch_shapes=[pltpu.VMEM((2, 2, 2 * side, half), jnp.float32)],
+        scratch_shapes=[
+            pltpu.VMEM((2, side, side), jnp.float32),
+            pltpu.VMEM((frames, side, side), jnp.float32),
+            pltpu.VMEM((2, side, side), BF16),
+            pltpu.VMEM((2, 2, 2 * side, half), jnp.float32),
+            pltpu.SemaphoreType.DMA((3,)),
+        ],
         cost_estimate=cost(3 * 10**9, 6 * 10**6),
-        compiler_params=PARAMS,
+        compiler_params=pltpu.CompilerParams(vmem_limit_bytes=60 * 1024 * 1024),
     )(places, probe_field, measured, sort)
+    near, prot = lax.optimization_barrier((near, prot))
+    corner = shifted(near, "col", -1)
     depth = side // n_col
     g_tile, g_right, g_down, sums, largest = pl.pallas_call(
         frame_kernel,
         out_shape=(
             f32(2, side, side),
-            f32(2, wide, half),
-            f32(2, 2 * margin + tall, half),
+            f32(2, wide + tall, half),
+            f32(2, 2 * margin, half),
             f32(n_col, 3, depth, side),
             f32(1, 1),
         ),
@@ -408,40 +429,27 @@
 
     from_above = shifted(g_down, "row", 1)
     part = jnp.sum(lax.all_to_all(sums, "col", 0, 0), 0)
-    g_corner = from_above[:, 2 * margin :]
-    g_right, part, g_corner = lax.optimization_barrier((g_right, part, g_corner))
-    g_right = jnp.concatenate(
-        [
-            g_right[:, :margin] + g_corner[:, :margin],
-            g_right[:, margin:side],
-            g_right[:, side : side + tall - margin] + g_corner[:, margin:],
-            g_right[:, side + tall - margin :],
-        ],
-        1,
-    )
+    g_right, part = lax.optimization_barrier((g_right, part))
     from_left = shifted(g_right, "col", 1)
-    if depth % n_row == 0:
-        thin = depth // n_row
-        part = part.reshape(3, n_row, thin, side).transpose(1, 0, 2, 3)
-        part = jnp.sum(lax.all_to_all(part, "row", 0, 0), 0)
-        start = (lax.axis_index("col") * n_row + lax.axis_index("row")) * thin
-        old = lax.dynamic_slice_in_dim(probe_field, start, thin, 1)
-        new = old + part[:2] / (part[2] + 1.0)
-        new = lax.all_to_all(jnp.broadcast_to(new, (n_row,) + new.shape), "row", 0, 0)
-    else:
-        part = lax.psum(part, "row")
-        old = lax.dynamic_slice_in_dim(probe_field, lax.axis_index("col") * depth, depth, 1)
-        new = (old + part[:2] / (part[2] + 1.0))[None]
+    first, second = part[:, : depth // 2], part[:, depth // 2 :]
+    first = lax.psum(first, "row")
+    first, second = lax.optimization_barrier((first, second))
+    second = lax.psum(second, "row")
+    part = jnp.concatenate([first, second], 1)
+    old = lax.dynamic_slice_in_dim(probe_field, lax.axis_index("col") * depth, depth, 1)
+    new = old + part[:2] / (part[2] + 1.0)
+    new, from_left = lax.optimization_barrier((new, from_left))
     new = lax.all_to_all(jnp.broadcast_to(new, (n_col,) + new.shape), "col", 0, 0)
-    new_probe = new.transpose(2, 0, 1, 3, 4).reshape(2, side, side)
+    from_corner = shifted(from_left[:, wide:], "row", 1)
+    new_probe = new.transpose(1, 0, 2, 3).reshape(2, side, side)
     new_object = pl.pallas_call(
         finish_kernel,
         out_shape=f32(2, side, side),
-        in_specs=[SMEM] + [VMEM] * 4,
+        in_specs=[SMEM] + [VMEM] * 5,
         out_specs=VMEM,
         cost_estimate=cost(10**6, 4 * 10**6),
         compiler_params=PARAMS,
-    )(largest, object_field, g_tile, from_left, from_above)
+    )(largest, object_field, g_tile, from_left, from_above, from_corner)
     return (new_object, new_probe)
 
 

time: 88.8 us -> 119 us (1.34)
  the two profiles are of different devices: /device:TPU:4 before, /device:TPU:20 now
where the time goes in v1:
time: 119 us; the launch traced here: 118 us
  waiting for transfers between devices  35.7 us (30%)
  blocking collectives  32.4 us (27%)
  starting transfers between devices  24.3 us (20%)
  Pallas kernels  16.1 us (14%)
  local copies, waits for them, and re-layouts  7.6 us (6%)
    ppermute x7, waiting for transfers between devices, shifted(): lax.ppermute(value, axis, [(source, source + steps) for source in range(i...  24.5 us
    ppermute x7, starting transfers between devices, shifted(): lax.ppermute(value, axis, [(source, source + steps) for source in range(i...  17.2 us
    psum x1, blocking collectives, body(): second = lax.psum(second, 'row')  16.6 us
    psum x1, blocking collectives, body(): first = lax.psum(first, 'row')  15.8 us
    all_to_all x1, waiting for transfers between devices, body(): part = jnp.sum(lax.all_to_all(sums, 'col', 0, 0), 0)  11.1 us
    pallas_call x1, Pallas kernels, body(): pl.pallas_call(frame_kernel, out_shape=(f32(2, side, side), f32(2, wide +...  8.24 us
    pallas_call x1, Pallas kernels, body(): pl.pallas_call(prepare_kernel, out_shape=(f32(frames, 2, side, side), f32...  6.09 us
    unnamed x23, local copies, waits for them, and re-layouts  5.88 us
  transfers between devices with their start and end apart: 9, of which 5 were waited for; matrix products, arithmetic and copies ran while one was open for 1% of the time, Pallas kernels for 7%

profile of v1, /device:TPU:20, one launch (start us, length us, event | category | flops | bytes accessed | tf_op | source)
XLA Modules:
  0.0 117.8 jit_solution(3574530859942392462)
XLA Ops:
  0.6 0.0 copy-start
  0.6 1.0 copy-done
  1.7 0.1 shard_map.122
  1.8 2.4 %collective-permute-start.1 = (f32[2,200,128]{2,1,0:T(8,128)S(1)}, f32[2,200,128]{2,1,0:T(8,128)S(1)}, u32[]{:S(2)}, u32[]{:S(2)}) collective-permute-start(f32[2,200,128]{2,1,0:T(8,128)S(1)} %get-tuple-element.21), channel_id=1, source_target_pairs={{8,0},{16,8},{24,16},{9,1},{17,9},{25,17},{10,2},{18,10},{26,18},{... | collective-permute-start | bytes 614408 | tf_op jit(solution)/shard_map/ppermute | solution.py:22
  4.2 2.5 %collective-permute-start = (f32[2,320,128]{2,1,0:T(8,128)S(1)}, f32[2,320,128]{2,1,0:T(8,128)S(1)}, u32[]{:S(2)}, u32[]{:S(2)}) collective-permute-start(f32[2,320,128]{2,1,0:T(8,128)S(1)} %get-tuple-element.20), channel_id=1, source_target_pairs={{1,0},{2,1},{3,2},{4,3},{5,4},{6,5},{7,6},{9,8},{10,9},{11,10},{12... | collective-permute-start | bytes 983048 | tf_op jit(solution)/shard_map/ppermute | solution.py:22
  6.7 0.0 copy-start.1
  6.7 0.0 copy-start.2
  6.7 0.0 copy-start.3
  6.7 0.0 copy-start.4
  6.7 0.0 copy-start.7
  6.7 0.0 copy-start.8
  6.7 6.1 %shard_map.123 = (f32[4,2,256,256]{3,2,1,0:T(8,128)}, f32[4,256,256]{2,1,0:T(8,128)}) custom-call(s32[2,4]{1,0:T(2,128)} %bitcast.6, f32[2,256,256]{2,1,0:T(8,128)} %probe_hbm.1, f32[4,256,256]{2,1,0:T(8,128)} %meas_hbm.1, bf16[2,256,256]{2,1,0:T(8,128)(2,1)} %constant.28.clone.sort_hbm), custom_call_target="tpu_custom_call" | custom-call | flops 3000000000 | bytes 6000000 | tf_op jit(solution)/shard_map/pallas_call | solution.py:385
  12.8 0.0 collective-permute-done.1.near_ref
  12.8 2.9 %collective-permute-start.3 = (f32[2,200,128]{2,1,0:T(8,128)S(1)}, f32[2,200,128]{2,1,0:T(8,128)S(1)}, u32[]{:S(2)}, u32[]{:S(2)}) collective-permute-start(f32[2,200,128]{2,1,0:T(8,128)S(1)} %collective-permute-done.1.near_ref), channel_id=1, source_target_pairs={{1,0},{2,1},{3,2},{4,3},{5,4},{6,5},{7,6},{9,8},{10,9},{11,10},{12... | collective-permute-start | bytes 614408 | tf_op jit(solution)/shard_map/ppermute | solution.py:22
  15.7 2.4 %collective-permute-start.2 = (f32[2,160,128]{2,1,0:T(8,128)S(1)}, f32[2,160,128]{2,1,0:T(8,128)S(1)}, u32[]{:S(2)}, u32[]{:S(2)}) collective-permute-start(f32[2,160,128]{2,1,0:T(8,128)S(1)} %get-tuple-element.24), channel_id=1, source_target_pairs={{8,0},{16,8},{24,16},{9,1},{17,9},{25,17},{10,2},{18,10},{26,18},{... | collective-permute-start | bytes 491528 | tf_op jit(solution)/shard_map/ppermute | solution.py:22
  18.1 5.2 %collective-permute-done.2.far_ref = f32[2,160,128]{2,1,0:T(8,128)S(1)} collective-permute-done((f32[2,160,128]{2,1,0:T(8,128)S(1)}, f32[2,160,128]{2,1,0:T(8,128)S(1)}, u32[]{:S(2)}, u32[]{:S(2)}) %collective-permute-start.2) | collective-permute-done | bytes 163872 | tf_op jit(solution)/shard_map/ppermute | solution.py:22
  23.3 0.0 collective-permute-done.right_ref
  23.3 0.0 collective-permute-done.3.corner_ref
  23.3 0.0 copy-done.1
  23.3 0.0 copy-done.2
  23.3 0.0 copy-done.3
  23.3 0.0 copy-done.4
  23.3 0.0 copy-done.7
  23.3 0.0 copy-done.8
  23.3 0.0 copy-start.5
  23.3 1.0 copy-done.5
  24.3 0.0 copy-start.6
  24.3 1.0 copy-done.6
  25.3 0.0 copy-start.9
  25.3 1.6 %copy-done.9 = f32[4,2,256,256]{3,2,1,0:T(8,128)S(1)} copy-done((f32[4,2,256,256]{3,2,1,0:T(8,128)S(1)}, f32[4,2,256,256]{3,2,1,0:T(8,128)}, u32[]{:S(2)}) %copy-start.9) | copy-done | bytes 2097176
  26.9 0.0 copy-start.10
  26.9 1.2 %copy-done.10 = f32[4,256,256]{2,1,0:T(8,128)S(1)} copy-done((f32[4,256,256]{2,1,0:T(8,128)S(1)}, f32[4,256,256]{2,1,0:T(8,128)}, u32[]{:S(2)}) %copy-start.10) | copy-done | bytes 1048600
  28.1 8.2 %shard_map.124 = (f32[2,256,256]{2,1,0:T(8,128)S(1)}, f32[2,520,128]{2,1,0:T(8,128)S(1)}, f32[2,320,128]{2,1,0:T(8,128)S(1)}, f32[8,3,32,256]{3,2,1,0:T(8,128)}, f32[1,1]{1,0:T(1,128)}) custom-call(s32[2,4]{1,0:T(2,128)S(1)} %bitcast.7, f32[2,256,256]{2,1,0:T(8,128)S(1)} %copy-done.1, f32[2,320,128]{2,1,0:T(8,128)S(1)} %collective-permute-done.right_ref, ...), custom_call_target="tpu_custom_call" | custom-call | flops 6000000000 | bytes 12000000 | tf_op jit(solution)/shard_map/pallas_call | solution.py:403
  36.4 3.7 %all-to-all-start = ((f32[8,3,32,256]{3,2,1,0:T(8,128)}), f32[8,3,32,256]{3,2,1,0:T(8,128)S(1)}, u32[]{:S(2)}, u32[]{:S(2)}) async-start(f32[8,3,32,256]{3,2,1,0:T(8,128)} %get-tuple-element.30), calls=%async_computation | async-start | bytes 1572864 | tf_op jit(solution)/shard_map/all_to_all | solution.py:431
  40.1 11.1 %all-to-all-done = f32[8,3,32,256]{3,2,1,0:T(8,128)S(1)} async-done(((f32[8,3,32,256]{3,2,1,0:T(8,128)}), f32[8,3,32,256]{3,2,1,0:T(8,128)S(1)}, u32[]{:S(2)}, u32[]{:S(2)}) %all-to-all-start) | async-done | bytes 786464 | tf_op jit(solution)/shard_map/all_to_all | solution.py:431
  51.2 0.1 reduce_sum.9
  51.3 15.8 %psum.14 = f32[3,16,256]{2,1,0:T(8,128)S(1)} all-reduce(f32[3,16,256]{2,1,0:T(8,128)S(1)} %get-tuple-element.39), channel_id=1, replica_groups=mesh['row'=4,'col'=8] {'row'}, use_global_device_ids=true, to_apply=%region_1.0 | all-reduce | flops 12288 | bytes 98304 | tf_op jit(solution)/shard_map/psum | solution.py:435
  67.1 16.6 %psum.15 = f32[3,16,256]{2,1,0:T(8,128)S(1)} all-reduce(f32[3,16,256]{2,1,0:T(8,128)S(1)} %get-tuple-element.33), channel_id=1, replica_groups=mesh['row'=4,'col'=8] {'row'}, use_global_device_ids=true, to_apply=%region_2.0 | all-reduce | flops 12288 | bytes 98304 | tf_op jit(solution)/shard_map/psum | solution.py:437
  83.7 1.9 %collective-permute-start.4 = (f32[2,520,128]{2,1,0:T(8,128)S(1)}, f32[2,520,128]{2,1,0:T(8,128)S(1)}, u32[]{:S(2)}, u32[]{:S(2)}) collective-permute-start(f32[2,520,128]{2,1,0:T(8,128)S(1)} %get-tuple-element.34), channel_id=1, source_target_pairs={{0,1},{1,2},{2,3},{3,4},{4,5},{5,6},{6,7},{8,9},{9,10},{10,11},{11... | collective-permute-start | bytes 1597448 | tf_op jit(solution)/shard_map/ppermute | solution.py:22
  85.7 0.9 fusion
  86.5 8.7 %collective-permute-done.4.right_ref = f32[2,520,128]{2,1,0:T(8,128)S(1)} collective-permute-done((f32[2,520,128]{2,1,0:T(8,128)S(1)}, f32[2,520,128]{2,1,0:T(8,128)S(1)}, u32[]{:S(2)}, u32[]{:S(2)}) %collective-permute-start.4) | collective-permute-done | bytes 532512 | tf_op jit(solution)/shard_map/ppermute | solution.py:22
  95.2 0.8 broadcast_in_dim.4
  96.0 3.4 %all-to-all-start.1 = ((f32[8,2,32,256]{3,2,1,0:T(8,128)}), f32[8,2,32,256]{3,2,1,0:T(8,128)S(1)}, u32[]{:S(2)}, u32[]{:S(2)}) async-start(f32[8,2,32,256]{3,2,1,0:T(8,128)} %broadcast_in_dim.4), calls=%async_computation.1 | async-start | bytes 1048576 | tf_op jit(solution)/shard_map/all_to_all | solution.py:442
  99.5 3.2 %collective-permute-start.5 = (f32[2,320,128]{2,1,0:T(8,128)S(1)}, f32[2,320,128]{2,1,0:T(8,128)S(1)}, u32[]{:S(2)}, u32[]{:S(2)}) collective-permute-start(f32[2,320,128]{2,1,0:T(8,128)S(1)} %get-tuple-element.36), channel_id=1, source_target_pairs={{0,8},{8,16},{16,24},{1,9},{9,17},{17,25},{2,10},{10,18},{18,26},{... | collective-permute-start | bytes 983048 | tf_op jit(solution)/shard_map/ppermute | solution.py:22
  102.8 1.9 %collective-permute-start.6 = (f32[2,200,128]{2,1,0:T(8,128)S(1)}, f32[2,200,128]{2,1,0:T(8,128)S(1)}, u32[]{:S(2)}, u32[]{:S(2)}) collective-permute-start(f32[2,200,128]{2,1,0:T(8,128)S(1)} %slice.19), channel_id=1, source_target_pairs={{0,8},{8,16},{16,24},{1,9},{9,17},{17,25},{2,10},{10,18},{18,26},{... | collective-permute-start | bytes 614408 | tf_op jit(solution)/shard_map/ppermute | solution.py:22
  104.7 7.3 %collective-permute-done.5.down_ref = f32[2,320,128]{2,1,0:T(8,128)S(1)} collective-permute-done((f32[2,320,128]{2,1,0:T(8,128)S(1)}, f32[2,320,128]{2,1,0:T(8,128)S(1)}, u32[]{:S(2)}, u32[]{:S(2)}) %collective-permute-start.5) | collective-permute-done | bytes 327712 | tf_op jit(solution)/shard_map/ppermute | solution.py:22
  112.0 3.4 %collective-permute-done.6.corner_ref = f32[2,200,128]{2,1,0:T(8,128)S(1)} collective-permute-done((f32[2,200,128]{2,1,0:T(8,128)S(1)}, f32[2,200,128]{2,1,0:T(8,128)S(1)}, u32[]{:S(2)}, u32[]{:S(2)}) %collective-permute-start.6) | collective-permute-done | bytes 204832 | tf_op jit(solution)/shard_map/ppermute | solution.py:22
  115.4 1.6 %shard_map.125 = f32[2,256,256]{2,1,0:T(8,128)} custom-call(f32[1,1]{1,0:T(1,128)} %get-tuple-element.27.max_ref, f32[2,256,256]{2,1,0:T(8,128)S(1)} %copy-done.1, f32[2,256,256]{2,1,0:T(8,128)S(1)} %get-tuple-element.28.grad_ref, f32[2,520,128]{2,1,0:T(8,128)S(1)} %collective-permute-done.4.right_ref, f32[2,320,128]{2,1,0:T(8,128)S(1)} %collective-permute-done.5.down_ref, ...), custom_call_target="tpu_custom_call" | custom-call | flops 1000000 | bytes 4000000 | tf_op jit(solution)/shard_map/pallas_call | solution.py:445
  117.0 0.0 all-to-all-done.1
  117.0 0.8 copy.13
  (5 shorter events, 0.0 us)
Async XLA Ops:
  0.6 1.0 copy-start
  1.8 11.0 %collective-permute-start.1 = (f32[2,200,128]{2,1,0:T(8,128)S(1)}, f32[2,200,128]{2,1,0:T(8,128)S(1)}, u32[]{:S(2)}, u32[]{:S(2)}) collective-permute-start(f32[2,200,128]{2,1,0:T(8,128)S(1)} %get-tuple-element.21), channel_id=1, source_target_pairs={{8,0},{16,8},{24,16},{9,1},{17,9},{25,17},{10,2},{18,10},{26,18},{... | collective-permute-start | bytes 614408 | tf_op jit(solution)/shard_map/ppermute | solution.py:22
  4.2 19.1 %collective-permute-start = (f32[2,320,128]{2,1,0:T(8,128)S(1)}, f32[2,320,128]{2,1,0:T(8,128)S(1)}, u32[]{:S(2)}, u32[]{:S(2)}) collective-permute-start(f32[2,320,128]{2,1,0:T(8,128)S(1)} %get-tuple-element.20), channel_id=1, source_target_pairs={{1,0},{2,1},{3,2},{4,3},{5,4},{6,5},{7,6},{9,8},{10,9},{11,10},{12... | collective-permute-start | bytes 983048 | tf_op jit(solution)/shard_map/ppermute | solution.py:22
  6.7 16.6 %copy-start.1 = (f32[2,256,256]{2,1,0:T(8,128)S(1)}, f32[2,256,256]{2,1,0:T(8,128)}, u32[]{:S(2)}) copy-start(f32[2,256,256]{2,1,0:T(8,128)} %tile_ref.5) | copy-start | bytes 1572868
  6.7 16.6 %copy-start.2 = (s32[4,2]{0,1:T(2,128)S(1)}, s32[4,2]{0,1:T(2,128)}, u32[]{:S(2)}) copy-start(s32[4,2]{0,1:T(2,128)} %param.14) | copy-start | bytes 100
  6.7 16.6 %copy-start.3 = (bf16[768,256]{1,0:T(8,128)(2,1)S(1)}, bf16[768,256]{1,0:T(8,128)(2,1)}, u32[]{:S(2)}) copy-start(bf16[768,256]{1,0:T(8,128)(2,1)} %constant.29.clone.fwd_right) | copy-start | bytes 1179652
  6.7 16.6 %copy-start.4 = (bf16[256,768]{1,0:T(8,128)(2,1)S(1)}, bf16[256,768]{1,0:T(8,128)(2,1)}, u32[]{:S(2)}) copy-start(bf16[256,768]{1,0:T(8,128)(2,1)} %constant.30.clone.fwd_left) | copy-start | bytes 1179652
  6.7 16.6 %copy-start.7 = (f32[2,128,128]{2,1,0:T(8,128)S(1)}, f32[2,128,128]{2,1,0:T(8,128)}, u32[]{:S(2)}) copy-start(f32[2,128,128]{2,1,0:T(8,128)} %constant.34.clone.row_ref) | copy-start | bytes 393220
  6.7 16.6 %copy-start.8 = (f32[2,8,128]{2,1,0:T(8,128)S(1)}, f32[2,8,128]{2,1,0:T(8,128)}, u32[]{:S(2)}) copy-start(f32[2,8,128]{2,1,0:T(8,128)} %constant.33.clone.lane_ref) | copy-start | bytes 24580
  12.8 10.4 %collective-permute-start.3 = (f32[2,200,128]{2,1,0:T(8,128)S(1)}, f32[2,200,128]{2,1,0:T(8,128)S(1)}, u32[]{:S(2)}, u32[]{:S(2)}) collective-permute-start(f32[2,200,128]{2,1,0:T(8,128)S(1)} %collective-permute-done.1.near_ref), channel_id=1, source_target_pairs={{1,0},{2,1},{3,2},{4,3},{5,4},{6,5},{7,6},{9,8},{10,9},{11,10},{12... | collective-permute-start | bytes 614408 | tf_op jit(solution)/shard_map/ppermute | solution.py:22
  15.7 7.6 %collective-permute-start.2 = (f32[2,160,128]{2,1,0:T(8,128)S(1)}, f32[2,160,128]{2,1,0:T(8,128)S(1)}, u32[]{:S(2)}, u32[]{:S(2)}) collective-permute-start(f32[2,160,128]{2,1,0:T(8,128)S(1)} %get-tuple-element.24), channel_id=1, source_target_pairs={{8,0},{16,8},{24,16},{9,1},{17,9},{25,17},{10,2},{18,10},{26,18},{... | collective-permute-start | bytes 491528 | tf_op jit(solution)/shard_map/ppermute | solution.py:22
  23.3 1.0 copy-start.5
  24.3 1.0 copy-start.6
  25.3 1.6 %copy-start.9 = (f32[4,2,256,256]{3,2,1,0:T(8,128)S(1)}, f32[4,2,256,256]{3,2,1,0:T(8,128)}, u32[]{:S(2)}) copy-start(f32[4,2,256,256]{3,2,1,0:T(8,128)} %get-tuple-element.25.prot_ref) | copy-start | bytes 6291460
  26.9 1.2 %copy-start.10 = (f32[4,256,256]{2,1,0:T(8,128)S(1)}, f32[4,256,256]{2,1,0:T(8,128)}, u32[]{:S(2)}) copy-start(f32[4,256,256]{2,1,0:T(8,128)} %get-tuple-element.26.meas_ref) | copy-start | bytes 3145732
  36.4 14.8 %all-to-all-start = ((f32[8,3,32,256]{3,2,1,0:T(8,128)}), f32[8,3,32,256]{3,2,1,0:T(8,128)S(1)}, u32[]{:S(2)}, u32[]{:S(2)}) async-start(f32[8,3,32,256]{3,2,1,0:T(8,128)} %get-tuple-element.30), calls=%async_computation | async-start | bytes 1572864 | tf_op jit(solution)/shard_map/all_to_all | solution.py:431
  83.7 11.5 %collective-permute-start.4 = (f32[2,520,128]{2,1,0:T(8,128)S(1)}, f32[2,520,128]{2,1,0:T(8,128)S(1)}, u32[]{:S(2)}, u32[]{:S(2)}) collective-permute-start(f32[2,520,128]{2,1,0:T(8,128)S(1)} %get-tuple-element.34), channel_id=1, source_target_pairs={{0,1},{1,2},{2,3},{3,4},{4,5},{5,6},{6,7},{8,9},{9,10},{10,11},{11... | collective-permute-start | bytes 1597448 | tf_op jit(solution)/shard_map/ppermute | solution.py:22
  96.0 21.0 %all-to-all-start.1 = ((f32[8,2,32,256]{3,2,1,0:T(8,128)}), f32[8,2,32,256]{3,2,1,0:T(8,128)S(1)}, u32[]{:S(2)}, u32[]{:S(2)}) async-start(f32[8,2,32,256]{3,2,1,0:T(8,128)} %broadcast_in_dim.4), calls=%async_computation.1 | async-start | bytes 1048576 | tf_op jit(solution)/shard_map/all_to_all | solution.py:442
  99.5 12.5 %collective-permute-start.5 = (f32[2,320,128]{2,1,0:T(8,128)S(1)}, f32[2,320,128]{2,1,0:T(8,128)S(1)}, u32[]{:S(2)}, u32[]{:S(2)}) collective-permute-start(f32[2,320,128]{2,1,0:T(8,128)S(1)} %get-tuple-element.36), channel_id=1, source_target_pairs={{0,8},{8,16},{16,24},{1,9},{9,17},{17,25},{2,10},{10,18},{18,26},{... | collective-permute-start | bytes 983048 | tf_op jit(solution)/shard_map/ppermute | solution.py:22
  102.8 12.6 %collective-permute-start.6 = (f32[2,200,128]{2,1,0:T(8,128)S(1)}, f32[2,200,128]{2,1,0:T(8,128)S(1)}, u32[]{:S(2)}, u32[]{:S(2)}) collective-permute-start(f32[2,200,128]{2,1,0:T(8,128)S(1)} %slice.19), channel_id=1, source_target_pairs={{0,8},{8,16},{16,24},{1,9},{9,17},{17,25},{2,10},{10,18},{18,26},{... | collective-permute-start | bytes 614408 | tf_op jit(solution)/shard_map/ppermute | solution.py:22

commit v2 on v1

--- a/solution.py
+++ b/solution.py
@@ -10,7 +10,6 @@
 
 HALO = 160
 VMEM = pl.BlockSpec(memory_space=pltpu.VMEM)
-HBM = pl.BlockSpec(memory_space=pltpu.HBM)
 SMEM = pl.BlockSpec(memory_space=pltpu.SMEM)
 PARAMS = pltpu.CompilerParams(vmem_limit_bytes=24 * 1024 * 1024)
 BF16 = jnp.bfloat16
@@ -20,6 +19,24 @@
     count = lax.axis_size(axis)
     initial, last = (max(0, -steps), min(count, count - steps))
     return lax.ppermute(value, axis, [(source, source + steps) for source in range(initial, last)])
+
+
+def diagonal(value):
+    rows, cols = lax.axis_size("row"), lax.axis_size("col")
+    pairs = [
+        ((row + 1) * cols + col + 1, row * cols + col) for row in range(rows - 1) for col in range(cols - 1)
+    ]
+    return lax.ppermute(value, ("row", "col"), pairs)
+
+
+def row_sum(value):
+    rows = lax.axis_size("row")
+    if rows != 4:
+        return lax.psum(value, "row")
+    one, two, three = (
+        lax.ppermute(value, "row", [(row, row ^ step) for row in range(rows)]) for step in (1, 2, 3)
+    )
+    return (value + one) + (two + three)
 
 
 def f32(*shape):
@@ -43,9 +60,6 @@
     twiddle = np.stack([np.cos(turn), np.sin(turn)]).astype(np.float32)
     lanes = np.ascontiguousarray(np.broadcast_to(twiddle[:, None, :], (2, 8, half)))
     rows = np.ascontiguousarray(np.broadcast_to(twiddle[:, :, None], (2, half, half)))
-    pick = np.concatenate([np.arange(0, side, 2), np.arange(1, side, 2)])
-    sort = np.zeros((side, side), np.float32)
-    sort[pick, np.arange(side)] = 1.0
     return (
         np.concatenate([high, high, low], 0),
         np.concatenate([high.T, high.T, low.T], 1),
@@ -53,7 +67,6 @@
         np.concatenate([high, high, low], 1),
         lanes,
         rows,
-        np.stack([sort, sort.T]).astype(BF16),
     )
 
 
@@ -73,19 +86,20 @@
         yield group * 8, group // per * 8, group % per * extra
 
 
-def pack_kernel(tile_ref, near_ref, far_ref, right_ref):
-    margin = far_ref.shape[1]
+def pack_kernel(tile_ref, below_ref, corner_ref, right_ref):
     side = tile_ref.shape[1]
-    half = far_ref.shape[2]
+    half = side // 2
+    margin = below_ref.shape[1] // 2
     extra = margin - half
-    near_ref[:, 0:margin, :] = tile_ref[:, 0:margin, 0:half]
-    far_ref[...] = tile_ref[:, 0:margin, half:]
+    below_ref[:, 0:margin, :] = tile_ref[:, 0:margin, 0:half]
+    below_ref[:, margin : 2 * margin, :] = tile_ref[:, 0:margin, half:]
+    corner_ref[:, 0:margin, :] = tile_ref[:, 0:margin, 0:half]
     right_ref[:, 0:side, :] = tile_ref[:, :, 0:half]
     for row, packed, lane in pack_extra(side, extra, half):
         piece = tile_ref[:, row : row + 8, half:margin]
         right_ref[:, side + packed : side + packed + 8, lane : lane + extra] = piece
         if row < margin:
-            near_ref[:, margin + packed : margin + packed + 8, lane : lane + extra] = piece
+            corner_ref[:, margin + packed : margin + packed + 8, lane : lane + extra] = piece
 
 
 def turned(load, steps, half, lanes):
@@ -98,16 +112,9 @@
     return jnp.where(stay, one, two), jnp.where(stay, two, one)
 
 
-def prepare_kernel(
-    pos_ref, probe_hbm, meas_hbm, sort_hbm, prot_ref, sorted_ref, probe_ref, meas_ref, sort_ref, twice, sems
-):
+def prepare_kernel(pos_ref, probe_ref, meas_ref, prot_ref, sorted_ref, twice):
     frames, side = meas_ref.shape[0], meas_ref.shape[1]
     half = side // 2
-    pairs = ((probe_hbm, probe_ref), (sort_hbm, sort_ref), (meas_hbm, meas_ref))
-    copies = [pltpu.make_async_copy(source, target, sems.at[index]) for index, (source, target) in enumerate(pairs)]
-    for copy in copies:
-        copy.start()
-    copies[0].wait()
     for part in range(2):
         for tile in range(2):
             piece = probe_ref[part, :, tile * half : (tile + 1) * half]
@@ -115,6 +122,10 @@
             twice[part, tile, side : 2 * side] = piece
     step = 64
     lanes = lax.broadcasted_iota(jnp.int32, (step, half), 1)
+    rows = lax.broadcasted_iota(jnp.int32, (side, side), 0)
+    cols = lax.broadcasted_iota(jnp.int32, (side, side), 1)
+    sort = jnp.where(rows == jnp.where(cols < half, 2 * cols, 2 * cols - side + 1), 1.0, 0.0).astype(BF16)
+    unsort = jnp.where(cols == jnp.where(rows < half, 2 * rows, 2 * rows - side + 1), 1.0, 0.0).astype(BF16)
 
     @pl.loop(0, frames)
     def _(frame):
@@ -127,31 +138,25 @@
                 )
                 prot_ref[frame, part, row : row + step, 0:half] = one
                 prot_ref[frame, part, row : row + step, half:side] = two
-
-    copies[1].wait()
-    copies[2].wait()
-
-    @pl.loop(0, frames)
-    def _(frame):
         value = meas_ref[frame]
         total = None
         for _ in range(3):
             piece = value.astype(BF16)
             value = value - piece.astype(jnp.float32)
-            term = dot(dot(sort_ref[1], piece).astype(BF16), sort_ref[0])
+            term = dot(dot(unsort, piece).astype(BF16), sort)
             total = term if total is None else total + term
         sorted_ref[frame] = total
 
 
 def frame_kernel(
-    pos_ref, tile_ref, right_ref, near_ref, far_ref, corner_ref, prot_ref, meas_ref,
+    pos_ref, tile_ref, right_ref, below_ref, corner_ref, prot_ref, meas_ref,
     fwd_right, fwd_left, inv_right, inv_left, lane_ref, row_ref,
     gt_ref, gr_ref, gz_ref, qs_ref, max_ref,
     right_extra, corner_extra, obj_ref, left_in, right_in, mid, twice,
 ):
     frames, side = meas_ref.shape[0], meas_ref.shape[1]
     half = side // 2
-    margin = far_ref.shape[1]
+    margin = below_ref.shape[1] // 2
     wide = right_ref.shape[1]
     extra = margin - half
     for row, packed, lane in pack_extra(side, extra, half):
@@ -194,7 +199,7 @@
                     right = right_extra[part, rows] if tile else right_ref[part, rows]
                     value = jnp.where(own_col[tile], tile_ref[part, rows, columns], right)
                     if row < margin:
-                        below = far_ref[part, rows] if tile else near_ref[part, rows]
+                        below = below_ref[part, tile * margin + row : tile * margin + row + step]
                         corner = corner_extra[part, rows] if tile else corner_ref[part, rows]
                         value = jnp.where(own_row, value, jnp.where(own_col[tile], below, corner))
                     obj_ref[frame, part, rows, columns] = value
@@ -366,39 +371,31 @@
     extra = margin - half
     frames = measured.shape[0]
     n_row, n_col = lax.axis_size("row"), lax.axis_size("col")
-    fwd_right, fwd_left, inv_right, inv_left, lane_tw, row_tw, sort = tables(side)
+    fwd_right, fwd_left, inv_right, inv_left, lane_tw, row_tw = tables(side)
     wide = side + side * extra // half
     tall = margin + margin * extra // half
 
-    near, far, right = pl.pallas_call(
+    below, corner, right = pl.pallas_call(
         pack_kernel,
-        out_shape=(f32(2, tall, half), f32(2, margin, half), f32(2, wide, half)),
+        out_shape=(f32(2, 2 * margin, half), f32(2, tall, half), f32(2, wide, half)),
         in_specs=[VMEM],
         out_specs=(VMEM,) * 3,
         cost_estimate=cost(10**6, 2 * 10**6),
         compiler_params=PARAMS,
     )(object_field)
-    near = shifted(near, "row", -1)
-    far = shifted(far, "row", -1)
+    below = shifted(below, "row", -1)
+    corner = diagonal(corner)
     right = shifted(right, "col", -1)
     places = positions.T
     prot, ampl = pl.pallas_call(
         prepare_kernel,
         out_shape=(f32(frames, 2, side, side), f32(frames, side, side)),
-        in_specs=[SMEM, HBM, HBM, HBM],
+        in_specs=[SMEM, VMEM, VMEM],
         out_specs=(VMEM, VMEM),
-        scratch_shapes=[
-            pltpu.VMEM((2, side, side), jnp.float32),
-            pltpu.VMEM((frames, side, side), jnp.float32),
-            pltpu.VMEM((2, side, side), BF16),
-            pltpu.VMEM((2, 2, 2 * side, half), jnp.float32),
-            pltpu.SemaphoreType.DMA((3,)),
-        ],
+        scratch_shapes=[pltpu.VMEM((2, 2, 2 * side, half), jnp.float32)],
         cost_estimate=cost(3 * 10**9, 6 * 10**6),
-        compiler_params=pltpu.CompilerParams(vmem_limit_bytes=60 * 1024 * 1024),
-    )(places, probe_field, measured, sort)
-    near, prot = lax.optimization_barrier((near, prot))
-    corner = shifted(near, "col", -1)
+        compiler_params=PARAMS,
+    )(places, probe_field, measured)
     depth = side // n_col
     g_tile, g_right, g_down, sums, largest = pl.pallas_call(
         frame_kernel,
@@ -409,7 +406,7 @@
             f32(n_col, 3, depth, side),
             f32(1, 1),
         ),
-        in_specs=[SMEM] + [VMEM] * 13,
+        in_specs=[SMEM] + [VMEM] * 12,
         out_specs=(VMEM,) * 4 + (SMEM,),
         scratch_shapes=[
             pltpu.VMEM((2, side, half), jnp.float32),
@@ -423,19 +420,15 @@
         cost_estimate=cost(6 * 10**9, 12 * 10**6),
         compiler_params=PARAMS,
     )(
-        places, object_field, right, near, far, corner, prot, ampl,
+        places, object_field, right, below, corner, prot, ampl,
         fwd_right, fwd_left, inv_right, inv_left, lane_tw, row_tw,
     )
 
     from_above = shifted(g_down, "row", 1)
     part = jnp.sum(lax.all_to_all(sums, "col", 0, 0), 0)
-    g_right, part = lax.optimization_barrier((g_right, part))
+    g_right, part, from_above = lax.optimization_barrier((g_right, part, from_above))
     from_left = shifted(g_right, "col", 1)
-    first, second = part[:, : depth // 2], part[:, depth // 2 :]
-    first = lax.psum(first, "row")
-    first, second = lax.optimization_barrier((first, second))
-    second = lax.psum(second, "row")
-    part = jnp.concatenate([first, second], 1)
+    part = row_sum(part)
     old = lax.dynamic_slice_in_dim(probe_field, lax.axis_index("col") * depth, depth, 1)
     new = old + part[:2] / (part[2] + 1.0)
     new, from_left = lax.optimization_barrier((new, from_left))

time: 119 us -> 76.4 us (0.64)
  blocking collectives: 32.4 us -> 0 us
  waiting for transfers between devices: 35.7 us -> 26.8 us
  Pallas kernels: 16.1 us -> 12.7 us
  starting transfers between devices: 24.3 us -> 26.3 us
  local copies, waits for them, and re-layouts: 7.6 us -> 5.71 us
  other arithmetic: 0.93 us -> 2.48 us
    psum x2 -> x0, blocking collectives: 32.4 us -> none  [the longest x1 16.6 us: body(): second = lax.psum(second, 'row')]
    ppermute x7 -> x5, waiting for transfers between devices: 24.5 us -> 7.13 us  [shifted(): lax.ppermute(value, axis, [(source, source + steps) for source in range(i...]
    ppermute x0 -> x4, waiting for transfers between devices: none -> 10.2 us  [the longest x3 6.49 us: row_sum(): lax.ppermute(value, 'row', [(row, row ^ step) for row in range(rows)])]
    ppermute x0 -> x4, starting transfers between devices: none -> 5.68 us  [the longest x3 3.49 us: row_sum(): lax.ppermute(value, 'row', [(row, row ^ step) for row in range(rows)])]
    ppermute x7 -> x5, starting transfers between devices: 17.2 us -> 11.9 us  [shifted(): lax.ppermute(value, axis, [(source, source + steps) for source in range(i...]
    pallas_call x1, Pallas kernels: 6.09 us -> 2.84 us  [body(): pl.pallas_call(prepare_kernel, out_shape=(f32(frames, 2, side, side), f32...]
    unnamed x23 -> x22, local copies, waits for them, and re-layouts: 5.88 us -> 4.01 us
    all_to_all x1, waiting for transfers between devices: 11.1 us -> 9.43 us  [body(): part = jnp.sum(lax.all_to_all(sums, 'col', 0, 0), 0)]
  transfers between devices with their start and end apart: 9 -> 11, of which waited for: 5 -> 7; matrix products, arithmetic and copies ran while one was open for 1% -> 3% of each run, Pallas kernels for 7% -> 6%
where the time goes in v2:
time: 76.4 us; the launch traced here: 74.8 us
  waiting for transfers between devices  26.8 us (35%)
  starting transfers between devices  26.3 us (34%)
  Pallas kernels  12.7 us (17%)
  local copies, waits for them, and re-layouts  5.71 us (7%)
  other arithmetic  2.48 us (3%)
  between operations  0.82 us (1%)
    ppermute x5, starting transfers between devices, shifted(): lax.ppermute(value, axis, [(source, source + steps) for source in range(i...  11.9 us
    all_to_all x1, waiting for transfers between devices, body(): part = jnp.sum(lax.all_to_all(sums, 'col', 0, 0), 0)  9.43 us
    pallas_call x1, Pallas kernels, body(): pl.pallas_call(frame_kernel, out_shape=(f32(2, side, side), f32(2, wide +...  8.15 us
    ppermute x5, waiting for transfers between devices, shifted(): lax.ppermute(value, axis, [(source, source + steps) for source in range(i...  7.13 us
    ppermute x3, waiting for transfers between devices, row_sum(): lax.ppermute(value, 'row', [(row, row ^ step) for row in range(rows)])  6.49 us
    all_to_all x1, starting transfers between devices, body(): part = jnp.sum(lax.all_to_all(sums, 'col', 0, 0), 0)  5.23 us
    unnamed x22, local copies, waits for them, and re-layouts  4.01 us
    ppermute x1, waiting for transfers between devices, diagonal(): return lax.ppermute(value, ('row', 'col'), pairs)  3.75 us
  transfers between devices with their start and end apart: 11, of which 7 were waited for; matrix products, arithmetic and copies ran while one was open for 3% of the time, Pallas kernels for 6%

profile of v2, /device:TPU:20, one launch (start us, length us, event | category | flops | bytes accessed | tf_op | source)
XLA Modules:
  0.0 74.8 jit_solution(3941353463196612497)
XLA Ops:
  0.6 0.0 copy-start
  0.6 1.0 %copy-done = f32[2,256,256]{2,1,0:T(8,128)S(1)} copy-done((f32[2,256,256]{2,1,0:T(8,128)S(1)}, f32[2,256,256]{2,1,0:T(8,128)}, u32[]{:S(2)}) %copy-start) | copy-done | bytes 524312
  1.7 0.1 shard_map.113
  1.8 2.8 %collective-permute-start = (f32[2,320,128]{2,1,0:T(8,128)S(1)}, f32[2,320,128]{2,1,0:T(8,128)S(1)}, u32[]{:S(2)}, u32[]{:S(2)}) collective-permute-start(f32[2,320,128]{2,1,0:T(8,128)S(1)} %get-tuple-element.17), channel_id=1, source_target_pairs={{1,0},{2,1},{3,2},{4,3},{5,4},{6,5},{7,6},{9,8},{10,9},{11,10},{12... | collective-permute-start | bytes 983048 | tf_op jit(solution)/shard_map/ppermute | solution.py:21
  4.6 2.4 %collective-permute-start.1 = (f32[2,320,128]{2,1,0:T(8,128)S(1)}, f32[2,320,128]{2,1,0:T(8,128)S(1)}, u32[]{:S(2)}, u32[]{:S(2)}) collective-permute-start(f32[2,320,128]{2,1,0:T(8,128)S(1)} %get-tuple-element.18), channel_id=1, source_target_pairs={{8,0},{16,8},{24,16},{9,1},{17,9},{25,17},{10,2},{18,10},{26,18},{... | collective-permute-start | bytes 983048 | tf_op jit(solution)/shard_map/ppermute | solution.py:21
  6.9 2.2 %collective-permute-start.2 = (f32[2,200,128]{2,1,0:T(8,128)S(1)}, f32[2,200,128]{2,1,0:T(8,128)S(1)}, u32[]{:S(2)}, u32[]{:S(2)}) collective-permute-start(f32[2,200,128]{2,1,0:T(8,128)S(1)} %get-tuple-element.19), channel_id=1, source_target_pairs={{9,0},{10,1},{11,2},{12,3},{13,4},{14,5},{15,6},{17,8},{18,9},{19,... | collective-permute-start | bytes 614408 | tf_op jit(solution)/shard_map/ppermute | solution.py:29
  9.1 0.0 copy-start.2
  9.2 1.0 %copy-done.2 = f32[2,256,256]{2,1,0:T(8,128)S(1)} copy-done((f32[2,256,256]{2,1,0:T(8,128)S(1)}, f32[2,256,256]{2,1,0:T(8,128)}, u32[]{:S(2)}) %copy-start.2) | copy-done | bytes 524312
  10.2 0.0 copy-start.3
  10.2 1.2 %copy-done.3 = f32[4,256,256]{2,1,0:T(8,128)S(1)} copy-done((f32[4,256,256]{2,1,0:T(8,128)S(1)}, f32[4,256,256]{2,1,0:T(8,128)}, u32[]{:S(2)}) %copy-start.3) | copy-done | bytes 1048600
  11.4 0.0 copy-start.4
  11.4 0.7 copy-done.4
  12.1 0.0 copy-start.1
  12.1 0.0 copy-start.5
  12.1 0.0 copy-start.6
  12.1 0.0 copy-start.7
  12.1 0.0 copy-start.8
  12.1 0.0 copy-start.9
  12.1 0.0 copy-start.10
  12.1 2.8 %shard_map.114 = (f32[4,2,256,256]{3,2,1,0:T(8,128)S(1)}, f32[4,256,256]{2,1,0:T(8,128)S(1)}) custom-call(s32[2,4]{1,0:T(2,128)S(1)} %bitcast.6, f32[2,256,256]{2,1,0:T(8,128)S(1)} %copy-done.2, f32[4,256,256]{2,1,0:T(8,128)S(1)} %copy-done.3), custom_call_target="tpu_custom_call" | custom-call | flops 3000000000 | bytes 6000000 | tf_op jit(solution)/shard_map/pallas_call | solution.py:390
  15.0 3.8 %collective-permute-done.2.corner_ref = f32[2,200,128]{2,1,0:T(8,128)S(1)} collective-permute-done((f32[2,200,128]{2,1,0:T(8,128)S(1)}, f32[2,200,128]{2,1,0:T(8,128)S(1)}, u32[]{:S(2)}, u32[]{:S(2)}) %collective-permute-start.2) | collective-permute-done | bytes 204832 | tf_op jit(solution)/shard_map/ppermute | solution.py:29
  18.7 0.0 collective-permute-done.right_ref
  18.7 0.0 collective-permute-done.1.below_ref
  18.7 0.0 copy-done.1
  18.7 0.0 copy-done.5
  18.8 0.0 copy-done.6
  18.8 0.0 copy-done.7
  18.8 0.0 copy-done.8
  18.8 0.0 copy-done.9
  18.8 0.0 copy-done.10
  18.8 8.2 %shard_map.115 = (f32[2,256,256]{2,1,0:T(8,128)S(1)}, f32[2,520,128]{2,1,0:T(8,128)S(1)}, f32[2,320,128]{2,1,0:T(8,128)S(1)}, f32[8,3,32,256]{3,2,1,0:T(8,128)}, f32[1,1]{1,0:T(1,128)}) custom-call(s32[2,4]{1,0:T(2,128)S(1)} %bitcast.7, f32[2,256,256]{2,1,0:T(8,128)S(1)} %copy-done.1, f32[2,320,128]{2,1,0:T(8,128)S(1)} %collective-permute-done.right_ref, ...), custom_call_target="tpu_custom_call" | custom-call | flops 6000000000 | bytes 12000000 | tf_op jit(solution)/shard_map/pallas_call | solution.py:400
  27.0 5.2 %all-to-all-start = ((f32[8,3,32,256]{3,2,1,0:T(8,128)}), f32[8,3,32,256]{3,2,1,0:T(8,128)S(1)}, u32[]{:S(2)}, u32[]{:S(2)}) async-start(f32[8,3,32,256]{3,2,1,0:T(8,128)} %get-tuple-element.25), calls=%async_computation | async-start | bytes 1572864 | tf_op jit(solution)/shard_map/all_to_all | solution.py:428
  32.2 1.9 %collective-permute-start.3 = (f32[2,320,128]{2,1,0:T(8,128)S(1)}, f32[2,320,128]{2,1,0:T(8,128)S(1)}, u32[]{:S(2)}, u32[]{:S(2)}) collective-permute-start(f32[2,320,128]{2,1,0:T(8,128)S(1)} %get-tuple-element.26), channel_id=1, source_target_pairs={{0,8},{8,16},{16,24},{1,9},{9,17},{17,25},{2,10},{10,18},{18,26},{... | collective-permute-start | bytes 983048 | tf_op jit(solution)/shard_map/ppermute | solution.py:21
  34.1 9.4 %all-to-all-done = f32[8,3,32,256]{3,2,1,0:T(8,128)S(1)} async-done(((f32[8,3,32,256]{3,2,1,0:T(8,128)}), f32[8,3,32,256]{3,2,1,0:T(8,128)S(1)}, u32[]{:S(2)}, u32[]{:S(2)}) %all-to-all-start) | async-done | bytes 786464 | tf_op jit(solution)/shard_map/all_to_all | solution.py:428
  43.5 0.7 reduce_sum.9
  44.2 0.0 collective-permute-done.3.down_ref
  44.2 0.2 collective-permute-start.4
  44.4 1.7 %collective-permute-start.5 = (f32[3,32,256]{2,1,0:T(8,128)}, f32[3,32,256]{2,1,0:T(8,128)S(1)}, u32[]{:S(2)}, u32[]{:S(2)}) collective-permute-start(f32[3,32,256]{2,1,0:T(8,128)} %reduce_sum.9), channel_id=1, source_target_pairs={{0,16},{8,24},{16,0},{24,8},{1,17},{9,25},{17,1},{25,9},{2,18},{10... | collective-permute-start | bytes 294920 | tf_op jit(solution)/shard_map/ppermute | solution.py:37
  46.1 1.6 %collective-permute-start.6 = (f32[3,32,256]{2,1,0:T(8,128)}, f32[3,32,256]{2,1,0:T(8,128)S(1)}, u32[]{:S(2)}, u32[]{:S(2)}) collective-permute-start(f32[3,32,256]{2,1,0:T(8,128)} %reduce_sum.9), channel_id=1, source_target_pairs={{0,24},{8,16},{16,8},{24,0},{1,25},{9,17},{17,9},{25,1},{2,26},{10... | collective-permute-start | bytes 294920 | tf_op jit(solution)/shard_map/ppermute | solution.py:37
  47.7 1.9 %collective-permute-start.7 = (f32[2,520,128]{2,1,0:T(8,128)S(1)}, f32[2,520,128]{2,1,0:T(8,128)S(1)}, u32[]{:S(2)}, u32[]{:S(2)}) collective-permute-start(f32[2,520,128]{2,1,0:T(8,128)S(1)} %get-tuple-element.28), channel_id=1, source_target_pairs={{0,1},{1,2},{2,3},{3,4},{4,5},{5,6},{6,7},{8,9},{9,10},{10,11},{11... | collective-permute-start | bytes 1597448 | tf_op jit(solution)/shard_map/ppermute | solution.py:21
  49.6 0.5 collective-permute-done.4
  50.2 3.1 %collective-permute-done.5 = f32[3,32,256]{2,1,0:T(8,128)S(1)} collective-permute-done((f32[3,32,256]{2,1,0:T(8,128)}, f32[3,32,256]{2,1,0:T(8,128)S(1)}, u32[]{:S(2)}, u32[]{:S(2)}) %collective-permute-start.5) | collective-permute-done | bytes 98336 | tf_op jit(solution)/shard_map/ppermute | solution.py:37
  53.2 2.9 %collective-permute-done.6 = f32[3,32,256]{2,1,0:T(8,128)S(1)} collective-permute-done((f32[3,32,256]{2,1,0:T(8,128)}, f32[3,32,256]{2,1,0:T(8,128)S(1)}, u32[]{:S(2)}, u32[]{:S(2)}) %collective-permute-start.6) | collective-permute-done | bytes 98336 | tf_op jit(solution)/shard_map/ppermute | solution.py:37
  56.1 0.9 %add_add_fusion = f32[3,32,256]{2,1,0:T(8,128)S(1)} fusion(f32[3,32,256]{2,1,0:T(8,128)S(1)} %collective-permute-done.5, f32[3,32,256]{2,1,0:T(8,128)S(1)} %collective-permute-done.6, f32[3,32,256]{2,1,0:T(8,128)} %reduce_sum.9, f32[3,32,256]{2,1,0:T(8,128)S(1)} %collective-permute-done.4), kind=kLoop, calls=%fused_computation | loop fusion | flops 73728 | bytes 491520 | tf_op jit(solution)/shard_map/add | solution.py:39
  57.1 0.9 %fusion = f32[2,32,256]{2,1,0:T(8,128)S(1)} fusion(f32[3,32,256]{2,1,0:T(8,128)S(1)} %add_add_fusion, f32[2,256,256]{2,1,0:T(8,128)} %probe_ref.1, s32[]{:T(128)S(6)} %select_n.3, f32[32,256]{1,0:T(8,128)S(1)} %fusion.1), kind=kLoop, calls=%fused_computation.2 | loop fusion | flops 32768 | bytes 229380 | tf_op jit(solution)/shard_map/add | solution.py:433
  57.9 1.3 %collective-permute-done.7.right_ref = f32[2,520,128]{2,1,0:T(8,128)S(1)} collective-permute-done((f32[2,520,128]{2,1,0:T(8,128)S(1)}, f32[2,520,128]{2,1,0:T(8,128)S(1)}, u32[]{:S(2)}, u32[]{:S(2)}) %collective-permute-start.7) | collective-permute-done | bytes 532512 | tf_op jit(solution)/shard_map/ppermute | solution.py:21
  59.2 0.8 %broadcast_in_dim.4 = f32[8,2,32,256]{3,2,1,0:T(8,128)} broadcast(f32[2,32,256]{2,1,0:T(8,128)S(1)} %fusion), dimensions={1,2,3} | broadcast | bytes 589824 | tf_op jit(solution)/shard_map/broadcast_in_dim | solution.py:435
  60.0 3.4 %all-to-all-start.1 = ((f32[8,2,32,256]{3,2,1,0:T(8,128)}), f32[8,2,32,256]{3,2,1,0:T(8,128)S(1)}, u32[]{:S(2)}, u32[]{:S(2)}) async-start(f32[8,2,32,256]{3,2,1,0:T(8,128)} %broadcast_in_dim.4), calls=%async_computation.1 | async-start | bytes 1048576 | tf_op jit(solution)/shard_map/all_to_all | solution.py:435
  63.5 3.0 %collective-permute-start.8 = (f32[2,200,128]{2,1,0:T(8,128)S(1)}, f32[2,200,128]{2,1,0:T(8,128)S(1)}, u32[]{:S(2)}, u32[]{:S(2)}) collective-permute-start(f32[2,200,128]{2,1,0:T(8,128)S(1)} %slice.11), channel_id=1, source_target_pairs={{0,8},{8,16},{16,24},{1,9},{9,17},{17,25},{2,10},{10,18},{18,26},{... | collective-permute-start | bytes 614408 | tf_op jit(solution)/shard_map/ppermute | solution.py:21
  66.5 5.9 %collective-permute-done.8.corner_ref = f32[2,200,128]{2,1,0:T(8,128)S(1)} collective-permute-done((f32[2,200,128]{2,1,0:T(8,128)S(1)}, f32[2,200,128]{2,1,0:T(8,128)S(1)}, u32[]{:S(2)}, u32[]{:S(2)}) %collective-permute-start.8) | collective-permute-done | bytes 204832 | tf_op jit(solution)/shard_map/ppermute | solution.py:21
  72.4 1.6 %shard_map.116 = f32[2,256,256]{2,1,0:T(8,128)} custom-call(f32[1,1]{1,0:T(1,128)} %get-tuple-element.22.max_ref, f32[2,256,256]{2,1,0:T(8,128)S(1)} %copy-done.1, f32[2,256,256]{2,1,0:T(8,128)S(1)} %get-tuple-element.23.grad_ref, f32[2,520,128]{2,1,0:T(8,128)S(1)} %collective-permute-done.7.right_ref, f32[2,320,128]{2,1,0:T(8,128)S(1)} %collective-permute-done.3.down_ref, ...), custom_call_target="tpu_custom_call" | custom-call | flops 1000000 | bytes 4000000 | tf_op jit(solution)/shard_map/pallas_call | solution.py:438
  74.0 0.0 all-to-all-done.1
  74.0 0.8 %copy.12 = f32[8,2,32,256]{3,2,0,1:T(8,128)} copy(f32[8,2,32,256]{3,2,1,0:T(8,128)S(1)} %all-to-all-done.1) | data formatting | bytes 1048576 | tf_op jit(solution)/shard_map/all_to_all | solution.py:435
  (2 shorter events, 0.0 us)
Async XLA Ops:
  0.6 1.0 %copy-start = (f32[2,256,256]{2,1,0:T(8,128)S(1)}, f32[2,256,256]{2,1,0:T(8,128)}, u32[]{:S(2)}) copy-start(f32[2,256,256]{2,1,0:T(8,128)} %tile_ref.5) | copy-start | bytes 1572868
  1.8 16.9 %collective-permute-start = (f32[2,320,128]{2,1,0:T(8,128)S(1)}, f32[2,320,128]{2,1,0:T(8,128)S(1)}, u32[]{:S(2)}, u32[]{:S(2)}) collective-permute-start(f32[2,320,128]{2,1,0:T(8,128)S(1)} %get-tuple-element.17), channel_id=1, source_target_pairs={{1,0},{2,1},{3,2},{4,3},{5,4},{6,5},{7,6},{9,8},{10,9},{11,10},{12... | collective-permute-start | bytes 983048 | tf_op jit(solution)/shard_map/ppermute | solution.py:21
  4.6 14.2 %collective-permute-start.1 = (f32[2,320,128]{2,1,0:T(8,128)S(1)}, f32[2,320,128]{2,1,0:T(8,128)S(1)}, u32[]{:S(2)}, u32[]{:S(2)}) collective-permute-start(f32[2,320,128]{2,1,0:T(8,128)S(1)} %get-tuple-element.18), channel_id=1, source_target_pairs={{8,0},{16,8},{24,16},{9,1},{17,9},{25,17},{10,2},{18,10},{26,18},{... | collective-permute-start | bytes 983048 | tf_op jit(solution)/shard_map/ppermute | solution.py:21
  6.9 11.8 %collective-permute-start.2 = (f32[2,200,128]{2,1,0:T(8,128)S(1)}, f32[2,200,128]{2,1,0:T(8,128)S(1)}, u32[]{:S(2)}, u32[]{:S(2)}) collective-permute-start(f32[2,200,128]{2,1,0:T(8,128)S(1)} %get-tuple-element.19), channel_id=1, source_target_pairs={{9,0},{10,1},{11,2},{12,3},{13,4},{14,5},{15,6},{17,8},{18,9},{19,... | collective-permute-start | bytes 614408 | tf_op jit(solution)/shard_map/ppermute | solution.py:29
  9.1 1.0 %copy-start.2 = (f32[2,256,256]{2,1,0:T(8,128)S(1)}, f32[2,256,256]{2,1,0:T(8,128)}, u32[]{:S(2)}) copy-start(f32[2,256,256]{2,1,0:T(8,128)} %probe_ref.1) | copy-start | bytes 1572868
  10.2 1.2 %copy-start.3 = (f32[4,256,256]{2,1,0:T(8,128)S(1)}, f32[4,256,256]{2,1,0:T(8,128)}, u32[]{:S(2)}) copy-start(f32[4,256,256]{2,1,0:T(8,128)} %meas_ref.1) | copy-start | bytes 3145732
  11.4 0.7 copy-start.4
  12.1 6.6 %copy-start.1 = (f32[2,256,256]{2,1,0:T(8,128)S(1)}, f32[2,256,256]{2,1,0:T(8,128)}, u32[]{:S(2)}) copy-start(f32[2,256,256]{2,1,0:T(8,128)} %tile_ref.5) | copy-start | bytes 1572868
  12.1 6.7 %copy-start.5 = (bf16[768,256]{1,0:T(8,128)(2,1)S(1)}, bf16[768,256]{1,0:T(8,128)(2,1)}, u32[]{:S(2)}) copy-start(bf16[768,256]{1,0:T(8,128)(2,1)} %constant.26.clone.fwd_right) | copy-start | bytes 1179652
  12.1 6.7 %copy-start.6 = (bf16[256,768]{1,0:T(8,128)(2,1)S(1)}, bf16[256,768]{1,0:T(8,128)(2,1)}, u32[]{:S(2)}) copy-start(bf16[256,768]{1,0:T(8,128)(2,1)} %constant.27.clone.fwd_left) | copy-start | bytes 1179652
  12.1 6.7 %copy-start.7 = (bf16[768,256]{1,0:T(8,128)(2,1)S(1)}, bf16[768,256]{1,0:T(8,128)(2,1)}, u32[]{:S(2)}) copy-start(bf16[768,256]{1,0:T(8,128)(2,1)} %constant.28.clone.inv_right) | copy-start | bytes 1179652
  12.1 6.7 %copy-start.8 = (bf16[256,768]{1,0:T(8,128)(2,1)S(1)}, bf16[256,768]{1,0:T(8,128)(2,1)}, u32[]{:S(2)}) copy-start(bf16[256,768]{1,0:T(8,128)(2,1)} %constant.29.clone.inv_left) | copy-start | bytes 1179652
  12.1 6.7 %copy-start.9 = (f32[2,128,128]{2,1,0:T(8,128)S(1)}, f32[2,128,128]{2,1,0:T(8,128)}, u32[]{:S(2)}) copy-start(f32[2,128,128]{2,1,0:T(8,128)} %constant.31.clone.row_ref) | copy-start | bytes 393220
  12.1 6.7 %copy-start.10 = (f32[2,8,128]{2,1,0:T(8,128)S(1)}, f32[2,8,128]{2,1,0:T(8,128)}, u32[]{:S(2)}) copy-start(f32[2,8,128]{2,1,0:T(8,128)} %constant.30.clone.lane_ref) | copy-start | bytes 24580
  27.0 16.6 %all-to-all-start = ((f32[8,3,32,256]{3,2,1,0:T(8,128)}), f32[8,3,32,256]{3,2,1,0:T(8,128)S(1)}, u32[]{:S(2)}, u32[]{:S(2)}) async-start(f32[8,3,32,256]{3,2,1,0:T(8,128)} %get-tuple-element.25), calls=%async_computation | async-start | bytes 1572864 | tf_op jit(solution)/shard_map/all_to_all | solution.py:428
  32.2 12.0 %collective-permute-start.3 = (f32[2,320,128]{2,1,0:T(8,128)S(1)}, f32[2,320,128]{2,1,0:T(8,128)S(1)}, u32[]{:S(2)}, u32[]{:S(2)}) collective-permute-start(f32[2,320,128]{2,1,0:T(8,128)S(1)} %get-tuple-element.26), channel_id=1, source_target_pairs={{0,8},{8,16},{16,24},{1,9},{9,17},{17,25},{2,10},{10,18},{18,26},{... | collective-permute-start | bytes 983048 | tf_op jit(solution)/shard_map/ppermute | solution.py:21
  44.2 5.9 %collective-permute-start.4 = (f32[3,32,256]{2,1,0:T(8,128)}, f32[3,32,256]{2,1,0:T(8,128)S(1)}, u32[]{:S(2)}, u32[]{:S(2)}) collective-permute-start(f32[3,32,256]{2,1,0:T(8,128)} %reduce_sum.9), channel_id=1, source_target_pairs={{0,8},{8,0},{16,24},{24,16},{1,9},{9,1},{17,25},{25,17},{2,10},{10... | collective-permute-start | bytes 294920 | tf_op jit(solution)/shard_map/ppermute | solution.py:37
  44.4 8.8 %collective-permute-start.5 = (f32[3,32,256]{2,1,0:T(8,128)}, f32[3,32,256]{2,1,0:T(8,128)S(1)}, u32[]{:S(2)}, u32[]{:S(2)}) collective-permute-start(f32[3,32,256]{2,1,0:T(8,128)} %reduce_sum.9), channel_id=1, source_target_pairs={{0,16},{8,24},{16,0},{24,8},{1,17},{9,25},{17,1},{25,9},{2,18},{10... | collective-permute-start | bytes 294920 | tf_op jit(solution)/shard_map/ppermute | solution.py:37
  46.1 10.0 %collective-permute-start.6 = (f32[3,32,256]{2,1,0:T(8,128)}, f32[3,32,256]{2,1,0:T(8,128)S(1)}, u32[]{:S(2)}, u32[]{:S(2)}) collective-permute-start(f32[3,32,256]{2,1,0:T(8,128)} %reduce_sum.9), channel_id=1, source_target_pairs={{0,24},{8,16},{16,8},{24,0},{1,25},{9,17},{17,9},{25,1},{2,26},{10... | collective-permute-start | bytes 294920 | tf_op jit(solution)/shard_map/ppermute | solution.py:37
  47.7 11.5 %collective-permute-start.7 = (f32[2,520,128]{2,1,0:T(8,128)S(1)}, f32[2,520,128]{2,1,0:T(8,128)S(1)}, u32[]{:S(2)}, u32[]{:S(2)}) collective-permute-start(f32[2,520,128]{2,1,0:T(8,128)S(1)} %get-tuple-element.28), channel_id=1, source_target_pairs={{0,1},{1,2},{2,3},{3,4},{4,5},{5,6},{6,7},{8,9},{9,10},{10,11},{11... | collective-permute-start | bytes 1597448 | tf_op jit(solution)/shard_map/ppermute | solution.py:21
  60.0 14.0 %all-to-all-start.1 = ((f32[8,2,32,256]{3,2,1,0:T(8,128)}), f32[8,2,32,256]{3,2,1,0:T(8,128)S(1)}, u32[]{:S(2)}, u32[]{:S(2)}) async-start(f32[8,2,32,256]{3,2,1,0:T(8,128)} %broadcast_in_dim.4), calls=%async_computation.1 | async-start | bytes 1048576 | tf_op jit(solution)/shard_map/all_to_all | solution.py:435
  63.5 8.9 %collective-permute-start.8 = (f32[2,200,128]{2,1,0:T(8,128)S(1)}, f32[2,200,128]{2,1,0:T(8,128)S(1)}, u32[]{:S(2)}, u32[]{:S(2)}) collective-permute-start(f32[2,200,128]{2,1,0:T(8,128)S(1)} %slice.11), channel_id=1, source_target_pairs={{0,8},{8,16},{16,24},{1,9},{9,17},{17,25},{2,10},{10,18},{18,26},{... | collective-permute-start | bytes 614408 | tf_op jit(solution)/shard_map/ppermute | solution.py:21

commit v3 on v2

--- a/solution.py
+++ b/solution.py
@@ -21,22 +21,13 @@
     return lax.ppermute(value, axis, [(source, source + steps) for source in range(initial, last)])
 
 
-def diagonal(value):
-    rows, cols = lax.axis_size("row"), lax.axis_size("col")
-    pairs = [
-        ((row + 1) * cols + col + 1, row * cols + col) for row in range(rows - 1) for col in range(cols - 1)
-    ]
-    return lax.ppermute(value, ("row", "col"), pairs)
-
-
-def row_sum(value):
+def row_terms(value):
     rows = lax.axis_size("row")
     if rows != 4:
-        return lax.psum(value, "row")
-    one, two, three = (
+        return [lax.psum(value, "row")]
+    return [value] + [
         lax.ppermute(value, "row", [(row, row ^ step) for row in range(rows)]) for step in (1, 2, 3)
-    )
-    return (value + one) + (two + three)
+    ]
 
 
 def f32(*shape):
@@ -86,20 +77,26 @@
         yield group * 8, group // per * 8, group % per * extra
 
 
-def pack_kernel(tile_ref, below_ref, corner_ref, right_ref):
+def pack_kernel(tile_ref, near_ref, far_ref, right_ref):
     side = tile_ref.shape[1]
     half = side // 2
-    margin = below_ref.shape[1] // 2
+    margin = far_ref.shape[1]
     extra = margin - half
-    below_ref[:, 0:margin, :] = tile_ref[:, 0:margin, 0:half]
-    below_ref[:, margin : 2 * margin, :] = tile_ref[:, 0:margin, half:]
-    corner_ref[:, 0:margin, :] = tile_ref[:, 0:margin, 0:half]
+    near_ref[:, 0:margin, :] = tile_ref[:, 0:margin, 0:half]
+    far_ref[...] = tile_ref[:, 0:margin, half:]
     right_ref[:, 0:side, :] = tile_ref[:, :, 0:half]
     for row, packed, lane in pack_extra(side, extra, half):
         piece = tile_ref[:, row : row + 8, half:margin]
         right_ref[:, side + packed : side + packed + 8, lane : lane + extra] = piece
         if row < margin:
-            corner_ref[:, margin + packed : margin + packed + 8, lane : lane + extra] = piece
+            near_ref[:, margin + packed : margin + packed + 8, lane : lane + extra] = piece
+
+
+def peak_kernel(probe_ref, meas_ref, out_ref):
+    re, im = probe_ref[0], probe_ref[1]
+    top = jnp.max(re * re + im * im, axis=(0, 1), keepdims=True)
+    out_ref[0] = jnp.broadcast_to(top, out_ref.shape[1:])
+    out_ref[1] = meas_ref[0, 0:8, 0 : out_ref.shape[2]]
 
 
 def turned(load, steps, half, lanes):
@@ -149,14 +146,14 @@
 
 
 def frame_kernel(
-    pos_ref, tile_ref, right_ref, below_ref, corner_ref, prot_ref, meas_ref,
+    pos_ref, tile_ref, right_ref, near_ref, far_ref, corner_ref, prot_ref, meas_ref,
     fwd_right, fwd_left, inv_right, inv_left, lane_ref, row_ref,
-    gt_ref, gr_ref, gz_ref, qs_ref, max_ref,
+    gt_ref, gr_ref, gz_ref, qs_ref,
     right_extra, corner_extra, obj_ref, left_in, right_in, mid, twice,
 ):
     frames, side = meas_ref.shape[0], meas_ref.shape[1]
     half = side // 2
-    margin = below_ref.shape[1] // 2
+    margin = far_ref.shape[1]
     wide = right_ref.shape[1]
     extra = margin - half
     for row, packed, lane in pack_extra(side, extra, half):
@@ -183,7 +180,6 @@
     step = 32
     lanes = lax.broadcasted_iota(jnp.int32, (step, half), 1)
     row_in = lax.broadcasted_iota(jnp.int32, (step, half), 0)
-    largest = jnp.zeros((step, half), jnp.float32)
     for frame in range(frames):
         dy = pos_ref[0, frame]
         dx = pos_ref[1, frame]
@@ -199,15 +195,13 @@
                     right = right_extra[part, rows] if tile else right_ref[part, rows]
                     value = jnp.where(own_col[tile], tile_ref[part, rows, columns], right)
                     if row < margin:
-                        below = below_ref[part, tile * margin + row : tile * margin + row + step]
+                        below = far_ref[part, rows] if tile else near_ref[part, rows]
                         corner = corner_extra[part, rows] if tile else corner_ref[part, rows]
                         value = jnp.where(own_row, value, jnp.where(own_col[tile], below, corner))
                     obj_ref[frame, part, rows, columns] = value
                     obj.append(value)
                 pro_re = prot_ref[frame, 0, rows, columns]
                 pro_im = prot_ref[frame, 1, rows, columns]
-                if frame == 0:
-                    largest = jnp.maximum(largest, pro_re * pro_re + pro_im * pro_im)
                 wave.append((pro_re * obj[0] - pro_im * obj[1], pro_re * obj[1] + pro_im * obj[0]))
             (re0, im0), (re1, im1) = wave
             store_left(2 * frame, rows, 0, re0 + re1)
@@ -217,7 +211,6 @@
             store_left(2 * frame + 1, rows, 1, re * lane_sin + im * lane_cos)
         for which in range(2):
             mid[2 * frame + which] = dot(left_in[2 * frame + which], fwd_right[...])
-    max_ref[0, 0] = jnp.max(largest)
 
     for frame in range(frames):
         for row in range(0, half, step):
@@ -342,12 +335,28 @@
             qs_ref[row // depth, index, place, half:side] = sums[1]
 
 
-def finish_kernel(max_ref, tile_ref, grad_ref, right_ref, down_ref, corner_ref, out_ref):
+def update_kernel(old_ref, *refs):
+    terms, out_ref = refs[:-1], refs[-1]
+
+    def total(index):
+        values = [term[index] for term in terms]
+        while len(values) > 1:
+            values = [values[at] + values[at + 1] for at in range(0, len(values), 2)]
+        return values[0]
+
+    weight = total(2) + 1.0
+    for part in range(2):
+        value = old_ref[part] + total(part) / weight
+        for copy in range(out_ref.shape[0]):
+            out_ref[copy, part] = value
+
+
+def finish_kernel(peak_ref, tile_ref, grad_ref, right_ref, down_ref, corner_ref, out_ref):
     side = tile_ref.shape[1]
     half = side // 2
     margin = down_ref.shape[1] // 2
     extra = margin - half
-    scale = 1.0 / max_ref[0, 0]
+    largest = peak_ref[0]
     step = 8
     for row, packed, lane in pack_extra(side, extra, half):
         place = slice(row, row + step)
@@ -359,9 +368,9 @@
                 one = one + down_ref[part, place] + corner_ref[part, place]
                 two = two + down_ref[part, margin + row : margin + row + step]
                 piece = piece + corner_ref[part, margin + packed : margin + packed + 8, lane : lane + extra]
-            out_ref[part, place, 0:half] = tile_ref[part, place, 0:half] + one * scale
-            out_ref[part, place, half:side] = tile_ref[part, place, half:side] + two * scale
-            out_ref[part, place, half:margin] += piece * scale
+            out_ref[part, place, 0:half] = tile_ref[part, place, 0:half] + one / largest
+            out_ref[part, place, half:side] = tile_ref[part, place, half:side] + two / largest
+            out_ref[part, place, half:margin] += piece / largest[:, 0:extra]
 
 
 def body(object_field, probe_field, measured, positions):
@@ -375,17 +384,27 @@
     wide = side + side * extra // half
     tall = margin + margin * extra // half
 
-    below, corner, right = pl.pallas_call(
+    near, far, right = pl.pallas_call(
         pack_kernel,
-        out_shape=(f32(2, 2 * margin, half), f32(2, tall, half), f32(2, wide, half)),
+        out_shape=(f32(2, tall, half), f32(2, margin, half), f32(2, wide, half)),
         in_specs=[VMEM],
         out_specs=(VMEM,) * 3,
         cost_estimate=cost(10**6, 2 * 10**6),
         compiler_params=PARAMS,
     )(object_field)
-    below = shifted(below, "row", -1)
-    corner = diagonal(corner)
+    near = shifted(near, "row", -1)
+    far = shifted(far, "row", -1)
     right = shifted(right, "col", -1)
+    peak = pl.pallas_call(
+        peak_kernel,
+        out_shape=f32(2, 8, half),
+        in_specs=[VMEM, VMEM],
+        out_specs=VMEM,
+        cost_estimate=cost(10**6, 2 * 10**6),
+        compiler_params=PARAMS,
+    )(probe_field, measured)
+    near, peak = lax.optimization_barrier((near, peak))
+    corner = shifted(near, "col", -1)
     places = positions.T
     prot, ampl = pl.pallas_call(
         prepare_kernel,
@@ -397,17 +416,16 @@
         compiler_params=PARAMS,
     )(places, probe_field, measured)
     depth = side // n_col
-    g_tile, g_right, g_down, sums, largest = pl.pallas_call(
+    g_tile, g_right, g_down, sums = pl.pallas_call(
         frame_kernel,
         out_shape=(
             f32(2, side, side),
             f32(2, wide + tall, half),
             f32(2, 2 * margin, half),
             f32(n_col, 3, depth, side),
-            f32(1, 1),
         ),
-        in_specs=[SMEM] + [VMEM] * 12,
-        out_specs=(VMEM,) * 4 + (SMEM,),
+        in_specs=[SMEM] + [VMEM] * 13,
+        out_specs=(VMEM,) * 4,
         scratch_shapes=[
             pltpu.VMEM((2, side, half), jnp.float32),
             pltpu.VMEM((2, margin, half), jnp.float32),
@@ -420,7 +438,7 @@
         cost_estimate=cost(6 * 10**9, 12 * 10**6),
         compiler_params=PARAMS,
     )(
-        places, object_field, right, below, corner, prot, ampl,
+        places, object_field, right, near, far, corner, prot, ampl,
         fwd_right, fwd_left, inv_right, inv_left, lane_tw, row_tw,
     )
 
@@ -428,21 +446,28 @@
     part = jnp.sum(lax.all_to_all(sums, "col", 0, 0), 0)
     g_right, part, from_above = lax.optimization_barrier((g_right, part, from_above))
     from_left = shifted(g_right, "col", 1)
-    part = row_sum(part)
     old = lax.dynamic_slice_in_dim(probe_field, lax.axis_index("col") * depth, depth, 1)
-    new = old + part[:2] / (part[2] + 1.0)
+    terms = row_terms(part)
+    new = pl.pallas_call(
+        update_kernel,
+        out_shape=f32(n_col, 2, depth, side),
+        in_specs=[VMEM] * (1 + len(terms)),
+        out_specs=VMEM,
+        cost_estimate=cost(10**6, 10**6),
+        compiler_params=PARAMS,
+    )(old, *terms)
     new, from_left = lax.optimization_barrier((new, from_left))
-    new = lax.all_to_all(jnp.broadcast_to(new, (n_col,) + new.shape), "col", 0, 0)
+    new = lax.all_to_all(new, "col", 0, 0)
     from_corner = shifted(from_left[:, wide:], "row", 1)
     new_probe = new.transpose(1, 0, 2, 3).reshape(2, side, side)
     new_object = pl.pallas_call(
         finish_kernel,
         out_shape=f32(2, side, side),
-        in_specs=[SMEM] + [VMEM] * 5,
+        in_specs=[VMEM] * 6,
         out_specs=VMEM,
         cost_estimate=cost(10**6, 4 * 10**6),
         compiler_params=PARAMS,
-    )(largest, object_field, g_tile, from_left, from_above, from_corner)
+    )(peak, object_field, g_tile, from_left, from_above, from_corner)
     return (new_object, new_probe)
 
 

time: 76.4 us -> 73.5 us (0.962)
  starting transfers between devices: 26.3 us -> 29.2 us
  other arithmetic: 2.48 us -> 0.05 us
  waiting for transfers between devices: 26.8 us -> 24.4 us
    ppermute x5 -> x7, starting transfers between devices: 11.9 us -> 17.1 us  [shifted(): lax.ppermute(value, axis, [(source, source + steps) for source in range(i...]
    ppermute x4 -> x3, starting transfers between devices: 5.68 us -> 3.55 us  [row_terms(): lax.ppermute(value, 'row', [(row, row ^ step) for row in range(rows)])]
    add x2 -> x0, other arithmetic: 1.79 us -> none  [the longest x1 0.92 us: row_sum(): return value + one + (two + three)]
    ppermute x4 -> x3, waiting for transfers between devices: 10.2 us -> 8.85 us  [row_terms(): lax.ppermute(value, 'row', [(row, row ^ step) for row in range(rows)])]
    all_to_all x1, waiting for transfers between devices: 9.43 us -> 8.07 us  [body(): part = jnp.sum(lax.all_to_all(sums, 'col', 0, 0), 0)]
    broadcast_in_dim x1 -> x0, local copies, waits for them, and re-layouts: 0.85 us -> none  [body(): jnp.broadcast_to(new, (n_col,) + new.shape)]
    dynamic_slice x0 -> x1, local copies, waits for them, and re-layouts: none -> 0.84 us  [body(): lax.dynamic_slice_in_dim(probe_field, lax.axis_index('col') * depth, dept...]
    transpose x0 -> x1, local copies, waits for them, and re-layouts: none -> 0.84 us  [body(): new_probe = new.transpose(1, 0, 2, 3).reshape(2, side, side)]
  transfers between devices with their start and end apart: 11 -> 12, of which waited for: 7 -> 6; matrix products, arithmetic and copies ran while one was open for 3% -> 1% of each run, Pallas kernels for 6% -> 7%
where the time goes in v3:
time: 73.5 us; the launch traced here: 72.6 us
  starting transfers between devices  29.2 us (40%)
  waiting for transfers between devices  24.4 us (33%)
  Pallas kernels  13 us (18%)
  local copies, waits for them, and re-layouts  5.05 us (7%)
  between operations  0.85 us (1%)
    ppermute x7, starting transfers between devices, shifted(): lax.ppermute(value, axis, [(source, source + steps) for source in range(i...  17.1 us
    ppermute x3, waiting for transfers between devices, row_terms(): lax.ppermute(value, 'row', [(row, row ^ step) for row in range(rows)])  8.85 us
    all_to_all x1, waiting for transfers between devices, body(): part = jnp.sum(lax.all_to_all(sums, 'col', 0, 0), 0)  8.07 us
    pallas_call x1, Pallas kernels, body(): pl.pallas_call(frame_kernel, out_shape=(f32(2, side, side), f32(2, wide +...  8.03 us
    ppermute x7, waiting for transfers between devices, shifted(): lax.ppermute(value, axis, [(source, source + steps) for source in range(i...  7.44 us
    all_to_all x1, starting transfers between devices, body(): part = jnp.sum(lax.all_to_all(sums, 'col', 0, 0), 0)  4.66 us
    all_to_all x1, starting transfers between devices, body(): new = lax.all_to_all(new, 'col', 0, 0)  3.93 us
    ppermute x3, starting transfers between devices, row_terms(): lax.ppermute(value, 'row', [(row, row ^ step) for row in range(rows)])  3.55 us
  transfers between devices with their start and end apart: 12, of which 6 were waited for; matrix products, arithmetic and copies ran while one was open for 1% of the time, Pallas kernels for 7%

profile of v3, /device:TPU:20, one launch (start us, length us, event | category | flops | bytes accessed | tf_op | source)
XLA Modules:
  0.0 72.6 jit_solution(4399144479361880139)
XLA Ops:
  0.6 0.0 copy-start
  0.6 1.0 %copy-done = f32[2,256,256]{2,1,0:T(8,128)S(1)} copy-done((f32[2,256,256]{2,1,0:T(8,128)S(1)}, f32[2,256,256]{2,1,0:T(8,128)}, u32[]{:S(2)}) %copy-start) | copy-done | bytes 524312
  1.7 0.0 copy-start.4
  1.7 0.1 shard_map.113
  1.8 2.4 %collective-permute-start = (f32[2,200,128]{2,1,0:T(8,128)S(1)}, f32[2,200,128]{2,1,0:T(8,128)S(1)}, u32[]{:S(2)}, u32[]{:S(2)}) collective-permute-start(f32[2,200,128]{2,1,0:T(8,128)S(1)} %get-tuple-element.18), channel_id=1, source_target_pairs={{8,0},{16,8},{24,16},{9,1},{17,9},{25,17},{10,2},{18,10},{26,18},{... | collective-permute-start | bytes 614408 | tf_op jit(solution)/shard_map/ppermute | solution.py:21
  4.2 2.5 %collective-permute-start.1 = (f32[2,320,128]{2,1,0:T(8,128)S(1)}, f32[2,320,128]{2,1,0:T(8,128)S(1)}, u32[]{:S(2)}, u32[]{:S(2)}) collective-permute-start(f32[2,320,128]{2,1,0:T(8,128)S(1)} %get-tuple-element.20), channel_id=1, source_target_pairs={{1,0},{2,1},{3,2},{4,3},{5,4},{6,5},{7,6},{9,8},{10,9},{11,10},{12... | collective-permute-start | bytes 983048 | tf_op jit(solution)/shard_map/ppermute | solution.py:21
  6.7 2.4 %collective-permute-start.2 = (f32[2,160,128]{2,1,0:T(8,128)S(1)}, f32[2,160,128]{2,1,0:T(8,128)S(1)}, u32[]{:S(2)}, u32[]{:S(2)}) collective-permute-start(f32[2,160,128]{2,1,0:T(8,128)S(1)} %get-tuple-element.22), channel_id=1, source_target_pairs={{8,0},{16,8},{24,16},{9,1},{17,9},{25,17},{10,2},{18,10},{26,18},{... | collective-permute-start | bytes 491528 | tf_op jit(solution)/shard_map/ppermute | solution.py:21
  9.0 0.0 copy-start.2
  9.0 1.2 %copy-done.2 = f32[4,256,256]{2,1,0:T(8,128)S(1)} copy-done((f32[4,256,256]{2,1,0:T(8,128)S(1)}, f32[4,256,256]{2,1,0:T(8,128)}, u32[]{:S(2)}) %copy-start.2) | copy-done | bytes 1048600
  10.3 0.0 copy-start.3
  10.3 1.0 %copy-done.3 = f32[2,256,256]{2,1,0:T(8,128)S(1)} copy-done((f32[2,256,256]{2,1,0:T(8,128)S(1)}, f32[2,256,256]{2,1,0:T(8,128)}, u32[]{:S(2)}) %copy-start.3) | copy-done | bytes 524312
  11.3 0.2 shard_map.114.peak_ref
  11.5 0.0 collective-permute-done.near_ref
  11.5 2.6 %collective-permute-start.3 = (f32[2,200,128]{2,1,0:T(8,128)S(1)}, f32[2,200,128]{2,1,0:T(8,128)S(1)}, u32[]{:S(2)}, u32[]{:S(2)}) collective-permute-start(f32[2,200,128]{2,1,0:T(8,128)S(1)} %collective-permute-done.near_ref), channel_id=1, source_target_pairs={{1,0},{2,1},{3,2},{4,3},{5,4},{6,5},{7,6},{9,8},{10,9},{11,10},{12... | collective-permute-start | bytes 614408 | tf_op jit(solution)/shard_map/ppermute | solution.py:21
  14.1 0.0 copy-done.4
  14.1 0.0 copy-start.1
  14.1 0.0 copy-start.5
  14.1 0.0 copy-start.6
  14.1 0.0 copy-start.7
  14.1 0.0 copy-start.8
  14.1 0.0 copy-start.9
  14.2 0.0 copy-start.10
  14.2 2.8 %shard_map.115 = (f32[4,2,256,256]{3,2,1,0:T(8,128)S(1)}, f32[4,256,256]{2,1,0:T(8,128)S(1)}) custom-call(s32[2,4]{1,0:T(2,128)S(1)} %bitcast.3, f32[2,256,256]{2,1,0:T(8,128)S(1)} %copy-done.3, f32[4,256,256]{2,1,0:T(8,128)S(1)} %copy-done.2), custom_call_target="tpu_custom_call" | custom-call | flops 3000000000 | bytes 6000000 | tf_op jit(solution)/shard_map/pallas_call | solution.py:409
  17.0 0.0 collective-permute-done.2.far_ref
  17.0 0.0 collective-permute-done.1.right_ref
  17.0 0.3 collective-permute-done.3.corner_ref
  17.3 0.0 copy-done.1
  17.3 0.0 copy-done.5
  17.3 0.0 copy-done.6
  17.3 0.0 copy-done.7
  17.3 0.0 copy-done.8
  17.4 0.0 copy-done.9
  17.4 0.0 copy-done.10
  17.4 8.0 %shard_map.116 = (f32[2,256,256]{2,1,0:T(8,128)S(1)}, f32[2,520,128]{2,1,0:T(8,128)S(1)}, f32[2,320,128]{2,1,0:T(8,128)S(1)}, f32[8,3,32,256]{3,2,1,0:T(8,128)}) custom-call(s32[2,4]{1,0:T(2,128)S(1)} %bitcast.4, f32[2,256,256]{2,1,0:T(8,128)S(1)} %copy-done.1, f32[2,320,128]{2,1,0:T(8,128)S(1)} %collective-permute-done.1.right_ref, ...), custom_call_target="tpu_custom_call" | custom-call | flops 6000000000 | bytes 12000000 | tf_op jit(solution)/shard_map/pallas_call | solution.py:419
  25.4 4.7 %all-to-all-start = ((f32[8,3,32,256]{3,2,1,0:T(8,128)}), f32[8,3,32,256]{3,2,1,0:T(8,128)S(1)}, u32[]{:S(2)}, u32[]{:S(2)}) async-start(f32[8,3,32,256]{3,2,1,0:T(8,128)} %get-tuple-element.27), calls=%async_computation | async-start | bytes 1572864 | tf_op jit(solution)/shard_map/all_to_all | solution.py:446
  30.1 3.5 %collective-permute-start.4 = (f32[2,320,128]{2,1,0:T(8,128)S(1)}, f32[2,320,128]{2,1,0:T(8,128)S(1)}, u32[]{:S(2)}, u32[]{:S(2)}) collective-permute-start(f32[2,320,128]{2,1,0:T(8,128)S(1)} %get-tuple-element.28), channel_id=1, source_target_pairs={{0,8},{8,16},{16,24},{1,9},{9,17},{17,25},{2,10},{10,18},{18,26},{... | collective-permute-start | bytes 983048 | tf_op jit(solution)/shard_map/ppermute | solution.py:21
  33.5 8.1 %all-to-all-done = f32[8,3,32,256]{3,2,1,0:T(8,128)S(1)} async-done(((f32[8,3,32,256]{3,2,1,0:T(8,128)}), f32[8,3,32,256]{3,2,1,0:T(8,128)S(1)}, u32[]{:S(2)}, u32[]{:S(2)}) %all-to-all-start) | async-done | bytes 786464 | tf_op jit(solution)/shard_map/all_to_all | solution.py:446
  41.6 0.1 reduce_sum.9.refs_0_
  41.7 0.0 collective-permute-done.4.down_ref
  41.7 1.9 %collective-permute-start.8 = (f32[2,520,128]{2,1,0:T(8,128)S(1)}, f32[2,520,128]{2,1,0:T(8,128)S(1)}, u32[]{:S(2)}, u32[]{:S(2)}) collective-permute-start(f32[2,520,128]{2,1,0:T(8,128)S(1)} %get-tuple-element.30), channel_id=1, source_target_pairs={{0,1},{1,2},{2,3},{3,4},{4,5},{5,6},{6,7},{8,9},{9,10},{10,11},{11... | collective-permute-start | bytes 1597448 | tf_op jit(solution)/shard_map/ppermute | solution.py:21
  43.6 1.6 %collective-permute-start.5 = (f32[3,32,256]{2,1,0:T(8,128)S(1)}, f32[3,32,256]{2,1,0:T(8,128)S(1)}, u32[]{:S(2)}, u32[]{:S(2)}) collective-permute-start(f32[3,32,256]{2,1,0:T(8,128)S(1)} %reduce_sum.9.refs_0_), channel_id=1, source_target_pairs={{0,8},{8,0},{16,24},{24,16},{1,9},{9,1},{17,25},{25,17},{2,10},{10... | collective-permute-start | bytes 294920 | tf_op jit(solution)/shard_map/ppermute | solution.py:29
  45.3 0.2 collective-permute-start.6
  45.5 1.7 %collective-permute-start.7 = (f32[3,32,256]{2,1,0:T(8,128)S(1)}, f32[3,32,256]{2,1,0:T(8,128)S(1)}, u32[]{:S(2)}, u32[]{:S(2)}) collective-permute-start(f32[3,32,256]{2,1,0:T(8,128)S(1)} %reduce_sum.9.refs_0_), channel_id=1, source_target_pairs={{0,24},{8,16},{16,8},{24,0},{1,25},{9,17},{17,9},{25,1},{2,26},{10... | collective-permute-start | bytes 294920 | tf_op jit(solution)/shard_map/ppermute | solution.py:29
  47.2 0.8 %constant_dynamic-slice_fusion.old_ref = f32[2,32,256]{2,1,0:T(8,128)S(1)} fusion(f32[2,256,256]{2,1,0:T(8,128)} %probe_ref.3, s32[]{:T(128)S(6)} %select_n.3), kind=kLoop, calls=%fused_computation | loop fusion | bytes 131076 | tf_op jit(solution)/shard_map/dynamic_slice | solution.py:449
  48.0 0.8 %collective-permute-done.5.refs_1_ = f32[3,32,256]{2,1,0:T(8,128)S(1)} collective-permute-done((f32[3,32,256]{2,1,0:T(8,128)S(1)}, f32[3,32,256]{2,1,0:T(8,128)S(1)}, u32[]{:S(2)}, u32[]{:S(2)}) %collective-permute-start.5) | collective-permute-done | bytes 98336 | tf_op jit(solution)/shard_map/ppermute | solution.py:29
  48.8 2.8 %collective-permute-done.6.refs_2_ = f32[3,32,256]{2,1,0:T(8,128)S(1)} collective-permute-done((f32[3,32,256]{2,1,0:T(8,128)S(1)}, f32[3,32,256]{2,1,0:T(8,128)S(1)}, u32[]{:S(2)}, u32[]{:S(2)}) %collective-permute-start.6) | collective-permute-done | bytes 98336 | tf_op jit(solution)/shard_map/ppermute | solution.py:29
  51.6 5.2 %collective-permute-done.7.refs_3_ = f32[3,32,256]{2,1,0:T(8,128)S(1)} collective-permute-done((f32[3,32,256]{2,1,0:T(8,128)S(1)}, f32[3,32,256]{2,1,0:T(8,128)S(1)}, u32[]{:S(2)}, u32[]{:S(2)}) %collective-permute-start.7) | collective-permute-done | bytes 98336 | tf_op jit(solution)/shard_map/ppermute | solution.py:29
  56.9 0.9 %shard_map.117 = f32[8,2,32,256]{3,2,1,0:T(8,128)} custom-call(f32[2,32,256]{2,1,0:T(8,128)S(1)} %constant_dynamic-slice_fusion.old_ref, f32[3,32,256]{2,1,0:T(8,128)S(1)} %reduce_sum.9.refs_0_, f32[3,32,256]{2,1,0:T(8,128)S(1)} %collective-permute-done.5.refs_1_, f32[3,32,256]{2,1,0:T(8,128)S(1)} %collective-permute-done.6.refs_2_, ...), custom_call_target="tpu_custom_call" | custom-call | flops 1000000 | bytes 1000000 | tf_op jit(solution)/shard_map/pallas_call | solution.py:451
  57.7 0.0 collective-permute-done.8.right_ref
  57.7 3.9 %all-to-all-start.1 = ((f32[8,2,32,256]{3,2,1,0:T(8,128)}), f32[8,2,32,256]{3,2,1,0:T(8,128)S(1)}, u32[]{:S(2)}, u32[]{:S(2)}) async-start(f32[8,2,32,256]{3,2,1,0:T(8,128)} %shard_map.117), calls=%async_computation.1 | async-start | bytes 1048576 | tf_op jit(solution)/shard_map/all_to_all | solution.py:460
  61.7 1.9 %collective-permute-start.9 = (f32[2,200,128]{2,1,0:T(8,128)S(1)}, f32[2,200,128]{2,1,0:T(8,128)S(1)}, u32[]{:S(2)}, u32[]{:S(2)}) collective-permute-start(f32[2,200,128]{2,1,0:T(8,128)S(1)} %slice.3), channel_id=1, source_target_pairs={{0,8},{8,16},{16,24},{1,9},{9,17},{17,25},{2,10},{10,18},{18,26},{... | collective-permute-start | bytes 614408 | tf_op jit(solution)/shard_map/ppermute | solution.py:21
  63.6 7.1 %collective-permute-done.9.corner_ref = f32[2,200,128]{2,1,0:T(8,128)S(1)} collective-permute-done((f32[2,200,128]{2,1,0:T(8,128)S(1)}, f32[2,200,128]{2,1,0:T(8,128)S(1)}, u32[]{:S(2)}, u32[]{:S(2)}) %collective-permute-start.9) | collective-permute-done | bytes 204832 | tf_op jit(solution)/shard_map/ppermute | solution.py:21
  70.7 1.0 %shard_map.118 = f32[2,256,256]{2,1,0:T(8,128)} custom-call(f32[2,8,128]{2,1,0:T(8,128)S(1)} %shard_map.114.peak_ref, f32[2,256,256]{2,1,0:T(8,128)S(1)} %copy-done.1, f32[2,256,256]{2,1,0:T(8,128)S(1)} %get-tuple-element.25.grad_ref, f32[2,520,128]{2,1,0:T(8,128)S(1)} %collective-permute-done.8.right_ref, ...), custom_call_target="tpu_custom_call" | custom-call | flops 1000000 | bytes 4000000 | tf_op jit(solution)/shard_map/pallas_call | solution.py:463
  71.7 0.0 all-to-all-done.1
  71.7 0.8 %copy.12 = f32[2,8,32,256]{3,2,1,0:T(8,128)} copy(f32[2,8,32,256]{3,2,0,1:T(8,128)S(1)} %bitcast.5) | data formatting | bytes 1048576 | tf_op jit(solution)/shard_map/transpose | solution.py:462
  (1 shorter events, 0.0 us)
Async XLA Ops:
  0.6 1.0 %copy-start = (f32[2,256,256]{2,1,0:T(8,128)S(1)}, f32[2,256,256]{2,1,0:T(8,128)}, u32[]{:S(2)}) copy-start(f32[2,256,256]{2,1,0:T(8,128)} %tile_ref.5) | copy-start | bytes 1572868
  1.7 12.4 %copy-start.4 = (s32[4,2]{0,1:T(2,128)S(1)}, s32[4,2]{0,1:T(2,128)}, u32[]{:S(2)}) copy-start(s32[4,2]{0,1:T(2,128)} %param.13) | copy-start | bytes 100
  1.8 9.7 %collective-permute-start = (f32[2,200,128]{2,1,0:T(8,128)S(1)}, f32[2,200,128]{2,1,0:T(8,128)S(1)}, u32[]{:S(2)}, u32[]{:S(2)}) collective-permute-start(f32[2,200,128]{2,1,0:T(8,128)S(1)} %get-tuple-element.18), channel_id=1, source_target_pairs={{8,0},{16,8},{24,16},{9,1},{17,9},{25,17},{10,2},{18,10},{26,18},{... | collective-permute-start | bytes 614408 | tf_op jit(solution)/shard_map/ppermute | solution.py:21
  4.2 12.9 %collective-permute-start.1 = (f32[2,320,128]{2,1,0:T(8,128)S(1)}, f32[2,320,128]{2,1,0:T(8,128)S(1)}, u32[]{:S(2)}, u32[]{:S(2)}) collective-permute-start(f32[2,320,128]{2,1,0:T(8,128)S(1)} %get-tuple-element.20), channel_id=1, source_target_pairs={{1,0},{2,1},{3,2},{4,3},{5,4},{6,5},{7,6},{9,8},{10,9},{11,10},{12... | collective-permute-start | bytes 983048 | tf_op jit(solution)/shard_map/ppermute | solution.py:21
  6.7 10.3 %collective-permute-start.2 = (f32[2,160,128]{2,1,0:T(8,128)S(1)}, f32[2,160,128]{2,1,0:T(8,128)S(1)}, u32[]{:S(2)}, u32[]{:S(2)}) collective-permute-start(f32[2,160,128]{2,1,0:T(8,128)S(1)} %get-tuple-element.22), channel_id=1, source_target_pairs={{8,0},{16,8},{24,16},{9,1},{17,9},{25,17},{10,2},{18,10},{26,18},{... | collective-permute-start | bytes 491528 | tf_op jit(solution)/shard_map/ppermute | solution.py:21
  9.0 1.2 %copy-start.2 = (f32[4,256,256]{2,1,0:T(8,128)S(1)}, f32[4,256,256]{2,1,0:T(8,128)}, u32[]{:S(2)}) copy-start(f32[4,256,256]{2,1,0:T(8,128)} %meas_ref.3) | copy-start | bytes 3145732
  10.3 1.0 %copy-start.3 = (f32[2,256,256]{2,1,0:T(8,128)S(1)}, f32[2,256,256]{2,1,0:T(8,128)}, u32[]{:S(2)}) copy-start(f32[2,256,256]{2,1,0:T(8,128)} %probe_ref.3) | copy-start | bytes 1572868
  11.5 5.8 %collective-permute-start.3 = (f32[2,200,128]{2,1,0:T(8,128)S(1)}, f32[2,200,128]{2,1,0:T(8,128)S(1)}, u32[]{:S(2)}, u32[]{:S(2)}) collective-permute-start(f32[2,200,128]{2,1,0:T(8,128)S(1)} %collective-permute-done.near_ref), channel_id=1, source_target_pairs={{1,0},{2,1},{3,2},{4,3},{5,4},{6,5},{7,6},{9,8},{10,9},{11,10},{12... | collective-permute-start | bytes 614408 | tf_op jit(solution)/shard_map/ppermute | solution.py:21
  14.1 3.2 %copy-start.1 = (f32[2,256,256]{2,1,0:T(8,128)S(1)}, f32[2,256,256]{2,1,0:T(8,128)}, u32[]{:S(2)}) copy-start(f32[2,256,256]{2,1,0:T(8,128)} %tile_ref.5) | copy-start | bytes 1572868
  14.1 3.2 %copy-start.5 = (bf16[768,256]{1,0:T(8,128)(2,1)S(1)}, bf16[768,256]{1,0:T(8,128)(2,1)}, u32[]{:S(2)}) copy-start(bf16[768,256]{1,0:T(8,128)(2,1)} %constant.24.clone.fwd_right) | copy-start | bytes 1179652
  14.1 3.2 %copy-start.6 = (bf16[256,768]{1,0:T(8,128)(2,1)S(1)}, bf16[256,768]{1,0:T(8,128)(2,1)}, u32[]{:S(2)}) copy-start(bf16[256,768]{1,0:T(8,128)(2,1)} %constant.25.clone.fwd_left) | copy-start | bytes 1179652
  14.1 3.2 %copy-start.7 = (bf16[768,256]{1,0:T(8,128)(2,1)S(1)}, bf16[768,256]{1,0:T(8,128)(2,1)}, u32[]{:S(2)}) copy-start(bf16[768,256]{1,0:T(8,128)(2,1)} %constant.26.clone.inv_right) | copy-start | bytes 1179652
  14.1 3.2 %copy-start.8 = (bf16[256,768]{1,0:T(8,128)(2,1)S(1)}, bf16[256,768]{1,0:T(8,128)(2,1)}, u32[]{:S(2)}) copy-start(bf16[256,768]{1,0:T(8,128)(2,1)} %constant.27.clone.inv_left) | copy-start | bytes 1179652
  14.1 3.2 %copy-start.9 = (f32[2,128,128]{2,1,0:T(8,128)S(1)}, f32[2,128,128]{2,1,0:T(8,128)}, u32[]{:S(2)}) copy-start(f32[2,128,128]{2,1,0:T(8,128)} %constant.29.clone.row_ref) | copy-start | bytes 393220
  14.2 3.2 %copy-start.10 = (f32[2,8,128]{2,1,0:T(8,128)S(1)}, f32[2,8,128]{2,1,0:T(8,128)}, u32[]{:S(2)}) copy-start(f32[2,8,128]{2,1,0:T(8,128)} %constant.28.clone.lane_ref) | copy-start | bytes 24580
  25.4 16.2 %all-to-all-start = ((f32[8,3,32,256]{3,2,1,0:T(8,128)}), f32[8,3,32,256]{3,2,1,0:T(8,128)S(1)}, u32[]{:S(2)}, u32[]{:S(2)}) async-start(f32[8,3,32,256]{3,2,1,0:T(8,128)} %get-tuple-element.27), calls=%async_computation | async-start | bytes 1572864 | tf_op jit(solution)/shard_map/all_to_all | solution.py:446
  30.1 11.6 %collective-permute-start.4 = (f32[2,320,128]{2,1,0:T(8,128)S(1)}, f32[2,320,128]{2,1,0:T(8,128)S(1)}, u32[]{:S(2)}, u32[]{:S(2)}) collective-permute-start(f32[2,320,128]{2,1,0:T(8,128)S(1)} %get-tuple-element.28), channel_id=1, source_target_pairs={{0,8},{8,16},{16,24},{1,9},{9,17},{17,25},{2,10},{10,18},{18,26},{... | collective-permute-start | bytes 983048 | tf_op jit(solution)/shard_map/ppermute | solution.py:21
  41.7 16.0 %collective-permute-start.8 = (f32[2,520,128]{2,1,0:T(8,128)S(1)}, f32[2,520,128]{2,1,0:T(8,128)S(1)}, u32[]{:S(2)}, u32[]{:S(2)}) collective-permute-start(f32[2,520,128]{2,1,0:T(8,128)S(1)} %get-tuple-element.30), channel_id=1, source_target_pairs={{0,1},{1,2},{2,3},{3,4},{4,5},{5,6},{6,7},{8,9},{9,10},{10,11},{11... | collective-permute-start | bytes 1597448 | tf_op jit(solution)/shard_map/ppermute | solution.py:21
  43.6 5.2 %collective-permute-start.5 = (f32[3,32,256]{2,1,0:T(8,128)S(1)}, f32[3,32,256]{2,1,0:T(8,128)S(1)}, u32[]{:S(2)}, u32[]{:S(2)}) collective-permute-start(f32[3,32,256]{2,1,0:T(8,128)S(1)} %reduce_sum.9.refs_0_), channel_id=1, source_target_pairs={{0,8},{8,0},{16,24},{24,16},{1,9},{9,1},{17,25},{25,17},{2,10},{10... | collective-permute-start | bytes 294920 | tf_op jit(solution)/shard_map/ppermute | solution.py:29
  45.3 6.4 %collective-permute-start.6 = (f32[3,32,256]{2,1,0:T(8,128)S(1)}, f32[3,32,256]{2,1,0:T(8,128)S(1)}, u32[]{:S(2)}, u32[]{:S(2)}) collective-permute-start(f32[3,32,256]{2,1,0:T(8,128)S(1)} %reduce_sum.9.refs_0_), channel_id=1, source_target_pairs={{0,16},{8,24},{16,0},{24,8},{1,17},{9,25},{17,1},{25,9},{2,18},{10... | collective-permute-start | bytes 294920 | tf_op jit(solution)/shard_map/ppermute | solution.py:29
  45.5 11.4 %collective-permute-start.7 = (f32[3,32,256]{2,1,0:T(8,128)S(1)}, f32[3,32,256]{2,1,0:T(8,128)S(1)}, u32[]{:S(2)}, u32[]{:S(2)}) collective-permute-start(f32[3,32,256]{2,1,0:T(8,128)S(1)} %reduce_sum.9.refs_0_), channel_id=1, source_target_pairs={{0,24},{8,16},{16,8},{24,0},{1,25},{9,17},{17,9},{25,1},{2,26},{10... | collective-permute-start | bytes 294920 | tf_op jit(solution)/shard_map/ppermute | solution.py:29
  57.7 14.0 %all-to-all-start.1 = ((f32[8,2,32,256]{3,2,1,0:T(8,128)}), f32[8,2,32,256]{3,2,1,0:T(8,128)S(1)}, u32[]{:S(2)}, u32[]{:S(2)}) async-start(f32[8,2,32,256]{3,2,1,0:T(8,128)} %shard_map.117), calls=%async_computation.1 | async-start | bytes 1048576 | tf_op jit(solution)/shard_map/all_to_all | solution.py:460
  61.7 9.0 %collective-permute-start.9 = (f32[2,200,128]{2,1,0:T(8,128)S(1)}, f32[2,200,128]{2,1,0:T(8,128)S(1)}, u32[]{:S(2)}, u32[]{:S(2)}) collective-permute-start(f32[2,200,128]{2,1,0:T(8,128)S(1)} %slice.3), channel_id=1, source_target_pairs={{0,8},{8,16},{16,24},{1,9},{9,17},{17,25},{2,10},{10,18},{18,26},{... | collective-permute-start | bytes 614408 | tf_op jit(solution)/shard_map/ppermute | solution.py:21

commit v4 on v3

--- a/solution.py
+++ b/solution.py
@@ -21,13 +21,22 @@
     return lax.ppermute(value, axis, [(source, source + steps) for source in range(initial, last)])
 
 
+def diagonal(value):
+    rows, cols = lax.axis_size("row"), lax.axis_size("col")
+    pairs = [
+        (row * cols + col, (row + 1) * cols + col + 1) for row in range(rows - 1) for col in range(cols - 1)
+    ]
+    return lax.ppermute(value, ("row", "col"), pairs)
+
+
 def row_terms(value):
     rows = lax.axis_size("row")
     if rows != 4:
         return [lax.psum(value, "row")]
-    return [value] + [
-        lax.ppermute(value, "row", [(row, row ^ step) for row in range(rows)]) for step in (1, 2, 3)
-    ]
+    three, two, one = (
+        lax.ppermute(value, "row", [(row, row ^ step) for row in range(rows)]) for step in (3, 2, 1)
+    )
+    return [two, three, value, one]
 
 
 def f32(*shape):
@@ -148,13 +157,12 @@
 def frame_kernel(
     pos_ref, tile_ref, right_ref, near_ref, far_ref, corner_ref, prot_ref, meas_ref,
     fwd_right, fwd_left, inv_right, inv_left, lane_ref, row_ref,
-    gt_ref, gr_ref, gz_ref, qs_ref,
+    gt_ref, gr_ref, gz_ref, gc_ref, qs_ref,
     right_extra, corner_extra, obj_ref, left_in, right_in, mid, twice,
 ):
     frames, side = meas_ref.shape[0], meas_ref.shape[1]
     half = side // 2
     margin = far_ref.shape[1]
-    wide = right_ref.shape[1]
     extra = margin - half
     for row, packed, lane in pack_extra(side, extra, half):
         right_extra[:, row : row + 8, 0:extra] = right_ref[:, side + packed : side + packed + 8, lane : lane + extra]
@@ -266,7 +274,18 @@
         for frame in range(frames):
             dy = pos_ref[0, frame]
             dx = pos_ref[1, frame]
-            own_row = row_in + row >= dy
+            masks = []
+            for tile in range(2):
+                own_col = lanes + tile * half >= dx
+                far_col = jnp.logical_not(own_col)
+                if row < margin:
+                    own_row = row_in + row >= dy
+                    far_row = jnp.logical_not(own_row)
+                    masks.append(
+                        {"t": own_row & own_col, "r": own_row & far_col, "b": far_row & own_col, "c": far_row & far_col}
+                    )
+                else:
+                    masks.append({"t": own_col, "r": far_col})
             even_re, even_im = mid[2 * frame, rows, 0:half], mid[2 * frame, rows, half:side]
             odd_re, odd_im = mid[2 * frame + 1, rows, 0:half], mid[2 * frame + 1, rows, half:side]
             re = odd_re * lane_cos + odd_im * lane_sin
@@ -275,7 +294,6 @@
                 columns = slice(tile * half, (tile + 1) * half)
                 chi_re = even_re - re if tile else even_re + re
                 chi_im = even_im - im if tile else even_im + im
-                own_col = lanes + tile * half >= dx
                 pro_re = prot_ref[frame, 0, rows, columns]
                 pro_im = prot_ref[frame, 1, rows, columns]
                 obj_re = obj_ref[frame, 0, rows, columns]
@@ -283,16 +301,8 @@
                 for part, value in enumerate(
                     (pro_re * chi_re + pro_im * chi_im, pro_re * chi_im - pro_im * chi_re)
                 ):
-                    own = value
-                    pieces = []
-                    if row < margin:
-                        own = jnp.where(own_row, value, 0.0)
-                        other = jnp.where(own_row, 0.0, value)
-                        pieces.append(("b", jnp.where(own_col, other, 0.0)))
-                        pieces.append(("c", jnp.where(own_col, 0.0, other)))
-                    pieces.append(("t", jnp.where(own_col, own, 0.0)))
-                    pieces.append(("r", jnp.where(own_col, 0.0, own)))
-                    for name, piece in pieces:
+                    for name, mask in masks[tile].items():
+                        piece = jnp.where(mask, value, 0.0)
                         key = (name, part, tile)
                         total[key] = piece if frame == 0 else total[key] + piece
                 for index, value in enumerate(
@@ -303,7 +313,8 @@
                     )
                 ):
                     twice[frame, index, tile, row : row + step] = value
-                    twice[frame, index, tile, side + row : side + row + step] = value
+                    if row < margin:
+                        twice[frame, index, tile, side + row : side + row + step] = value
         packed, lane = places[row]
         for part in range(2):
             gt_ref[part, rows, 0:half] = total["t", part, 0]
@@ -313,9 +324,9 @@
             if row < margin:
                 gz_ref[part, rows] = total["b", part, 0]
                 gz_ref[part, margin + row : margin + row + step] = total["b", part, 1]
-                gr_ref[part, wide + row : wide + row + step] = total["c", part, 0]
-                base = wide + margin + packed
-                gr_ref[part, base : base + 8, lane : lane + extra] = total["c", part, 1][:, 0:extra]
+                gc_ref[part, rows] = total["c", part, 0]
+                base = margin + packed
+                gc_ref[part, base : base + 8, lane : lane + extra] = total["c", part, 1][:, 0:extra]
 
     depth = qs_ref.shape[2]
     step = min(32, depth)
@@ -416,16 +427,17 @@
         compiler_params=PARAMS,
     )(places, probe_field, measured)
     depth = side // n_col
-    g_tile, g_right, g_down, sums = pl.pallas_call(
+    g_tile, g_right, g_down, g_corner, sums = pl.pallas_call(
         frame_kernel,
         out_shape=(
             f32(2, side, side),
-            f32(2, wide + tall, half),
+            f32(2, wide, half),
             f32(2, 2 * margin, half),
+            f32(2, tall, half),
             f32(n_col, 3, depth, side),
         ),
         in_specs=[SMEM] + [VMEM] * 13,
-        out_specs=(VMEM,) * 4,
+        out_specs=(VMEM,) * 5,
         scratch_shapes=[
             pltpu.VMEM((2, side, half), jnp.float32),
             pltpu.VMEM((2, margin, half), jnp.float32),
@@ -433,7 +445,7 @@
             pltpu.VMEM((2 * frames, side, 3 * side), BF16),
             pltpu.VMEM((2 * frames, 3 * side, side), BF16),
             pltpu.VMEM((2 * frames, side, side), jnp.float32),
-            pltpu.VMEM((frames, 3, 2, 2 * side, half), jnp.float32),
+            pltpu.VMEM((frames, 3, 2, side + margin, half), jnp.float32),
         ],
         cost_estimate=cost(6 * 10**9, 12 * 10**6),
         compiler_params=PARAMS,
@@ -444,10 +456,13 @@
 
     from_above = shifted(g_down, "row", 1)
     part = jnp.sum(lax.all_to_all(sums, "col", 0, 0), 0)
-    g_right, part, from_above = lax.optimization_barrier((g_right, part, from_above))
-    from_left = shifted(g_right, "col", 1)
+    part, from_above = lax.optimization_barrier((part, from_above))
     old = lax.dynamic_slice_in_dim(probe_field, lax.axis_index("col") * depth, depth, 1)
     terms = row_terms(part)
+    g_right, terms[-1] = lax.optimization_barrier((g_right, terms[-1]))
+    from_left = shifted(g_right, "col", 1)
+    g_corner, terms[0] = lax.optimization_barrier((g_corner, terms[0]))
+    from_corner = diagonal(g_corner)
     new = pl.pallas_call(
         update_kernel,
         out_shape=f32(n_col, 2, depth, side),
@@ -456,9 +471,7 @@
         cost_estimate=cost(10**6, 10**6),
         compiler_params=PARAMS,
     )(old, *terms)
-    new, from_left = lax.optimization_barrier((new, from_left))
     new = lax.all_to_all(new, "col", 0, 0)
-    from_corner = shifted(from_left[:, wide:], "row", 1)
     new_probe = new.transpose(1, 0, 2, 3).reshape(2, side, side)
     new_object = pl.pallas_call(
         finish_kernel,

time: 73.5 us -> 74.8 us (1.018)
  starting transfers between devices: 29.2 us -> 31.1 us
    ppermute x0 -> x1, waiting for transfers between devices: none -> 7.04 us  [diagonal(): return lax.ppermute(value, ('row', 'col'), pairs)]
    ppermute x7 -> x6, waiting for transfers between devices: 7.44 us -> 1.87 us  [shifted(): lax.ppermute(value, axis, [(source, source + steps) for source in range(i...]
    ppermute x0 -> x1, starting transfers between devices: none -> 3.36 us  [diagonal(): return lax.ppermute(value, ('row', 'col'), pairs)]
    ppermute x7 -> x6, starting transfers between devices: 17.1 us -> 15.3 us  [shifted(): lax.ppermute(value, axis, [(source, source + steps) for source in range(i...]
    ppermute x3, waiting for transfers between devices: 8.85 us -> 7.15 us  [row_terms(): lax.ppermute(value, 'row', [(row, row ^ step) for row in range(rows)])]
  transfers between devices with their start and end apart: 12 -> 12, of which waited for: 6 -> 7; matrix products, arithmetic and copies ran while one was open for 1% -> 1% of each run, Pallas kernels for 7% -> 5%
where the time goes in v4:
time: 74.8 us; the launch traced here: 74.2 us
  starting transfers between devices  31.1 us (42%)
  waiting for transfers between devices  24.1 us (32%)
  Pallas kernels  13 us (17%)
  local copies, waits for them, and re-layouts  5.04 us (7%)
  between operations  0.85 us (1%)
    ppermute x6, starting transfers between devices, shifted(): lax.ppermute(value, axis, [(source, source + steps) for source in range(i...  15.3 us
    all_to_all x1, waiting for transfers between devices, body(): part = jnp.sum(lax.all_to_all(sums, 'col', 0, 0), 0)  8.05 us
    pallas_call x1, Pallas kernels, body(): pl.pallas_call(frame_kernel, out_shape=(f32(2, side, side), f32(2, wide,...  8.05 us
    ppermute x3, waiting for transfers between devices, row_terms(): lax.ppermute(value, 'row', [(row, row ^ step) for row in range(rows)])  7.15 us
    ppermute x1, waiting for transfers between devices, diagonal(): return lax.ppermute(value, ('row', 'col'), pairs)  7.04 us
    all_to_all x1, starting transfers between devices, body(): part = jnp.sum(lax.all_to_all(sums, 'col', 0, 0), 0)  4.63 us
    all_to_all x1, starting transfers between devices, body(): new = lax.all_to_all(new, 'col', 0, 0)  4.29 us
    ppermute x3, starting transfers between devices, row_terms(): lax.ppermute(value, 'row', [(row, row ^ step) for row in range(rows)])  3.53 us
  transfers between devices with their start and end apart: 12, of which 7 were waited for; matrix products, arithmetic and copies ran while one was open for 1% of the time, Pallas kernels for 5%

profile of v4, /device:TPU:20, one launch (start us, length us, event | category | flops | bytes accessed | tf_op | source)
XLA Modules:
  0.0 74.2 jit_solution(11372718532379611707)
XLA Ops:
  0.6 0.0 copy-start
  0.6 1.0 %copy-done = f32[2,256,256]{2,1,0:T(8,128)S(1)} copy-done((f32[2,256,256]{2,1,0:T(8,128)S(1)}, f32[2,256,256]{2,1,0:T(8,128)}, u32[]{:S(2)}) %copy-start) | copy-done | bytes 524312
  1.7 0.0 copy-start.4
  1.7 0.1 shard_map.113
  1.8 2.4 %collective-permute-start = (f32[2,200,128]{2,1,0:T(8,128)S(1)}, f32[2,200,128]{2,1,0:T(8,128)S(1)}, u32[]{:S(2)}, u32[]{:S(2)}) collective-permute-start(f32[2,200,128]{2,1,0:T(8,128)S(1)} %get-tuple-element.20), channel_id=1, source_target_pairs={{8,0},{16,8},{24,16},{9,1},{17,9},{25,17},{10,2},{18,10},{26,18},{... | collective-permute-start | bytes 614408 | tf_op jit(solution)/shard_map/ppermute | solution.py:21
  4.2 2.5 %collective-permute-start.1 = (f32[2,320,128]{2,1,0:T(8,128)S(1)}, f32[2,320,128]{2,1,0:T(8,128)S(1)}, u32[]{:S(2)}, u32[]{:S(2)}) collective-permute-start(f32[2,320,128]{2,1,0:T(8,128)S(1)} %get-tuple-element.22), channel_id=1, source_target_pairs={{1,0},{2,1},{3,2},{4,3},{5,4},{6,5},{7,6},{9,8},{10,9},{11,10},{12... | collective-permute-start | bytes 983048 | tf_op jit(solution)/shard_map/ppermute | solution.py:21
  6.7 2.4 %collective-permute-start.2 = (f32[2,160,128]{2,1,0:T(8,128)S(1)}, f32[2,160,128]{2,1,0:T(8,128)S(1)}, u32[]{:S(2)}, u32[]{:S(2)}) collective-permute-start(f32[2,160,128]{2,1,0:T(8,128)S(1)} %get-tuple-element.24), channel_id=1, source_target_pairs={{8,0},{16,8},{24,16},{9,1},{17,9},{25,17},{10,2},{18,10},{26,18},{... | collective-permute-start | bytes 491528 | tf_op jit(solution)/shard_map/ppermute | solution.py:21
  9.0 0.0 copy-start.2
  9.0 1.2 %copy-done.2 = f32[4,256,256]{2,1,0:T(8,128)S(1)} copy-done((f32[4,256,256]{2,1,0:T(8,128)S(1)}, f32[4,256,256]{2,1,0:T(8,128)}, u32[]{:S(2)}) %copy-start.2) | copy-done | bytes 1048600
  10.3 0.0 copy-start.3
  10.3 1.0 %copy-done.3 = f32[2,256,256]{2,1,0:T(8,128)S(1)} copy-done((f32[2,256,256]{2,1,0:T(8,128)S(1)}, f32[2,256,256]{2,1,0:T(8,128)}, u32[]{:S(2)}) %copy-start.3) | copy-done | bytes 524312
  11.3 0.2 shard_map.114.peak_ref
  11.5 0.0 collective-permute-done.near_ref
  11.5 2.6 %collective-permute-start.3 = (f32[2,200,128]{2,1,0:T(8,128)S(1)}, f32[2,200,128]{2,1,0:T(8,128)S(1)}, u32[]{:S(2)}, u32[]{:S(2)}) collective-permute-start(f32[2,200,128]{2,1,0:T(8,128)S(1)} %collective-permute-done.near_ref), channel_id=1, source_target_pairs={{1,0},{2,1},{3,2},{4,3},{5,4},{6,5},{7,6},{9,8},{10,9},{11,10},{12... | collective-permute-start | bytes 614408 | tf_op jit(solution)/shard_map/ppermute | solution.py:21
  14.1 0.0 copy-done.4
  14.1 0.0 copy-start.1
  14.1 0.0 copy-start.5
  14.1 0.0 copy-start.6
  14.1 0.0 copy-start.7
  14.1 0.0 copy-start.8
  14.1 0.0 copy-start.9
  14.2 0.0 copy-start.10
  14.2 2.8 %shard_map.115 = (f32[4,2,256,256]{3,2,1,0:T(8,128)S(1)}, f32[4,256,256]{2,1,0:T(8,128)S(1)}) custom-call(s32[2,4]{1,0:T(2,128)S(1)} %bitcast.3, f32[2,256,256]{2,1,0:T(8,128)S(1)} %copy-done.3, f32[4,256,256]{2,1,0:T(8,128)S(1)} %copy-done.2), custom_call_target="tpu_custom_call" | custom-call | flops 3000000000 | bytes 6000000 | tf_op jit(solution)/shard_map/pallas_call | solution.py:420
  17.0 0.0 collective-permute-done.2.far_ref
  17.0 0.0 collective-permute-done.1.right_ref
  17.0 0.3 collective-permute-done.3.corner_ref
  17.3 0.0 copy-done.1
  17.3 0.0 copy-done.5
  17.3 0.0 copy-done.6
  17.3 0.0 copy-done.7
  17.3 0.0 copy-done.8
  17.4 0.0 copy-done.9
  17.4 0.0 copy-done.10
  17.4 8.1 %shard_map.116 = (f32[2,256,256]{2,1,0:T(8,128)S(1)}, f32[2,320,128]{2,1,0:T(8,128)S(1)}, f32[2,320,128]{2,1,0:T(8,128)S(1)}, f32[2,200,128]{2,1,0:T(8,128)S(1)}, f32[8,3,32,256]{3,2,1,0:T(8,128)}) custom-call(s32[2,4]{1,0:T(2,128)S(1)} %bitcast.4, f32[2,256,256]{2,1,0:T(8,128)S(1)} %copy-done.1, f32[2,320,128]{2,1,0:T(8,128)S(1)} %collective-permute-done.1.right_ref, ...), custom_call_target="tpu_custom_call" | custom-call | flops 6000000000 | bytes 12000000 | tf_op jit(solution)/shard_map/pallas_call | solution.py:430
  25.4 4.6 %all-to-all-start = ((f32[8,3,32,256]{3,2,1,0:T(8,128)}), f32[8,3,32,256]{3,2,1,0:T(8,128)S(1)}, u32[]{:S(2)}, u32[]{:S(2)}) async-start(f32[8,3,32,256]{3,2,1,0:T(8,128)} %get-tuple-element.29), calls=%async_computation | async-start | bytes 1572864 | tf_op jit(solution)/shard_map/all_to_all | solution.py:458
  30.1 3.5 %collective-permute-start.4 = (f32[2,320,128]{2,1,0:T(8,128)S(1)}, f32[2,320,128]{2,1,0:T(8,128)S(1)}, u32[]{:S(2)}, u32[]{:S(2)}) collective-permute-start(f32[2,320,128]{2,1,0:T(8,128)S(1)} %get-tuple-element.30), channel_id=1, source_target_pairs={{0,8},{8,16},{16,24},{1,9},{9,17},{17,25},{2,10},{10,18},{18,26},{... | collective-permute-start | bytes 983048 | tf_op jit(solution)/shard_map/ppermute | solution.py:21
  33.6 8.1 %all-to-all-done = f32[8,3,32,256]{3,2,1,0:T(8,128)S(1)} async-done(((f32[8,3,32,256]{3,2,1,0:T(8,128)}), f32[8,3,32,256]{3,2,1,0:T(8,128)S(1)}, u32[]{:S(2)}, u32[]{:S(2)}) %all-to-all-start) | async-done | bytes 786464 | tf_op jit(solution)/shard_map/all_to_all | solution.py:458
  41.6 0.1 reduce_sum.9.refs_2_
  41.7 0.0 collective-permute-done.4.down_ref
  41.7 1.6 %collective-permute-start.5 = (f32[3,32,256]{2,1,0:T(8,128)S(1)}, f32[3,32,256]{2,1,0:T(8,128)S(1)}, u32[]{:S(2)}, u32[]{:S(2)}) collective-permute-start(f32[3,32,256]{2,1,0:T(8,128)S(1)} %reduce_sum.9.refs_2_), channel_id=1, source_target_pairs={{0,8},{8,0},{16,24},{24,16},{1,9},{9,1},{17,25},{25,17},{2,10},{10... | collective-permute-start | bytes 294920 | tf_op jit(solution)/shard_map/ppermute | solution.py:37
  43.3 0.2 collective-permute-start.7
  43.5 1.7 %collective-permute-start.9 = (f32[3,32,256]{2,1,0:T(8,128)S(1)}, f32[3,32,256]{2,1,0:T(8,128)S(1)}, u32[]{:S(2)}, u32[]{:S(2)}) collective-permute-start(f32[3,32,256]{2,1,0:T(8,128)S(1)} %reduce_sum.9.refs_2_), channel_id=1, source_target_pairs={{0,24},{8,16},{16,8},{24,0},{1,25},{9,17},{17,9},{25,1},{2,26},{10... | collective-permute-start | bytes 294920 | tf_op jit(solution)/shard_map/ppermute | solution.py:37
  45.2 0.8 %constant_dynamic-slice_fusion.old_ref = f32[2,32,256]{2,1,0:T(8,128)S(1)} fusion(f32[2,256,256]{2,1,0:T(8,128)} %probe_ref.3, s32[]{:T(128)S(6)} %select_n.3), kind=kLoop, calls=%fused_computation | loop fusion | bytes 131076 | tf_op jit(solution)/shard_map/dynamic_slice | solution.py:460
  46.1 0.7 collective-permute-done.5.refs_3_
  46.8 3.4 %collective-permute-done.7.refs_0_ = f32[3,32,256]{2,1,0:T(8,128)S(1)} collective-permute-done((f32[3,32,256]{2,1,0:T(8,128)S(1)}, f32[3,32,256]{2,1,0:T(8,128)S(1)}, u32[]{:S(2)}, u32[]{:S(2)}) %collective-permute-start.7) | collective-permute-done | bytes 98336 | tf_op jit(solution)/shard_map/ppermute | solution.py:37
  50.1 3.1 %collective-permute-done.9.refs_1_ = f32[3,32,256]{2,1,0:T(8,128)S(1)} collective-permute-done((f32[3,32,256]{2,1,0:T(8,128)S(1)}, f32[3,32,256]{2,1,0:T(8,128)S(1)}, u32[]{:S(2)}, u32[]{:S(2)}) %collective-permute-start.9) | collective-permute-done | bytes 98336 | tf_op jit(solution)/shard_map/ppermute | solution.py:37
  53.2 0.8 %shard_map.118 = f32[8,2,32,256]{3,2,1,0:T(8,128)} custom-call(f32[2,32,256]{2,1,0:T(8,128)S(1)} %constant_dynamic-slice_fusion.old_ref, f32[3,32,256]{2,1,0:T(8,128)S(1)} %collective-permute-done.7.refs_0_, f32[3,32,256]{2,1,0:T(8,128)S(1)} %collective-permute-done.9.refs_1_, f32[3,32,256]{2,1,0:T(8,128)S(1)} %reduce_sum.9.refs_2_, ...), custom_call_target="tpu_custom_call" | custom-call | flops 1000000 | bytes 1000000 | tf_op jit(solution)/shard_map/pallas_call | solution.py:466
  54.1 4.3 %all-to-all-start.1 = ((f32[8,2,32,256]{3,2,1,0:T(8,128)}), f32[8,2,32,256]{3,2,1,0:T(8,128)S(1)}, u32[]{:S(2)}, u32[]{:S(2)}) async-start(f32[8,2,32,256]{3,2,1,0:T(8,128)} %shard_map.118), calls=%async_computation.1 | async-start | bytes 1048576 | tf_op jit(solution)/shard_map/all_to_all | solution.py:474
  58.4 2.0 %collective-permute-start.6 = (f32[2,320,128]{2,1,0:T(8,128)S(1)}, f32[2,320,128]{2,1,0:T(8,128)S(1)}, u32[]{:S(2)}, u32[]{:S(2)}) collective-permute-start(f32[2,320,128]{2,1,0:T(8,128)S(1)} %get-tuple-element.32), channel_id=1, source_target_pairs={{0,1},{1,2},{2,3},{3,4},{4,5},{5,6},{6,7},{8,9},{9,10},{10,11},{11... | collective-permute-start | bytes 983048 | tf_op jit(solution)/shard_map/ppermute | solution.py:21
  60.4 3.4 %collective-permute-start.8 = (f32[2,200,128]{2,1,0:T(8,128)S(1)}, f32[2,200,128]{2,1,0:T(8,128)S(1)}, u32[]{:S(2)}, u32[]{:S(2)}) collective-permute-start(f32[2,200,128]{2,1,0:T(8,128)S(1)} %get-tuple-element.35), channel_id=1, source_target_pairs={{0,9},{1,10},{2,11},{3,12},{4,13},{5,14},{6,15},{8,17},{9,18},{10,... | collective-permute-start | bytes 614408 | tf_op jit(solution)/shard_map/ppermute | solution.py:29
  63.8 7.0 %collective-permute-done.8.corner_ref = f32[2,200,128]{2,1,0:T(8,128)S(1)} collective-permute-done((f32[2,200,128]{2,1,0:T(8,128)S(1)}, f32[2,200,128]{2,1,0:T(8,128)S(1)}, u32[]{:S(2)}, u32[]{:S(2)}) %collective-permute-start.8) | collective-permute-done | bytes 204832 | tf_op jit(solution)/shard_map/ppermute | solution.py:29
  70.8 1.5 %collective-permute-done.6.right_ref = f32[2,320,128]{2,1,0:T(8,128)S(1)} collective-permute-done((f32[2,320,128]{2,1,0:T(8,128)S(1)}, f32[2,320,128]{2,1,0:T(8,128)S(1)}, u32[]{:S(2)}, u32[]{:S(2)}) %collective-permute-start.6) | collective-permute-done | bytes 327712 | tf_op jit(solution)/shard_map/ppermute | solution.py:21
  72.4 1.0 %shard_map.117 = f32[2,256,256]{2,1,0:T(8,128)} custom-call(f32[2,8,128]{2,1,0:T(8,128)S(1)} %shard_map.114.peak_ref, f32[2,256,256]{2,1,0:T(8,128)S(1)} %copy-done.1, f32[2,256,256]{2,1,0:T(8,128)S(1)} %get-tuple-element.27.grad_ref, f32[2,320,128]{2,1,0:T(8,128)S(1)} %collective-permute-done.6.right_ref, ...), custom_call_target="tpu_custom_call" | custom-call | flops 1000000 | bytes 4000000 | tf_op jit(solution)/shard_map/pallas_call | solution.py:476
  73.4 0.0 all-to-all-done.1
  73.4 0.8 %copy.12 = f32[2,8,32,256]{3,2,1,0:T(8,128)} copy(f32[2,8,32,256]{3,2,0,1:T(8,128)S(1)} %bitcast.5) | data formatting | bytes 1048576 | tf_op jit(solution)/shard_map/transpose | solution.py:475
Async XLA Ops:
  0.6 1.0 %copy-start = (f32[2,256,256]{2,1,0:T(8,128)S(1)}, f32[2,256,256]{2,1,0:T(8,128)}, u32[]{:S(2)}) copy-start(f32[2,256,256]{2,1,0:T(8,128)} %tile_ref.5) | copy-start | bytes 1572868
  1.7 12.4 %copy-start.4 = (s32[4,2]{0,1:T(2,128)S(1)}, s32[4,2]{0,1:T(2,128)}, u32[]{:S(2)}) copy-start(s32[4,2]{0,1:T(2,128)} %param.13) | copy-start | bytes 100
  1.8 9.7 %collective-permute-start = (f32[2,200,128]{2,1,0:T(8,128)S(1)}, f32[2,200,128]{2,1,0:T(8,128)S(1)}, u32[]{:S(2)}, u32[]{:S(2)}) collective-permute-start(f32[2,200,128]{2,1,0:T(8,128)S(1)} %get-tuple-element.20), channel_id=1, source_target_pairs={{8,0},{16,8},{24,16},{9,1},{17,9},{25,17},{10,2},{18,10},{26,18},{... | collective-permute-start | bytes 614408 | tf_op jit(solution)/shard_map/ppermute | solution.py:21
  4.2 12.9 %collective-permute-start.1 = (f32[2,320,128]{2,1,0:T(8,128)S(1)}, f32[2,320,128]{2,1,0:T(8,128)S(1)}, u32[]{:S(2)}, u32[]{:S(2)}) collective-permute-start(f32[2,320,128]{2,1,0:T(8,128)S(1)} %get-tuple-element.22), channel_id=1, source_target_pairs={{1,0},{2,1},{3,2},{4,3},{5,4},{6,5},{7,6},{9,8},{10,9},{11,10},{12... | collective-permute-start | bytes 983048 | tf_op jit(solution)/shard_map/ppermute | solution.py:21
  6.7 10.3 %collective-permute-start.2 = (f32[2,160,128]{2,1,0:T(8,128)S(1)}, f32[2,160,128]{2,1,0:T(8,128)S(1)}, u32[]{:S(2)}, u32[]{:S(2)}) collective-permute-start(f32[2,160,128]{2,1,0:T(8,128)S(1)} %get-tuple-element.24), channel_id=1, source_target_pairs={{8,0},{16,8},{24,16},{9,1},{17,9},{25,17},{10,2},{18,10},{26,18},{... | collective-permute-start | bytes 491528 | tf_op jit(solution)/shard_map/ppermute | solution.py:21
  9.0 1.2 %copy-start.2 = (f32[4,256,256]{2,1,0:T(8,128)S(1)}, f32[4,256,256]{2,1,0:T(8,128)}, u32[]{:S(2)}) copy-start(f32[4,256,256]{2,1,0:T(8,128)} %meas_ref.3) | copy-start | bytes 3145732
  10.3 1.0 %copy-start.3 = (f32[2,256,256]{2,1,0:T(8,128)S(1)}, f32[2,256,256]{2,1,0:T(8,128)}, u32[]{:S(2)}) copy-start(f32[2,256,256]{2,1,0:T(8,128)} %probe_ref.3) | copy-start | bytes 1572868
  11.5 5.8 %collective-permute-start.3 = (f32[2,200,128]{2,1,0:T(8,128)S(1)}, f32[2,200,128]{2,1,0:T(8,128)S(1)}, u32[]{:S(2)}, u32[]{:S(2)}) collective-permute-start(f32[2,200,128]{2,1,0:T(8,128)S(1)} %collective-permute-done.near_ref), channel_id=1, source_target_pairs={{1,0},{2,1},{3,2},{4,3},{5,4},{6,5},{7,6},{9,8},{10,9},{11,10},{12... | collective-permute-start | bytes 614408 | tf_op jit(solution)/shard_map/ppermute | solution.py:21
  14.1 3.2 %copy-start.1 = (f32[2,256,256]{2,1,0:T(8,128)S(1)}, f32[2,256,256]{2,1,0:T(8,128)}, u32[]{:S(2)}) copy-start(f32[2,256,256]{2,1,0:T(8,128)} %tile_ref.5) | copy-start | bytes 1572868
  14.1 3.2 %copy-start.5 = (bf16[768,256]{1,0:T(8,128)(2,1)S(1)}, bf16[768,256]{1,0:T(8,128)(2,1)}, u32[]{:S(2)}) copy-start(bf16[768,256]{1,0:T(8,128)(2,1)} %constant.24.clone.fwd_right) | copy-start | bytes 1179652
  14.1 3.2 %copy-start.6 = (bf16[256,768]{1,0:T(8,128)(2,1)S(1)}, bf16[256,768]{1,0:T(8,128)(2,1)}, u32[]{:S(2)}) copy-start(bf16[256,768]{1,0:T(8,128)(2,1)} %constant.25.clone.fwd_left) | copy-start | bytes 1179652
  14.1 3.2 %copy-start.7 = (bf16[768,256]{1,0:T(8,128)(2,1)S(1)}, bf16[768,256]{1,0:T(8,128)(2,1)}, u32[]{:S(2)}) copy-start(bf16[768,256]{1,0:T(8,128)(2,1)} %constant.26.clone.inv_right) | copy-start | bytes 1179652
  14.1 3.2 %copy-start.8 = (bf16[256,768]{1,0:T(8,128)(2,1)S(1)}, bf16[256,768]{1,0:T(8,128)(2,1)}, u32[]{:S(2)}) copy-start(bf16[256,768]{1,0:T(8,128)(2,1)} %constant.27.clone.inv_left) | copy-start | bytes 1179652
  14.1 3.2 %copy-start.9 = (f32[2,128,128]{2,1,0:T(8,128)S(1)}, f32[2,128,128]{2,1,0:T(8,128)}, u32[]{:S(2)}) copy-start(f32[2,128,128]{2,1,0:T(8,128)} %constant.29.clone.row_ref) | copy-start | bytes 393220
  14.2 3.2 %copy-start.10 = (f32[2,8,128]{2,1,0:T(8,128)S(1)}, f32[2,8,128]{2,1,0:T(8,128)}, u32[]{:S(2)}) copy-start(f32[2,8,128]{2,1,0:T(8,128)} %constant.28.clone.lane_ref) | copy-start | bytes 24580
  25.4 16.2 %all-to-all-start = ((f32[8,3,32,256]{3,2,1,0:T(8,128)}), f32[8,3,32,256]{3,2,1,0:T(8,128)S(1)}, u32[]{:S(2)}, u32[]{:S(2)}) async-start(f32[8,3,32,256]{3,2,1,0:T(8,128)} %get-tuple-element.29), calls=%async_computation | async-start | bytes 1572864 | tf_op jit(solution)/shard_map/all_to_all | solution.py:458
  30.1 11.6 %collective-permute-start.4 = (f32[2,320,128]{2,1,0:T(8,128)S(1)}, f32[2,320,128]{2,1,0:T(8,128)S(1)}, u32[]{:S(2)}, u32[]{:S(2)}) collective-permute-start(f32[2,320,128]{2,1,0:T(8,128)S(1)} %get-tuple-element.30), channel_id=1, source_target_pairs={{0,8},{8,16},{16,24},{1,9},{9,17},{17,25},{2,10},{10,18},{18,26},{... | collective-permute-start | bytes 983048 | tf_op jit(solution)/shard_map/ppermute | solution.py:21
  41.7 5.1 %collective-permute-start.5 = (f32[3,32,256]{2,1,0:T(8,128)S(1)}, f32[3,32,256]{2,1,0:T(8,128)S(1)}, u32[]{:S(2)}, u32[]{:S(2)}) collective-permute-start(f32[3,32,256]{2,1,0:T(8,128)S(1)} %reduce_sum.9.refs_2_), channel_id=1, source_target_pairs={{0,8},{8,0},{16,24},{24,16},{1,9},{9,1},{17,25},{25,17},{2,10},{10... | collective-permute-start | bytes 294920 | tf_op jit(solution)/shard_map/ppermute | solution.py:37
  43.3 6.8 %collective-permute-start.7 = (f32[3,32,256]{2,1,0:T(8,128)S(1)}, f32[3,32,256]{2,1,0:T(8,128)S(1)}, u32[]{:S(2)}, u32[]{:S(2)}) collective-permute-start(f32[3,32,256]{2,1,0:T(8,128)S(1)} %reduce_sum.9.refs_2_), channel_id=1, source_target_pairs={{0,16},{8,24},{16,0},{24,8},{1,17},{9,25},{17,1},{25,9},{2,18},{10... | collective-permute-start | bytes 294920 | tf_op jit(solution)/shard_map/ppermute | solution.py:37
  43.5 9.7 %collective-permute-start.9 = (f32[3,32,256]{2,1,0:T(8,128)S(1)}, f32[3,32,256]{2,1,0:T(8,128)S(1)}, u32[]{:S(2)}, u32[]{:S(2)}) collective-permute-start(f32[3,32,256]{2,1,0:T(8,128)S(1)} %reduce_sum.9.refs_2_), channel_id=1, source_target_pairs={{0,24},{8,16},{16,8},{24,0},{1,25},{9,17},{17,9},{25,1},{2,26},{10... | collective-permute-start | bytes 294920 | tf_op jit(solution)/shard_map/ppermute | solution.py:37
  54.1 19.3 %all-to-all-start.1 = ((f32[8,2,32,256]{3,2,1,0:T(8,128)}), f32[8,2,32,256]{3,2,1,0:T(8,128)S(1)}, u32[]{:S(2)}, u32[]{:S(2)}) async-start(f32[8,2,32,256]{3,2,1,0:T(8,128)} %shard_map.118), calls=%async_computation.1 | async-start | bytes 1048576 | tf_op jit(solution)/shard_map/all_to_all | solution.py:474
  58.4 14.0 %collective-permute-start.6 = (f32[2,320,128]{2,1,0:T(8,128)S(1)}, f32[2,320,128]{2,1,0:T(8,128)S(1)}, u32[]{:S(2)}, u32[]{:S(2)}) collective-permute-start(f32[2,320,128]{2,1,0:T(8,128)S(1)} %get-tuple-element.32), channel_id=1, source_target_pairs={{0,1},{1,2},{2,3},{3,4},{4,5},{5,6},{6,7},{8,9},{9,10},{10,11},{11... | collective-permute-start | bytes 983048 | tf_op jit(solution)/shard_map/ppermute | solution.py:21
  60.4 10.4 %collective-permute-start.8 = (f32[2,200,128]{2,1,0:T(8,128)S(1)}, f32[2,200,128]{2,1,0:T(8,128)S(1)}, u32[]{:S(2)}, u32[]{:S(2)}) collective-permute-start(f32[2,200,128]{2,1,0:T(8,128)S(1)} %get-tuple-element.35), channel_id=1, source_target_pairs={{0,9},{1,10},{2,11},{3,12},{4,13},{5,14},{6,15},{8,17},{9,18},{10,... | collective-permute-start | bytes 614408 | tf_op jit(solution)/shard_map/ppermute | solution.py:29

commit v5 on v4

--- a/solution.py
+++ b/solution.py
@@ -175,6 +175,7 @@
     def store_left(where, rows, tile, value):
         high, low = halves(value)
         lane = tile * half
+        where, rows = where // 2, slice(where % 2 * side + rows.start, where % 2 * side + rows.stop)
         left_in[where, rows, lane : lane + half] = high
         left_in[where, rows, side + lane : side + lane + half] = low
         left_in[where, rows, 2 * side + lane : 2 * side + lane + half] = high
@@ -217,8 +218,8 @@
             re, im = re0 - re1, im0 - im1
             store_left(2 * frame + 1, rows, 0, re * lane_cos - im * lane_sin)
             store_left(2 * frame + 1, rows, 1, re * lane_sin + im * lane_cos)
-        for which in range(2):
-            mid[2 * frame + which] = dot(left_in[2 * frame + which], fwd_right[...])
+        product = dot(left_in[frame], fwd_right[...])
+        mid[2 * frame], mid[2 * frame + 1] = product[:side], product[side:]
 
     for frame in range(frames):
         for row in range(0, half, step):
@@ -261,8 +262,8 @@
                 store_left(2 * frame + which, top, 1, even_im + im)
                 store_left(2 * frame + which, low, 0, even_re - re)
                 store_left(2 * frame + which, low, 1, even_im - im)
-        for which in range(2):
-            mid[2 * frame + which] = dot(left_in[2 * frame + which], inv_right[...])
+        product = dot(left_in[frame], inv_right[...])
+        mid[2 * frame], mid[2 * frame + 1] = product[:side], product[side:]
 
     step = 8
     lanes = lax.broadcasted_iota(jnp.int32, (step, half), 1)
@@ -362,11 +363,14 @@
             out_ref[copy, part] = value
 
 
-def finish_kernel(peak_ref, tile_ref, grad_ref, right_ref, down_ref, corner_ref, out_ref):
+def finish_kernel(peak_ref, tile_ref, grad_ref, right_ref, down_ref, corner_ref, new_ref, out_ref, probe_ref):
     side = tile_ref.shape[1]
     half = side // 2
     margin = down_ref.shape[1] // 2
     extra = margin - half
+    depth = new_ref.shape[2]
+    for block in range(new_ref.shape[0]):
+        probe_ref[:, block * depth : (block + 1) * depth, :] = new_ref[block]
     largest = peak_ref[0]
     step = 8
     for row, packed, lane in pack_extra(side, extra, half):
@@ -442,7 +446,7 @@
             pltpu.VMEM((2, side, half), jnp.float32),
             pltpu.VMEM((2, margin, half), jnp.float32),
             pltpu.VMEM((frames, 2, side, side), jnp.float32),
-            pltpu.VMEM((2 * frames, side, 3 * side), BF16),
+            pltpu.VMEM((frames, 2 * side, 3 * side), BF16),
             pltpu.VMEM((2 * frames, 3 * side, side), BF16),
             pltpu.VMEM((2 * frames, side, side), jnp.float32),
             pltpu.VMEM((frames, 3, 2, side + margin, half), jnp.float32),
@@ -456,10 +460,9 @@
 
     from_above = shifted(g_down, "row", 1)
     part = jnp.sum(lax.all_to_all(sums, "col", 0, 0), 0)
-    part, from_above = lax.optimization_barrier((part, from_above))
+    part, from_above, g_right = lax.optimization_barrier((part, from_above, g_right))
     old = lax.dynamic_slice_in_dim(probe_field, lax.axis_index("col") * depth, depth, 1)
     terms = row_terms(part)
-    g_right, terms[-1] = lax.optimization_barrier((g_right, terms[-1]))
     from_left = shifted(g_right, "col", 1)
     g_corner, terms[0] = lax.optimization_barrier((g_corner, terms[0]))
     from_corner = diagonal(g_corner)
@@ -468,19 +471,19 @@
         out_shape=f32(n_col, 2, depth, side),
         in_specs=[VMEM] * (1 + len(terms)),
         out_specs=VMEM,
-        cost_estimate=cost(10**6, 10**6),
+        cost_estimate=cost(10**10, 10**6),
         compiler_params=PARAMS,
     )(old, *terms)
+    new, from_left = lax.optimization_barrier((new, from_left))
     new = lax.all_to_all(new, "col", 0, 0)
-    new_probe = new.transpose(1, 0, 2, 3).reshape(2, side, side)
-    new_object = pl.pallas_call(
+    new_object, new_probe = pl.pallas_call(
         finish_kernel,
-        out_shape=f32(2, side, side),
-        in_specs=[VMEM] * 6,
-        out_specs=VMEM,
+        out_shape=(f32(2, side, side), f32(2, side, side)),
+        in_specs=[VMEM] * 7,
+        out_specs=(VMEM, VMEM),
         cost_estimate=cost(10**6, 4 * 10**6),
         compiler_params=PARAMS,
-    )(peak, object_field, g_tile, from_left, from_above, from_corner)
+    )(peak, object_field, g_tile, from_left, from_above, from_corner, new)
     return (new_object, new_probe)
 
 

time: 74.8 us -> 72.2 us (0.965)
  starting transfers between devices: 31.1 us -> 29.8 us
  waiting for transfers between devices: 24.1 us -> 23.1 us
  local copies, waits for them, and re-layouts: 5.04 us -> 4.19 us
    ppermute x3, waiting for transfers between devices: 7.15 us -> 4.04 us  [row_terms(): lax.ppermute(value, 'row', [(row, row ^ step) for row in range(rows)])]
    ppermute x1, starting transfers between devices: 3.36 us -> 2.17 us  [diagonal(): return lax.ppermute(value, ('row', 'col'), pairs)]
    ppermute x1, waiting for transfers between devices: 7.04 us -> 8.15 us  [diagonal(): return lax.ppermute(value, ('row', 'col'), pairs)]
    ppermute x6, waiting for transfers between devices: 1.87 us -> 2.8 us  [shifted(): lax.ppermute(value, axis, [(source, source + steps) for source in range(i...]
    ppermute x3, starting transfers between devices: 3.53 us -> 4.42 us  [row_terms(): lax.ppermute(value, 'row', [(row, row ^ step) for row in range(rows)])]
    transpose x1 -> x0, local copies, waits for them, and re-layouts: 0.84 us -> none  [body(): new_probe = new.transpose(1, 0, 2, 3).reshape(2, side, side)]
    all_to_all x1, starting transfers between devices: 4.29 us -> 3.45 us  [body(): new = lax.all_to_all(new, 'col', 0, 0)]
  transfers between devices with their start and end apart: 12 -> 12, of which waited for: 7 -> 5; matrix products, arithmetic and copies ran while one was open for 1% -> 1% of each run, Pallas kernels for 5% -> 5%
where the time goes in v5:
time: 72.2 us; the launch traced here: 71.6 us
  starting transfers between devices  29.8 us (41%)
  waiting for transfers between devices  23.1 us (32%)
  Pallas kernels  13.5 us (19%)
  local copies, waits for them, and re-layouts  4.19 us (6%)
  between operations  0.87 us (1%)
    ppermute x6, starting transfers between devices, shifted(): lax.ppermute(value, axis, [(source, source + steps) for source in range(i...  15.2 us
    pallas_call x1, Pallas kernels, body(): pl.pallas_call(frame_kernel, out_shape=(f32(2, side, side), f32(2, wide,...  8.41 us
    ppermute x1, waiting for transfers between devices, diagonal(): return lax.ppermute(value, ('row', 'col'), pairs)  8.15 us
    all_to_all x1, waiting for transfers between devices, body(): part = jnp.sum(lax.all_to_all(sums, 'col', 0, 0), 0)  8.07 us
    all_to_all x1, starting transfers between devices, body(): part = jnp.sum(lax.all_to_all(sums, 'col', 0, 0), 0)  4.63 us
    ppermute x3, starting transfers between devices, row_terms(): lax.ppermute(value, 'row', [(row, row ^ step) for row in range(rows)])  4.42 us
    ppermute x3, waiting for transfers between devices, row_terms(): lax.ppermute(value, 'row', [(row, row ^ step) for row in range(rows)])  4.04 us
    all_to_all x1, starting transfers between devices, body(): new = lax.all_to_all(new, 'col', 0, 0)  3.45 us
  transfers between devices with their start and end apart: 12, of which 5 were waited for; matrix products, arithmetic and copies ran while one was open for 1% of the time, Pallas kernels for 5%

profile of v5, /device:TPU:20, one launch (start us, length us, event | category | flops | bytes accessed | tf_op | source)
XLA Modules:
  0.0 71.6 jit_solution(4157610660738197974)
XLA Ops:
  0.6 0.0 copy-start
  0.6 1.0 %copy-done = f32[2,256,256]{2,1,0:T(8,128)S(1)} copy-done((f32[2,256,256]{2,1,0:T(8,128)S(1)}, f32[2,256,256]{2,1,0:T(8,128)}, u32[]{:S(2)}) %copy-start) | copy-done | bytes 524312
  1.7 0.0 copy-start.4
  1.7 0.1 shard_map.113
  1.8 2.4 %collective-permute-start = (f32[2,200,128]{2,1,0:T(8,128)S(1)}, f32[2,200,128]{2,1,0:T(8,128)S(1)}, u32[]{:S(2)}, u32[]{:S(2)}) collective-permute-start(f32[2,200,128]{2,1,0:T(8,128)S(1)} %get-tuple-element.21), channel_id=1, source_target_pairs={{8,0},{16,8},{24,16},{9,1},{17,9},{25,17},{10,2},{18,10},{26,18},{... | collective-permute-start | bytes 614408 | tf_op jit(solution)/shard_map/ppermute | solution.py:21
  4.2 2.5 %collective-permute-start.1 = (f32[2,320,128]{2,1,0:T(8,128)S(1)}, f32[2,320,128]{2,1,0:T(8,128)S(1)}, u32[]{:S(2)}, u32[]{:S(2)}) collective-permute-start(f32[2,320,128]{2,1,0:T(8,128)S(1)} %get-tuple-element.23), channel_id=1, source_target_pairs={{1,0},{2,1},{3,2},{4,3},{5,4},{6,5},{7,6},{9,8},{10,9},{11,10},{12... | collective-permute-start | bytes 983048 | tf_op jit(solution)/shard_map/ppermute | solution.py:21
  6.7 2.4 %collective-permute-start.2 = (f32[2,160,128]{2,1,0:T(8,128)S(1)}, f32[2,160,128]{2,1,0:T(8,128)S(1)}, u32[]{:S(2)}, u32[]{:S(2)}) collective-permute-start(f32[2,160,128]{2,1,0:T(8,128)S(1)} %get-tuple-element.25), channel_id=1, source_target_pairs={{8,0},{16,8},{24,16},{9,1},{17,9},{25,17},{10,2},{18,10},{26,18},{... | collective-permute-start | bytes 491528 | tf_op jit(solution)/shard_map/ppermute | solution.py:21
  9.0 0.0 copy-start.2
  9.0 1.2 %copy-done.2 = f32[4,256,256]{2,1,0:T(8,128)S(1)} copy-done((f32[4,256,256]{2,1,0:T(8,128)S(1)}, f32[4,256,256]{2,1,0:T(8,128)}, u32[]{:S(2)}) %copy-start.2) | copy-done | bytes 1048600
  10.3 0.0 copy-start.3
  10.3 1.0 %copy-done.3 = f32[2,256,256]{2,1,0:T(8,128)S(1)} copy-done((f32[2,256,256]{2,1,0:T(8,128)S(1)}, f32[2,256,256]{2,1,0:T(8,128)}, u32[]{:S(2)}) %copy-start.3) | copy-done | bytes 524312
  11.3 0.2 shard_map.114.peak_ref
  11.5 0.0 collective-permute-done.near_ref
  11.5 2.6 %collective-permute-start.3 = (f32[2,200,128]{2,1,0:T(8,128)S(1)}, f32[2,200,128]{2,1,0:T(8,128)S(1)}, u32[]{:S(2)}, u32[]{:S(2)}) collective-permute-start(f32[2,200,128]{2,1,0:T(8,128)S(1)} %collective-permute-done.near_ref), channel_id=1, source_target_pairs={{1,0},{2,1},{3,2},{4,3},{5,4},{6,5},{7,6},{9,8},{10,9},{11,10},{12... | collective-permute-start | bytes 614408 | tf_op jit(solution)/shard_map/ppermute | solution.py:21
  14.1 0.0 copy-done.4
  14.1 0.0 copy-start.1
  14.1 0.0 copy-start.5
  14.1 0.0 copy-start.6
  14.1 0.0 copy-start.7
  14.1 0.0 copy-start.8
  14.1 0.0 copy-start.9
  14.2 0.0 copy-start.10
  14.2 2.8 %shard_map.115 = (f32[4,2,256,256]{3,2,1,0:T(8,128)S(1)}, f32[4,256,256]{2,1,0:T(8,128)S(1)}) custom-call(s32[2,4]{1,0:T(2,128)S(1)} %bitcast.1, f32[2,256,256]{2,1,0:T(8,128)S(1)} %copy-done.3, f32[4,256,256]{2,1,0:T(8,128)S(1)} %copy-done.2), custom_call_target="tpu_custom_call" | custom-call | flops 3000000000 | bytes 6000000 | tf_op jit(solution)/shard_map/pallas_call | solution.py:424
  17.0 0.0 collective-permute-done.2.far_ref
  17.0 0.0 collective-permute-done.1.right_ref
  17.0 0.3 collective-permute-done.3.corner_ref
  17.3 0.0 copy-done.1
  17.3 0.0 copy-done.5
  17.3 0.0 copy-done.6
  17.3 0.0 copy-done.7
  17.3 0.0 copy-done.8
  17.4 0.0 copy-done.9
  17.4 0.0 copy-done.10
  17.4 8.4 %shard_map.116 = (f32[2,256,256]{2,1,0:T(8,128)S(1)}, f32[2,320,128]{2,1,0:T(8,128)S(1)}, f32[2,320,128]{2,1,0:T(8,128)S(1)}, f32[2,200,128]{2,1,0:T(8,128)S(1)}, f32[8,3,32,256]{3,2,1,0:T(8,128)}) custom-call(s32[2,4]{1,0:T(2,128)S(1)} %bitcast.2, f32[2,256,256]{2,1,0:T(8,128)S(1)} %copy-done.1, f32[2,320,128]{2,1,0:T(8,128)S(1)} %collective-permute-done.1.right_ref, ...), custom_call_target="tpu_custom_call" | custom-call | flops 6000000000 | bytes 12000000 | tf_op jit(solution)/shard_map/pallas_call | solution.py:434
  25.8 4.6 %all-to-all-start = ((f32[8,3,32,256]{3,2,1,0:T(8,128)}), f32[8,3,32,256]{3,2,1,0:T(8,128)S(1)}, u32[]{:S(2)}, u32[]{:S(2)}) async-start(f32[8,3,32,256]{3,2,1,0:T(8,128)} %get-tuple-element.30), calls=%async_computation | async-start | bytes 1572864 | tf_op jit(solution)/shard_map/all_to_all | solution.py:462
  30.4 3.5 %collective-permute-start.4 = (f32[2,320,128]{2,1,0:T(8,128)S(1)}, f32[2,320,128]{2,1,0:T(8,128)S(1)}, u32[]{:S(2)}, u32[]{:S(2)}) collective-permute-start(f32[2,320,128]{2,1,0:T(8,128)S(1)} %get-tuple-element.31), channel_id=1, source_target_pairs={{0,8},{8,16},{16,24},{1,9},{9,17},{17,25},{2,10},{10,18},{18,26},{... | collective-permute-start | bytes 983048 | tf_op jit(solution)/shard_map/ppermute | solution.py:21
  33.9 8.1 %all-to-all-done = f32[8,3,32,256]{3,2,1,0:T(8,128)S(1)} async-done(((f32[8,3,32,256]{3,2,1,0:T(8,128)}), f32[8,3,32,256]{3,2,1,0:T(8,128)S(1)}, u32[]{:S(2)}, u32[]{:S(2)}) %all-to-all-start) | async-done | bytes 786464 | tf_op jit(solution)/shard_map/all_to_all | solution.py:462
  42.0 0.1 reduce_sum.9.refs_2_
  42.0 0.0 collective-permute-done.4.down_ref
  42.1 0.0 collective-permute-start.5
  42.1 3.0 %collective-permute-start.6 = (f32[3,32,256]{2,1,0:T(8,128)S(1)}, f32[3,32,256]{2,1,0:T(8,128)S(1)}, u32[]{:S(2)}, u32[]{:S(2)}) collective-permute-start(f32[3,32,256]{2,1,0:T(8,128)S(1)} %reduce_sum.9.refs_2_), channel_id=1, source_target_pairs={{0,24},{8,16},{16,8},{24,0},{1,25},{9,17},{17,9},{25,1},{2,26},{10... | collective-permute-start | bytes 294920 | tf_op jit(solution)/shard_map/ppermute | solution.py:37
  45.1 1.4 %collective-permute-start.7 = (f32[3,32,256]{2,1,0:T(8,128)S(1)}, f32[3,32,256]{2,1,0:T(8,128)S(1)}, u32[]{:S(2)}, u32[]{:S(2)}) collective-permute-start(f32[3,32,256]{2,1,0:T(8,128)S(1)} %reduce_sum.9.refs_2_), channel_id=1, source_target_pairs={{0,8},{8,0},{16,24},{24,16},{1,9},{9,1},{17,25},{25,17},{2,10},{10... | collective-permute-start | bytes 294920 | tf_op jit(solution)/shard_map/ppermute | solution.py:37
  46.5 0.8 %constant_dynamic-slice_fusion.old_ref = f32[2,32,256]{2,1,0:T(8,128)S(1)} fusion(f32[2,256,256]{2,1,0:T(8,128)} %probe_ref.3, s32[]{:T(128)S(6)} %select_n.3), kind=kLoop, calls=%fused_computation | loop fusion | bytes 131076 | tf_op jit(solution)/shard_map/dynamic_slice | solution.py:464
  47.3 1.9 %collective-permute-start.8 = (f32[2,320,128]{2,1,0:T(8,128)S(1)}, f32[2,320,128]{2,1,0:T(8,128)S(1)}, u32[]{:S(2)}, u32[]{:S(2)}) collective-permute-start(f32[2,320,128]{2,1,0:T(8,128)S(1)} %get-tuple-element.35), channel_id=1, source_target_pairs={{0,1},{1,2},{2,3},{3,4},{4,5},{5,6},{6,7},{8,9},{9,10},{10,11},{11... | collective-permute-start | bytes 983048 | tf_op jit(solution)/shard_map/ppermute | solution.py:21
  49.2 0.0 collective-permute-done.5.refs_0_
  49.3 4.0 %collective-permute-done.6.refs_1_ = f32[3,32,256]{2,1,0:T(8,128)S(1)} collective-permute-done((f32[3,32,256]{2,1,0:T(8,128)S(1)}, f32[3,32,256]{2,1,0:T(8,128)S(1)}, u32[]{:S(2)}, u32[]{:S(2)}) %collective-permute-start.6) | collective-permute-done | bytes 98336 | tf_op jit(solution)/shard_map/ppermute | solution.py:37
  53.3 0.0 collective-permute-done.7.refs_3_
  53.3 0.8 %shard_map.117 = f32[8,2,32,256]{3,2,1,0:T(8,128)} custom-call(f32[2,32,256]{2,1,0:T(8,128)S(1)} %constant_dynamic-slice_fusion.old_ref, f32[3,32,256]{2,1,0:T(8,128)S(1)} %collective-permute-done.5.refs_0_, f32[3,32,256]{2,1,0:T(8,128)S(1)} %collective-permute-done.6.refs_1_, f32[3,32,256]{2,1,0:T(8,128)S(1)} %reduce_sum.9.refs_2_, ...), custom_call_target="tpu_custom_call" | custom-call | flops 10000000000 | bytes 1000000 | tf_op jit(solution)/shard_map/pallas_call | solution.py:469
  54.1 2.5 %collective-permute-done.8.right_ref = f32[2,320,128]{2,1,0:T(8,128)S(1)} collective-permute-done((f32[2,320,128]{2,1,0:T(8,128)S(1)}, f32[2,320,128]{2,1,0:T(8,128)S(1)}, u32[]{:S(2)}, u32[]{:S(2)}) %collective-permute-start.8) | collective-permute-done | bytes 327712 | tf_op jit(solution)/shard_map/ppermute | solution.py:21
  56.6 3.4 %all-to-all-start.1 = ((f32[8,2,32,256]{3,2,1,0:T(8,128)}), f32[8,2,32,256]{3,2,1,0:T(8,128)S(1)}, u32[]{:S(2)}, u32[]{:S(2)}) async-start(f32[8,2,32,256]{3,2,1,0:T(8,128)} %shard_map.117), calls=%async_computation.1 | async-start | bytes 1048576 | tf_op jit(solution)/shard_map/all_to_all | solution.py:478
  60.1 2.2 %collective-permute-start.9 = (f32[2,200,128]{2,1,0:T(8,128)S(1)}, f32[2,200,128]{2,1,0:T(8,128)S(1)}, u32[]{:S(2)}, u32[]{:S(2)}) collective-permute-start(f32[2,200,128]{2,1,0:T(8,128)S(1)} %get-tuple-element.38), channel_id=1, source_target_pairs={{0,9},{1,10},{2,11},{3,12},{4,13},{5,14},{6,15},{8,17},{9,18},{10,... | collective-permute-start | bytes 614408 | tf_op jit(solution)/shard_map/ppermute | solution.py:29
  62.2 8.2 %collective-permute-done.9.corner_ref = f32[2,200,128]{2,1,0:T(8,128)S(1)} collective-permute-done((f32[2,200,128]{2,1,0:T(8,128)S(1)}, f32[2,200,128]{2,1,0:T(8,128)S(1)}, u32[]{:S(2)}, u32[]{:S(2)}) %collective-permute-start.9) | collective-permute-done | bytes 204832 | tf_op jit(solution)/shard_map/ppermute | solution.py:29
  70.4 0.0 all-to-all-done.1.new_ref
  70.4 1.2 %shard_map.118 = (f32[2,256,256]{2,1,0:T(8,128)}, f32[2,256,256]{2,1,0:T(8,128)}) custom-call(f32[2,8,128]{2,1,0:T(8,128)S(1)} %shard_map.114.peak_ref, f32[2,256,256]{2,1,0:T(8,128)S(1)} %copy-done.1, f32[2,256,256]{2,1,0:T(8,128)S(1)} %get-tuple-element.28.grad_ref, f32[2,320,128]{2,1,0:T(8,128)S(1)} %collective-permute-done.8.right_ref, ...), custom_call_target="tpu_custom_call" | custom-call | flops 1000000 | bytes 4000000 | tf_op jit(solution)/shard_map/pallas_call | solution.py:479
Async XLA Ops:
  0.6 1.0 %copy-start = (f32[2,256,256]{2,1,0:T(8,128)S(1)}, f32[2,256,256]{2,1,0:T(8,128)}, u32[]{:S(2)}) copy-start(f32[2,256,256]{2,1,0:T(8,128)} %tile_ref.5) | copy-start | bytes 1572868
  1.7 12.4 %copy-start.4 = (s32[4,2]{0,1:T(2,128)S(1)}, s32[4,2]{0,1:T(2,128)}, u32[]{:S(2)}) copy-start(s32[4,2]{0,1:T(2,128)} %param.13) | copy-start | bytes 100
  1.8 9.7 %collective-permute-start = (f32[2,200,128]{2,1,0:T(8,128)S(1)}, f32[2,200,128]{2,1,0:T(8,128)S(1)}, u32[]{:S(2)}, u32[]{:S(2)}) collective-permute-start(f32[2,200,128]{2,1,0:T(8,128)S(1)} %get-tuple-element.21), channel_id=1, source_target_pairs={{8,0},{16,8},{24,16},{9,1},{17,9},{25,17},{10,2},{18,10},{26,18},{... | collective-permute-start | bytes 614408 | tf_op jit(solution)/shard_map/ppermute | solution.py:21
  4.2 12.9 %collective-permute-start.1 = (f32[2,320,128]{2,1,0:T(8,128)S(1)}, f32[2,320,128]{2,1,0:T(8,128)S(1)}, u32[]{:S(2)}, u32[]{:S(2)}) collective-permute-start(f32[2,320,128]{2,1,0:T(8,128)S(1)} %get-tuple-element.23), channel_id=1, source_target_pairs={{1,0},{2,1},{3,2},{4,3},{5,4},{6,5},{7,6},{9,8},{10,9},{11,10},{12... | collective-permute-start | bytes 983048 | tf_op jit(solution)/shard_map/ppermute | solution.py:21
  6.7 10.3 %collective-permute-start.2 = (f32[2,160,128]{2,1,0:T(8,128)S(1)}, f32[2,160,128]{2,1,0:T(8,128)S(1)}, u32[]{:S(2)}, u32[]{:S(2)}) collective-permute-start(f32[2,160,128]{2,1,0:T(8,128)S(1)} %get-tuple-element.25), channel_id=1, source_target_pairs={{8,0},{16,8},{24,16},{9,1},{17,9},{25,17},{10,2},{18,10},{26,18},{... | collective-permute-start | bytes 491528 | tf_op jit(solution)/shard_map/ppermute | solution.py:21
  9.0 1.2 %copy-start.2 = (f32[4,256,256]{2,1,0:T(8,128)S(1)}, f32[4,256,256]{2,1,0:T(8,128)}, u32[]{:S(2)}) copy-start(f32[4,256,256]{2,1,0:T(8,128)} %meas_ref.3) | copy-start | bytes 3145732
  10.3 1.0 %copy-start.3 = (f32[2,256,256]{2,1,0:T(8,128)S(1)}, f32[2,256,256]{2,1,0:T(8,128)}, u32[]{:S(2)}) copy-start(f32[2,256,256]{2,1,0:T(8,128)} %probe_ref.3) | copy-start | bytes 1572868
  11.5 5.8 %collective-permute-start.3 = (f32[2,200,128]{2,1,0:T(8,128)S(1)}, f32[2,200,128]{2,1,0:T(8,128)S(1)}, u32[]{:S(2)}, u32[]{:S(2)}) collective-permute-start(f32[2,200,128]{2,1,0:T(8,128)S(1)} %collective-permute-done.near_ref), channel_id=1, source_target_pairs={{1,0},{2,1},{3,2},{4,3},{5,4},{6,5},{7,6},{9,8},{10,9},{11,10},{12... | collective-permute-start | bytes 614408 | tf_op jit(solution)/shard_map/ppermute | solution.py:21
  14.1 3.2 %copy-start.1 = (f32[2,256,256]{2,1,0:T(8,128)S(1)}, f32[2,256,256]{2,1,0:T(8,128)}, u32[]{:S(2)}) copy-start(f32[2,256,256]{2,1,0:T(8,128)} %tile_ref.5) | copy-start | bytes 1572868
  14.1 3.2 %copy-start.5 = (bf16[768,256]{1,0:T(8,128)(2,1)S(1)}, bf16[768,256]{1,0:T(8,128)(2,1)}, u32[]{:S(2)}) copy-start(bf16[768,256]{1,0:T(8,128)(2,1)} %constant.24.clone.fwd_right) | copy-start | bytes 1179652
  14.1 3.2 %copy-start.6 = (bf16[256,768]{1,0:T(8,128)(2,1)S(1)}, bf16[256,768]{1,0:T(8,128)(2,1)}, u32[]{:S(2)}) copy-start(bf16[256,768]{1,0:T(8,128)(2,1)} %constant.25.clone.fwd_left) | copy-start | bytes 1179652
  14.1 3.2 %copy-start.7 = (bf16[768,256]{1,0:T(8,128)(2,1)S(1)}, bf16[768,256]{1,0:T(8,128)(2,1)}, u32[]{:S(2)}) copy-start(bf16[768,256]{1,0:T(8,128)(2,1)} %constant.26.clone.inv_right) | copy-start | bytes 1179652
  14.1 3.2 %copy-start.8 = (bf16[256,768]{1,0:T(8,128)(2,1)S(1)}, bf16[256,768]{1,0:T(8,128)(2,1)}, u32[]{:S(2)}) copy-start(bf16[256,768]{1,0:T(8,128)(2,1)} %constant.27.clone.inv_left) | copy-start | bytes 1179652
  14.1 3.2 %copy-start.9 = (f32[2,128,128]{2,1,0:T(8,128)S(1)}, f32[2,128,128]{2,1,0:T(8,128)}, u32[]{:S(2)}) copy-start(f32[2,128,128]{2,1,0:T(8,128)} %constant.29.clone.row_ref) | copy-start | bytes 393220
  14.2 3.2 %copy-start.10 = (f32[2,8,128]{2,1,0:T(8,128)S(1)}, f32[2,8,128]{2,1,0:T(8,128)}, u32[]{:S(2)}) copy-start(f32[2,8,128]{2,1,0:T(8,128)} %constant.28.clone.lane_ref) | copy-start | bytes 24580
  25.8 16.2 %all-to-all-start = ((f32[8,3,32,256]{3,2,1,0:T(8,128)}), f32[8,3,32,256]{3,2,1,0:T(8,128)S(1)}, u32[]{:S(2)}, u32[]{:S(2)}) async-start(f32[8,3,32,256]{3,2,1,0:T(8,128)} %get-tuple-element.30), calls=%async_computation | async-start | bytes 1572864 | tf_op jit(solution)/shard_map/all_to_all | solution.py:462
  30.4 11.6 %collective-permute-start.4 = (f32[2,320,128]{2,1,0:T(8,128)S(1)}, f32[2,320,128]{2,1,0:T(8,128)S(1)}, u32[]{:S(2)}, u32[]{:S(2)}) collective-permute-start(f32[2,320,128]{2,1,0:T(8,128)S(1)} %get-tuple-element.31), channel_id=1, source_target_pairs={{0,8},{8,16},{16,24},{1,9},{9,17},{17,25},{2,10},{10,18},{18,26},{... | collective-permute-start | bytes 983048 | tf_op jit(solution)/shard_map/ppermute | solution.py:21
  42.1 7.2 %collective-permute-start.5 = (f32[3,32,256]{2,1,0:T(8,128)S(1)}, f32[3,32,256]{2,1,0:T(8,128)S(1)}, u32[]{:S(2)}, u32[]{:S(2)}) collective-permute-start(f32[3,32,256]{2,1,0:T(8,128)S(1)} %reduce_sum.9.refs_2_), channel_id=1, source_target_pairs={{0,16},{8,24},{16,0},{24,8},{1,17},{9,25},{17,1},{25,9},{2,18},{10... | collective-permute-start | bytes 294920 | tf_op jit(solution)/shard_map/ppermute | solution.py:37
  42.1 11.2 %collective-permute-start.6 = (f32[3,32,256]{2,1,0:T(8,128)S(1)}, f32[3,32,256]{2,1,0:T(8,128)S(1)}, u32[]{:S(2)}, u32[]{:S(2)}) collective-permute-start(f32[3,32,256]{2,1,0:T(8,128)S(1)} %reduce_sum.9.refs_2_), channel_id=1, source_target_pairs={{0,24},{8,16},{16,8},{24,0},{1,25},{9,17},{17,9},{25,1},{2,26},{10... | collective-permute-start | bytes 294920 | tf_op jit(solution)/shard_map/ppermute | solution.py:37
  45.1 8.2 %collective-permute-start.7 = (f32[3,32,256]{2,1,0:T(8,128)S(1)}, f32[3,32,256]{2,1,0:T(8,128)S(1)}, u32[]{:S(2)}, u32[]{:S(2)}) collective-permute-start(f32[3,32,256]{2,1,0:T(8,128)S(1)} %reduce_sum.9.refs_2_), channel_id=1, source_target_pairs={{0,8},{8,0},{16,24},{24,16},{1,9},{9,1},{17,25},{25,17},{2,10},{10... | collective-permute-start | bytes 294920 | tf_op jit(solution)/shard_map/ppermute | solution.py:37
  47.3 9.3 %collective-permute-start.8 = (f32[2,320,128]{2,1,0:T(8,128)S(1)}, f32[2,320,128]{2,1,0:T(8,128)S(1)}, u32[]{:S(2)}, u32[]{:S(2)}) collective-permute-start(f32[2,320,128]{2,1,0:T(8,128)S(1)} %get-tuple-element.35), channel_id=1, source_target_pairs={{0,1},{1,2},{2,3},{3,4},{4,5},{5,6},{6,7},{8,9},{9,10},{10,11},{11... | collective-permute-start | bytes 983048 | tf_op jit(solution)/shard_map/ppermute | solution.py:21
  56.6 13.8 %all-to-all-start.1 = ((f32[8,2,32,256]{3,2,1,0:T(8,128)}), f32[8,2,32,256]{3,2,1,0:T(8,128)S(1)}, u32[]{:S(2)}, u32[]{:S(2)}) async-start(f32[8,2,32,256]{3,2,1,0:T(8,128)} %shard_map.117), calls=%async_computation.1 | async-start | bytes 1048576 | tf_op jit(solution)/shard_map/all_to_all | solution.py:478
  60.1 10.3 %collective-permute-start.9 = (f32[2,200,128]{2,1,0:T(8,128)S(1)}, f32[2,200,128]{2,1,0:T(8,128)S(1)}, u32[]{:S(2)}, u32[]{:S(2)}) collective-permute-start(f32[2,200,128]{2,1,0:T(8,128)S(1)} %get-tuple-element.38), channel_id=1, source_target_pairs={{0,9},{1,10},{2,11},{3,12},{4,13},{5,14},{6,15},{8,17},{9,18},{10,... | collective-permute-start | bytes 614408 | tf_op jit(solution)/shard_map/ppermute | solution.py:29

commit v6 on v5

--- a/solution.py
+++ b/solution.py
@@ -175,7 +175,6 @@
     def store_left(where, rows, tile, value):
         high, low = halves(value)
         lane = tile * half
-        where, rows = where // 2, slice(where % 2 * side + rows.start, where % 2 * side + rows.stop)
         left_in[where, rows, lane : lane + half] = high
         left_in[where, rows, side + lane : side + lane + half] = low
         left_in[where, rows, 2 * side + lane : 2 * side + lane + half] = high
@@ -218,8 +217,8 @@
             re, im = re0 - re1, im0 - im1
             store_left(2 * frame + 1, rows, 0, re * lane_cos - im * lane_sin)
             store_left(2 * frame + 1, rows, 1, re * lane_sin + im * lane_cos)
-        product = dot(left_in[frame], fwd_right[...])
-        mid[2 * frame], mid[2 * frame + 1] = product[:side], product[side:]
+        for which in range(2):
+            mid[2 * frame + which] = dot(left_in[2 * frame + which], fwd_right[...])
 
     for frame in range(frames):
         for row in range(0, half, step):
@@ -262,8 +261,8 @@
                 store_left(2 * frame + which, top, 1, even_im + im)
                 store_left(2 * frame + which, low, 0, even_re - re)
                 store_left(2 * frame + which, low, 1, even_im - im)
-        product = dot(left_in[frame], inv_right[...])
-        mid[2 * frame], mid[2 * frame + 1] = product[:side], product[side:]
+        for which in range(2):
+            mid[2 * frame + which] = dot(left_in[2 * frame + which], inv_right[...])
 
     step = 8
     lanes = lax.broadcasted_iota(jnp.int32, (step, half), 1)
@@ -410,6 +409,7 @@
     near = shifted(near, "row", -1)
     far = shifted(far, "row", -1)
     right = shifted(right, "col", -1)
+    near, probe, ampl = lax.optimization_barrier((near, probe_field, measured))
     peak = pl.pallas_call(
         peak_kernel,
         out_shape=f32(2, 8, half),
@@ -417,8 +417,7 @@
         out_specs=VMEM,
         cost_estimate=cost(10**6, 2 * 10**6),
         compiler_params=PARAMS,
-    )(probe_field, measured)
-    near, peak = lax.optimization_barrier((near, peak))
+    )(probe, ampl)
     corner = shifted(near, "col", -1)
     places = positions.T
     prot, ampl = pl.pallas_call(
@@ -429,7 +428,7 @@
         scratch_shapes=[pltpu.VMEM((2, 2, 2 * side, half), jnp.float32)],
         cost_estimate=cost(3 * 10**9, 6 * 10**6),
         compiler_params=PARAMS,
-    )(places, probe_field, measured)
+    )(places, probe, ampl)
     depth = side // n_col
     g_tile, g_right, g_down, g_corner, sums = pl.pallas_call(
         frame_kernel,
@@ -446,7 +445,7 @@
             pltpu.VMEM((2, side, half), jnp.float32),
             pltpu.VMEM((2, margin, half), jnp.float32),
             pltpu.VMEM((frames, 2, side, side), jnp.float32),
-            pltpu.VMEM((frames, 2 * side, 3 * side), BF16),
+            pltpu.VMEM((2 * frames, side, 3 * side), BF16),
             pltpu.VMEM((2 * frames, 3 * side, side), BF16),
             pltpu.VMEM((2 * frames, side, side), jnp.float32),
             pltpu.VMEM((frames, 3, 2, side + margin, half), jnp.float32),

time: 72.2 us -> 76.1 us (1.054)
  local copies, waits for them, and re-layouts: 4.19 us -> 8.81 us
  waiting for transfers between devices: 23.1 us -> 26.3 us
  starting transfers between devices: 29.8 us -> 27.2 us
  Pallas kernels: 13.5 us -> 12.3 us
    unnamed x22 -> x40, local copies, waits for them, and re-layouts: 3.35 us -> 8.81 us
    ppermute x6, starting transfers between devices: 15.2 us -> 13 us  [shifted(): lax.ppermute(value, axis, [(source, source + steps) for source in range(i...]
    ppermute x6, waiting for transfers between devices: 2.8 us -> 4.59 us  [shifted(): lax.ppermute(value, axis, [(source, source + steps) for source in range(i...]
    all_to_all x1, waiting for transfers between devices: 8.07 us -> 9.22 us  [body(): part = jnp.sum(lax.all_to_all(sums, 'col', 0, 0), 0)]
    dynamic_slice x1, local copies, waits for them, and re-layouts: 0.84 us -> 0.01 us  [body(): lax.dynamic_slice_in_dim(probe_field, lax.axis_index('col') * depth, dept...]
    pallas_call x1, Pallas kernels: 0.85 us -> 0.05 us  [body(): pl.pallas_call(update_kernel, out_shape=f32(n_col, 2, depth, side), in_sp...]
  transfers between devices with their start and end apart: 12 -> 12, of which waited for: 5 -> 7; matrix products, arithmetic and copies ran while one was open for 1% -> 0% of each run, Pallas kernels for 5% -> 4%
where the time goes in v6:
time: 76.1 us; the launch traced here: 75.5 us
  starting transfers between devices  27.2 us (36%)
  waiting for transfers between devices  26.3 us (35%)
  Pallas kernels  12.3 us (16%)
  local copies, waits for them, and re-layouts  8.81 us (12%)
  between operations  0.89 us (1%)
    ppermute x6, starting transfers between devices, shifted(): lax.ppermute(value, axis, [(source, source + steps) for source in range(i...  13 us
    all_to_all x1, waiting for transfers between devices, body(): part = jnp.sum(lax.all_to_all(sums, 'col', 0, 0), 0)  9.22 us
    unnamed x40, local copies, waits for them, and re-layouts  8.81 us
    ppermute x1, waiting for transfers between devices, diagonal(): return lax.ppermute(value, ('row', 'col'), pairs)  8.44 us
    pallas_call x1, Pallas kernels, body(): pl.pallas_call(frame_kernel, out_shape=(f32(2, side, side), f32(2, wide,...  7.92 us
    ppermute x6, waiting for transfers between devices, shifted(): lax.ppermute(value, axis, [(source, source + steps) for source in range(i...  4.59 us
    all_to_all x1, starting transfers between devices, body(): part = jnp.sum(lax.all_to_all(sums, 'col', 0, 0), 0)  4.47 us
    ppermute x3, starting transfers between devices, row_terms(): lax.ppermute(value, 'row', [(row, row ^ step) for row in range(rows)])  4.39 us
  transfers between devices with their start and end apart: 12, of which 7 were waited for; matrix products, arithmetic and copies ran while one was open for 0% of the time, Pallas kernels for 4%

profile of v6, /device:TPU:20, one launch (start us, length us, event | category | flops | bytes accessed | tf_op | source)
XLA Modules:
  0.0 75.5 jit_solution(2192945267419222165)
XLA Ops:
  0.6 0.0 copy-start
  0.6 1.0 %copy-done = f32[2,256,256]{2,1,0:T(8,128)S(1)} copy-done((f32[2,256,256]{2,1,0:T(8,128)S(1)}, f32[2,256,256]{2,1,0:T(8,128)}, u32[]{:S(2)}) %copy-start) | copy-done | bytes 524312
  1.7 0.1 shard_map.113
  1.8 2.4 %collective-permute-start = (f32[2,200,128]{2,1,0:T(8,128)S(1)}, f32[2,200,128]{2,1,0:T(8,128)S(1)}, u32[]{:S(2)}, u32[]{:S(2)}) collective-permute-start(f32[2,200,128]{2,1,0:T(8,128)S(1)} %get-tuple-element.22), channel_id=1, source_target_pairs={{8,0},{16,8},{24,16},{9,1},{17,9},{25,17},{10,2},{18,10},{26,18},{... | collective-permute-start | bytes 614408 | tf_op jit(solution)/shard_map/ppermute | solution.py:21
  4.2 2.5 %collective-permute-start.1 = (f32[2,320,128]{2,1,0:T(8,128)S(1)}, f32[2,320,128]{2,1,0:T(8,128)S(1)}, u32[]{:S(2)}, u32[]{:S(2)}) collective-permute-start(f32[2,320,128]{2,1,0:T(8,128)S(1)} %get-tuple-element.25), channel_id=1, source_target_pairs={{1,0},{2,1},{3,2},{4,3},{5,4},{6,5},{7,6},{9,8},{10,9},{11,10},{12... | collective-permute-start | bytes 983048 | tf_op jit(solution)/shard_map/ppermute | solution.py:21
  6.7 2.4 %collective-permute-start.2 = (f32[2,160,128]{2,1,0:T(8,128)S(1)}, f32[2,160,128]{2,1,0:T(8,128)S(1)}, u32[]{:S(2)}, u32[]{:S(2)}) collective-permute-start(f32[2,160,128]{2,1,0:T(8,128)S(1)} %get-tuple-element.27), channel_id=1, source_target_pairs={{8,0},{16,8},{24,16},{9,1},{17,9},{25,17},{10,2},{18,10},{26,18},{... | collective-permute-start | bytes 491528 | tf_op jit(solution)/shard_map/ppermute | solution.py:21
  9.0 1.5 %collective-permute-done.near_ref = f32[2,200,128]{2,1,0:T(8,128)S(1)} collective-permute-done((f32[2,200,128]{2,1,0:T(8,128)S(1)}, f32[2,200,128]{2,1,0:T(8,128)S(1)}, u32[]{:S(2)}, u32[]{:S(2)}) %collective-permute-start) | collective-permute-done | bytes 204832 | tf_op jit(solution)/shard_map/ppermute | solution.py:21
  10.5 1.9 %collective-permute-start.3 = (f32[2,200,128]{2,1,0:T(8,128)S(1)}, f32[2,200,128]{2,1,0:T(8,128)S(1)}, u32[]{:S(2)}, u32[]{:S(2)}) collective-permute-start(f32[2,200,128]{2,1,0:T(8,128)S(1)} %collective-permute-done.near_ref), channel_id=1, source_target_pairs={{1,0},{2,1},{3,2},{4,3},{5,4},{6,5},{7,6},{9,8},{10,9},{11,10},{12... | collective-permute-start | bytes 614408 | tf_op jit(solution)/shard_map/ppermute | solution.py:21
  12.4 0.0 copy-start.2
  12.4 1.2 %copy-done.2 = f32[4,256,256]{2,1,0:T(8,128)S(1)} copy-done((f32[4,256,256]{2,1,0:T(8,128)S(1)}, f32[4,256,256]{2,1,0:T(8,128)}, u32[]{:S(2)}) %copy-start.2) | copy-done | bytes 1048600
  13.6 0.0 copy-start.4
  13.6 1.0 %copy-done.4 = f32[2,256,256]{2,1,0:T(8,128)S(1)} copy-done((f32[2,256,256]{2,1,0:T(8,128)S(1)}, f32[2,256,256]{2,1,0:T(8,128)}, u32[]{:S(2)}) %copy-start.4) | copy-done | bytes 524312
  14.7 0.0 copy-start.12
  14.7 0.7 copy-done.12
  15.4 0.0 copy-start.1
  15.4 0.0 copy-start.13
  15.4 0.0 copy-start.14
  15.4 0.0 copy-start.15
  15.4 0.0 copy-start.16
  15.4 0.0 copy-start.17
  15.4 0.0 copy-start.18
  15.4 0.0 copy-start.19
  15.4 2.8 %shard_map.115 = (f32[4,2,256,256]{3,2,1,0:T(8,128)S(1)}, f32[4,256,256]{2,1,0:T(8,128)S(1)}) custom-call(s32[2,4]{1,0:T(2,128)S(1)} %bitcast.1, f32[2,256,256]{2,1,0:T(8,128)S(1)} %copy-done.4, f32[4,256,256]{2,1,0:T(8,128)S(1)} %copy-done.2), custom_call_target="tpu_custom_call" | custom-call | flops 3000000000 | bytes 6000000 | tf_op jit(solution)/shard_map/pallas_call | solution.py:423
  18.3 0.0 collective-permute-done.2.far_ref
  18.3 0.0 collective-permute-done.1.right_ref
  18.3 0.0 collective-permute-done.3.corner_ref
  18.3 0.0 copy-done.1
  18.3 0.0 copy-done.13
  18.3 0.0 copy-done.14
  18.3 0.0 copy-done.15
  18.3 0.0 copy-done.16
  18.4 0.0 copy-done.17
  18.4 0.0 copy-done.18
  18.4 0.0 copy-done.19
  18.4 7.9 %shard_map.116 = (f32[2,256,256]{2,1,0:T(8,128)S(1)}, f32[2,320,128]{2,1,0:T(8,128)}, f32[2,320,128]{2,1,0:T(8,128)S(1)}, f32[2,200,128]{2,1,0:T(8,128)S(1)}, f32[8,3,32,256]{3,2,1,0:T(8,128)}) custom-call(s32[2,4]{1,0:T(2,128)S(1)} %bitcast.2, f32[2,256,256]{2,1,0:T(8,128)S(1)} %copy-done.1, f32[2,320,128]{2,1,0:T(8,128)S(1)} %collective-permute-done.1.right_ref, ...), custom_call_target="tpu_custom_call" | custom-call | flops 6000000000 | bytes 12000000 | tf_op jit(solution)/shard_map/pallas_call | solution.py:433
  26.3 0.0 copy-start.11
  26.3 0.7 copy-done.11
  27.0 4.5 %all-to-all-start = ((f32[8,3,32,256]{3,2,1,0:T(8,128)}), f32[8,3,32,256]{3,2,1,0:T(8,128)S(1)}, u32[]{:S(2)}, u32[]{:S(2)}) async-start(f32[8,3,32,256]{3,2,1,0:T(8,128)} %get-tuple-element.32), calls=%async_computation | async-start | bytes 1572864 | tf_op jit(solution)/shard_map/all_to_all | solution.py:461
  31.5 1.9 %collective-permute-start.4 = (f32[2,320,128]{2,1,0:T(8,128)S(1)}, f32[2,320,128]{2,1,0:T(8,128)S(1)}, u32[]{:S(2)}, u32[]{:S(2)}) collective-permute-start(f32[2,320,128]{2,1,0:T(8,128)S(1)} %get-tuple-element.33), channel_id=1, source_target_pairs={{0,8},{8,16},{16,24},{1,9},{9,17},{17,25},{2,10},{10,18},{18,26},{... | collective-permute-start | bytes 983048 | tf_op jit(solution)/shard_map/ppermute | solution.py:21
  33.4 9.2 %all-to-all-done = f32[8,3,32,256]{3,2,1,0:T(8,128)S(1)} async-done(((f32[8,3,32,256]{3,2,1,0:T(8,128)}), f32[8,3,32,256]{3,2,1,0:T(8,128)S(1)}, u32[]{:S(2)}, u32[]{:S(2)}) %all-to-all-start) | async-done | bytes 786464 | tf_op jit(solution)/shard_map/all_to_all | solution.py:461
  42.6 0.1 reduce_sum.9.refs_2_
  42.7 0.5 collective-permute-done.4.down_ref
  43.1 0.0 collective-permute-start.5
  43.1 1.8 %collective-permute-start.6 = (f32[3,32,256]{2,1,0:T(8,128)S(1)}, f32[3,32,256]{2,1,0:T(8,128)S(1)}, u32[]{:S(2)}, u32[]{:S(2)}) collective-permute-start(f32[3,32,256]{2,1,0:T(8,128)S(1)} %reduce_sum.9.refs_2_), channel_id=1, source_target_pairs={{0,24},{8,16},{16,8},{24,0},{1,25},{9,17},{17,9},{25,1},{2,26},{10... | collective-permute-start | bytes 294920 | tf_op jit(solution)/shard_map/ppermute | solution.py:37
  44.9 2.6 %collective-permute-start.7 = (f32[3,32,256]{2,1,0:T(8,128)S(1)}, f32[3,32,256]{2,1,0:T(8,128)S(1)}, u32[]{:S(2)}, u32[]{:S(2)}) collective-permute-start(f32[3,32,256]{2,1,0:T(8,128)S(1)} %reduce_sum.9.refs_2_), channel_id=1, source_target_pairs={{0,8},{8,0},{16,24},{24,16},{1,9},{9,1},{17,25},{25,17},{2,10},{10... | collective-permute-start | bytes 294920 | tf_op jit(solution)/shard_map/ppermute | solution.py:37
  47.5 0.0 copy-done.5
  47.5 1.9 %collective-permute-start.8 = (f32[2,320,128]{2,1,0:T(8,128)}, f32[2,320,128]{2,1,0:T(8,128)S(1)}, u32[]{:S(2)}, u32[]{:S(2)}) collective-permute-start(f32[2,320,128]{2,1,0:T(8,128)} %get-tuple-element.37), channel_id=1, source_target_pairs={{0,1},{1,2},{2,3},{3,4},{4,5},{5,6},{6,7},{8,9},{9,10},{10,11},{11... | collective-permute-start | bytes 983048 | tf_op jit(solution)/shard_map/ppermute | solution.py:21
  49.4 0.6 collective-permute-done.5.refs_0_
  50.1 3.4 %collective-permute-done.6.refs_1_ = f32[3,32,256]{2,1,0:T(8,128)S(1)} collective-permute-done((f32[3,32,256]{2,1,0:T(8,128)S(1)}, f32[3,32,256]{2,1,0:T(8,128)S(1)}, u32[]{:S(2)}, u32[]{:S(2)}) %collective-permute-start.6) | collective-permute-done | bytes 98336 | tf_op jit(solution)/shard_map/ppermute | solution.py:37
  53.5 0.0 collective-permute-done.7.refs_3_
  53.6 0.0 copy-start.6
  53.6 0.8 %copy-done.6 = f32[8,2,32,256]{3,2,1,0:T(8,128)} copy-done((f32[8,2,32,256]{3,2,1,0:T(8,128)}, f32[8,2,32,256]{3,2,1,0:T(8,128)S(1)}, u32[]{:S(2)}) %copy-start.6) | copy-done | bytes 524312
  54.4 2.7 %collective-permute-done.8.right_ref = f32[2,320,128]{2,1,0:T(8,128)S(1)} collective-permute-done((f32[2,320,128]{2,1,0:T(8,128)}, f32[2,320,128]{2,1,0:T(8,128)S(1)}, u32[]{:S(2)}, u32[]{:S(2)}) %collective-permute-start.8) | collective-permute-done | bytes 327712 | tf_op jit(solution)/shard_map/ppermute | solution.py:21
  57.0 0.7 copy-done.7
  57.7 3.4 %all-to-all-start.1 = ((f32[8,2,32,256]{3,2,1,0:T(8,128)}), f32[8,2,32,256]{3,2,1,0:T(8,128)S(1)}, u32[]{:S(2)}, u32[]{:S(2)}) async-start(f32[8,2,32,256]{3,2,1,0:T(8,128)} %copy-done.6), calls=%async_computation.1 | async-start | bytes 1048576 | tf_op jit(solution)/shard_map/all_to_all | solution.py:477
  61.2 1.9 %collective-permute-start.9 = (f32[2,200,128]{2,1,0:T(8,128)}, f32[2,200,128]{2,1,0:T(8,128)S(1)}, u32[]{:S(2)}, u32[]{:S(2)}) collective-permute-start(f32[2,200,128]{2,1,0:T(8,128)} %copy-done.11), channel_id=1, source_target_pairs={{0,9},{1,10},{2,11},{3,12},{4,13},{5,14},{6,15},{8,17},{9,18},{10,... | collective-permute-start | bytes 614408 | tf_op jit(solution)/shard_map/ppermute | solution.py:29
  63.1 0.0 copy-done.3
  63.1 0.2 shard_map.114.peak_ref
  63.3 8.4 %collective-permute-done.9.corner_ref = f32[2,200,128]{2,1,0:T(8,128)S(1)} collective-permute-done((f32[2,200,128]{2,1,0:T(8,128)}, f32[2,200,128]{2,1,0:T(8,128)S(1)}, u32[]{:S(2)}, u32[]{:S(2)}) %collective-permute-start.9) | collective-permute-done | bytes 204832 | tf_op jit(solution)/shard_map/ppermute | solution.py:29
  71.7 0.7 copy-done.9
  72.4 0.0 all-to-all-done.1.new_ref
  72.4 1.0 %copy-done.8 = f32[2,320,128]{2,1,0:T(8,128)S(1)} copy-done((f32[2,320,128]{2,1,0:T(8,128)S(1)}, f32[2,320,128]{2,1,0:T(8,128)}, u32[]{:S(2)}) %copy-start.8) | copy-done | bytes 327704
  73.4 0.9 %copy-done.10 = f32[2,200,128]{2,1,0:T(8,128)S(1)} copy-done((f32[2,200,128]{2,1,0:T(8,128)S(1)}, f32[2,200,128]{2,1,0:T(8,128)}, u32[]{:S(2)}) %copy-start.10) | copy-done | bytes 204824
  74.3 1.2 %shard_map.118 = (f32[2,256,256]{2,1,0:T(8,128)}, f32[2,256,256]{2,1,0:T(8,128)}) custom-call(f32[2,8,128]{2,1,0:T(8,128)S(1)} %shard_map.114.peak_ref, f32[2,256,256]{2,1,0:T(8,128)S(1)} %copy-done.1, f32[2,256,256]{2,1,0:T(8,128)S(1)} %get-tuple-element.30.grad_ref, f32[2,320,128]{2,1,0:T(8,128)S(1)} %copy-done.8, ...), custom_call_target="tpu_custom_call" | custom-call | flops 1000000 | bytes 4000000 | tf_op jit(solution)/shard_map/pallas_call | solution.py:478
  (8 shorter events, 0.1 us)
Async XLA Ops:
  0.6 1.0 %copy-start = (f32[2,256,256]{2,1,0:T(8,128)S(1)}, f32[2,256,256]{2,1,0:T(8,128)}, u32[]{:S(2)}) copy-start(f32[2,256,256]{2,1,0:T(8,128)} %tile_ref.5) | copy-start | bytes 1572868
  1.8 8.7 %collective-permute-start = (f32[2,200,128]{2,1,0:T(8,128)S(1)}, f32[2,200,128]{2,1,0:T(8,128)S(1)}, u32[]{:S(2)}, u32[]{:S(2)}) collective-permute-start(f32[2,200,128]{2,1,0:T(8,128)S(1)} %get-tuple-element.22), channel_id=1, source_target_pairs={{8,0},{16,8},{24,16},{9,1},{17,9},{25,17},{10,2},{18,10},{26,18},{... | collective-permute-start | bytes 614408 | tf_op jit(solution)/shard_map/ppermute | solution.py:21
  4.2 14.1 %collective-permute-start.1 = (f32[2,320,128]{2,1,0:T(8,128)S(1)}, f32[2,320,128]{2,1,0:T(8,128)S(1)}, u32[]{:S(2)}, u32[]{:S(2)}) collective-permute-start(f32[2,320,128]{2,1,0:T(8,128)S(1)} %get-tuple-element.25), channel_id=1, source_target_pairs={{1,0},{2,1},{3,2},{4,3},{5,4},{6,5},{7,6},{9,8},{10,9},{11,10},{12... | collective-permute-start | bytes 983048 | tf_op jit(solution)/shard_map/ppermute | solution.py:21
  6.7 11.6 %collective-permute-start.2 = (f32[2,160,128]{2,1,0:T(8,128)S(1)}, f32[2,160,128]{2,1,0:T(8,128)S(1)}, u32[]{:S(2)}, u32[]{:S(2)}) collective-permute-start(f32[2,160,128]{2,1,0:T(8,128)S(1)} %get-tuple-element.27), channel_id=1, source_target_pairs={{8,0},{16,8},{24,16},{9,1},{17,9},{25,17},{10,2},{18,10},{26,18},{... | collective-permute-start | bytes 491528 | tf_op jit(solution)/shard_map/ppermute | solution.py:21
  10.5 7.8 %collective-permute-start.3 = (f32[2,200,128]{2,1,0:T(8,128)S(1)}, f32[2,200,128]{2,1,0:T(8,128)S(1)}, u32[]{:S(2)}, u32[]{:S(2)}) collective-permute-start(f32[2,200,128]{2,1,0:T(8,128)S(1)} %collective-permute-done.near_ref), channel_id=1, source_target_pairs={{1,0},{2,1},{3,2},{4,3},{5,4},{6,5},{7,6},{9,8},{10,9},{11,10},{12... | collective-permute-start | bytes 614408 | tf_op jit(solution)/shard_map/ppermute | solution.py:21
  12.4 1.2 %copy-start.2 = (f32[4,256,256]{2,1,0:T(8,128)S(1)}, f32[4,256,256]{2,1,0:T(8,128)}, u32[]{:S(2)}) copy-start(f32[4,256,256]{2,1,0:T(8,128)} %meas_ref.1) | copy-start | bytes 3145732
  13.6 1.0 %copy-start.4 = (f32[2,256,256]{2,1,0:T(8,128)S(1)}, f32[2,256,256]{2,1,0:T(8,128)}, u32[]{:S(2)}) copy-start(f32[2,256,256]{2,1,0:T(8,128)} %probe_ref.1) | copy-start | bytes 1572868
  14.7 0.7 copy-start.12
  15.4 2.9 %copy-start.1 = (f32[2,256,256]{2,1,0:T(8,128)S(1)}, f32[2,256,256]{2,1,0:T(8,128)}, u32[]{:S(2)}) copy-start(f32[2,256,256]{2,1,0:T(8,128)} %tile_ref.5) | copy-start | bytes 1572868
  15.4 2.9 %copy-start.13 = (s32[4,2]{0,1:T(2,128)S(1)}, s32[4,2]{0,1:T(2,128)}, u32[]{:S(2)}) copy-start(s32[4,2]{0,1:T(2,128)} %param.13) | copy-start | bytes 100
  15.4 3.0 %copy-start.14 = (bf16[768,256]{1,0:T(8,128)(2,1)S(1)}, bf16[768,256]{1,0:T(8,128)(2,1)}, u32[]{:S(2)}) copy-start(bf16[768,256]{1,0:T(8,128)(2,1)} %constant.24.clone.fwd_right) | copy-start | bytes 1179652
  15.4 3.0 %copy-start.15 = (bf16[256,768]{1,0:T(8,128)(2,1)S(1)}, bf16[256,768]{1,0:T(8,128)(2,1)}, u32[]{:S(2)}) copy-start(bf16[256,768]{1,0:T(8,128)(2,1)} %constant.25.clone.fwd_left) | copy-start | bytes 1179652
  15.4 3.0 %copy-start.16 = (bf16[768,256]{1,0:T(8,128)(2,1)S(1)}, bf16[768,256]{1,0:T(8,128)(2,1)}, u32[]{:S(2)}) copy-start(bf16[768,256]{1,0:T(8,128)(2,1)} %constant.26.clone.inv_right) | copy-start | bytes 1179652
  15.4 3.0 %copy-start.17 = (bf16[256,768]{1,0:T(8,128)(2,1)S(1)}, bf16[256,768]{1,0:T(8,128)(2,1)}, u32[]{:S(2)}) copy-start(bf16[256,768]{1,0:T(8,128)(2,1)} %constant.27.clone.inv_left) | copy-start | bytes 1179652
  15.4 3.0 %copy-start.18 = (f32[2,128,128]{2,1,0:T(8,128)S(1)}, f32[2,128,128]{2,1,0:T(8,128)}, u32[]{:S(2)}) copy-start(f32[2,128,128]{2,1,0:T(8,128)} %constant.29.clone.row_ref) | copy-start | bytes 393220
  15.4 3.0 %copy-start.19 = (f32[2,8,128]{2,1,0:T(8,128)S(1)}, f32[2,8,128]{2,1,0:T(8,128)}, u32[]{:S(2)}) copy-start(f32[2,8,128]{2,1,0:T(8,128)} %constant.28.clone.lane_ref) | copy-start | bytes 24580
  26.3 0.7 copy-start.11
  27.0 20.5 %copy-start.5 = (f32[2,256,256]{2,1,0:T(8,128)S(1)}, f32[2,256,256]{2,1,0:T(8,128)}, u32[]{:S(2)}) copy-start(f32[2,256,256]{2,1,0:T(8,128)} %probe_ref.1) | copy-start | bytes 1572868
  27.0 15.6 %all-to-all-start = ((f32[8,3,32,256]{3,2,1,0:T(8,128)}), f32[8,3,32,256]{3,2,1,0:T(8,128)S(1)}, u32[]{:S(2)}, u32[]{:S(2)}) async-start(f32[8,3,32,256]{3,2,1,0:T(8,128)} %get-tuple-element.32), calls=%async_computation | async-start | bytes 1572864 | tf_op jit(solution)/shard_map/all_to_all | solution.py:461
  31.5 11.6 %collective-permute-start.4 = (f32[2,320,128]{2,1,0:T(8,128)S(1)}, f32[2,320,128]{2,1,0:T(8,128)S(1)}, u32[]{:S(2)}, u32[]{:S(2)}) collective-permute-start(f32[2,320,128]{2,1,0:T(8,128)S(1)} %get-tuple-element.33), channel_id=1, source_target_pairs={{0,8},{8,16},{16,24},{1,9},{9,17},{17,25},{2,10},{10,18},{18,26},{... | collective-permute-start | bytes 983048 | tf_op jit(solution)/shard_map/ppermute | solution.py:21
  43.1 6.9 %collective-permute-start.5 = (f32[3,32,256]{2,1,0:T(8,128)S(1)}, f32[3,32,256]{2,1,0:T(8,128)S(1)}, u32[]{:S(2)}, u32[]{:S(2)}) collective-permute-start(f32[3,32,256]{2,1,0:T(8,128)S(1)} %reduce_sum.9.refs_2_), channel_id=1, source_target_pairs={{0,16},{8,24},{16,0},{24,8},{1,17},{9,25},{17,1},{25,9},{2,18},{10... | collective-permute-start | bytes 294920 | tf_op jit(solution)/shard_map/ppermute | solution.py:37
  43.1 10.4 %collective-permute-start.6 = (f32[3,32,256]{2,1,0:T(8,128)S(1)}, f32[3,32,256]{2,1,0:T(8,128)S(1)}, u32[]{:S(2)}, u32[]{:S(2)}) collective-permute-start(f32[3,32,256]{2,1,0:T(8,128)S(1)} %reduce_sum.9.refs_2_), channel_id=1, source_target_pairs={{0,24},{8,16},{16,8},{24,0},{1,25},{9,17},{17,9},{25,1},{2,26},{10... | collective-permute-start | bytes 294920 | tf_op jit(solution)/shard_map/ppermute | solution.py:37
  44.9 8.6 %collective-permute-start.7 = (f32[3,32,256]{2,1,0:T(8,128)S(1)}, f32[3,32,256]{2,1,0:T(8,128)S(1)}, u32[]{:S(2)}, u32[]{:S(2)}) collective-permute-start(f32[3,32,256]{2,1,0:T(8,128)S(1)} %reduce_sum.9.refs_2_), channel_id=1, source_target_pairs={{0,8},{8,0},{16,24},{24,16},{1,9},{9,1},{17,25},{25,17},{2,10},{10... | collective-permute-start | bytes 294920 | tf_op jit(solution)/shard_map/ppermute | solution.py:37
  47.5 9.5 %collective-permute-start.8 = (f32[2,320,128]{2,1,0:T(8,128)}, f32[2,320,128]{2,1,0:T(8,128)S(1)}, u32[]{:S(2)}, u32[]{:S(2)}) collective-permute-start(f32[2,320,128]{2,1,0:T(8,128)} %get-tuple-element.37), channel_id=1, source_target_pairs={{0,1},{1,2},{2,3},{3,4},{4,5},{5,6},{6,7},{8,9},{9,10},{10,11},{11... | collective-permute-start | bytes 983048 | tf_op jit(solution)/shard_map/ppermute | solution.py:21
  50.1 13.1 %copy-start.3 = (f32[4,256,256]{2,1,0:T(8,128)S(1)}, f32[4,256,256]{2,1,0:T(8,128)}, u32[]{:S(2)}) copy-start(f32[4,256,256]{2,1,0:T(8,128)} %meas_ref.1) | copy-start | bytes 3145732
  53.6 0.8 %copy-start.6 = (f32[8,2,32,256]{3,2,1,0:T(8,128)}, f32[8,2,32,256]{3,2,1,0:T(8,128)S(1)}, u32[]{:S(2)}) copy-start(f32[8,2,32,256]{3,2,1,0:T(8,128)S(1)} %shard_map.117) | copy-start | bytes 1572868
  57.0 0.7 copy-start.7
  57.7 14.7 %all-to-all-start.1 = ((f32[8,2,32,256]{3,2,1,0:T(8,128)}), f32[8,2,32,256]{3,2,1,0:T(8,128)S(1)}, u32[]{:S(2)}, u32[]{:S(2)}) async-start(f32[8,2,32,256]{3,2,1,0:T(8,128)} %copy-done.6), calls=%async_computation.1 | async-start | bytes 1048576 | tf_op jit(solution)/shard_map/all_to_all | solution.py:477
  61.2 10.5 %collective-permute-start.9 = (f32[2,200,128]{2,1,0:T(8,128)}, f32[2,200,128]{2,1,0:T(8,128)S(1)}, u32[]{:S(2)}, u32[]{:S(2)}) collective-permute-start(f32[2,200,128]{2,1,0:T(8,128)} %copy-done.11), channel_id=1, source_target_pairs={{0,9},{1,10},{2,11},{3,12},{4,13},{5,14},{6,15},{8,17},{9,18},{10,... | collective-permute-start | bytes 614408 | tf_op jit(solution)/shard_map/ppermute | solution.py:29
  71.7 0.7 copy-start.9
  72.4 1.0 %copy-start.8 = (f32[2,320,128]{2,1,0:T(8,128)S(1)}, f32[2,320,128]{2,1,0:T(8,128)}, u32[]{:S(2)}) copy-start(f32[2,320,128]{2,1,0:T(8,128)} %copy-done.7) | copy-start | bytes 983044
  73.4 0.9 %copy-start.10 = (f32[2,200,128]{2,1,0:T(8,128)S(1)}, f32[2,200,128]{2,1,0:T(8,128)}, u32[]{:S(2)}) copy-start(f32[2,200,128]{2,1,0:T(8,128)} %copy-done.9) | copy-start | bytes 614404

commit v7 on v6

--- a/solution.py
+++ b/solution.py
@@ -101,11 +101,10 @@
             near_ref[:, margin + packed : margin + packed + 8, lane : lane + extra] = piece
 
 
-def peak_kernel(probe_ref, meas_ref, out_ref):
+def peak_kernel(probe_ref, out_ref):
     re, im = probe_ref[0], probe_ref[1]
     top = jnp.max(re * re + im * im, axis=(0, 1), keepdims=True)
-    out_ref[0] = jnp.broadcast_to(top, out_ref.shape[1:])
-    out_ref[1] = meas_ref[0, 0:8, 0 : out_ref.shape[2]]
+    out_ref[...] = jnp.broadcast_to(top, out_ref.shape)
 
 
 def turned(load, steps, half, lanes):
@@ -370,7 +369,7 @@
     depth = new_ref.shape[2]
     for block in range(new_ref.shape[0]):
         probe_ref[:, block * depth : (block + 1) * depth, :] = new_ref[block]
-    largest = peak_ref[0]
+    largest = peak_ref[...]
     step = 8
     for row, packed, lane in pack_extra(side, extra, half):
         place = slice(row, row + step)
@@ -412,12 +411,12 @@
     near, probe, ampl = lax.optimization_barrier((near, probe_field, measured))
     peak = pl.pallas_call(
         peak_kernel,
-        out_shape=f32(2, 8, half),
-        in_specs=[VMEM, VMEM],
+        out_shape=f32(8, half),
+        in_specs=[VMEM],
         out_specs=VMEM,
         cost_estimate=cost(10**6, 2 * 10**6),
         compiler_params=PARAMS,
-    )(probe, ampl)
+    )(probe)
     corner = shifted(near, "col", -1)
     places = positions.T
     prot, ampl = pl.pallas_call(
@@ -429,6 +428,7 @@
         cost_estimate=cost(3 * 10**9, 6 * 10**6),
         compiler_params=PARAMS,
     )(places, probe, ampl)
+    prot, peak = lax.optimization_barrier((prot, peak))
     depth = side // n_col
     g_tile, g_right, g_down, g_corner, sums = pl.pallas_call(
         frame_kernel,

time: 76.1 us -> 72.6 us (0.954)
  local copies, waits for them, and re-layouts: 8.81 us -> 4.85 us
  Pallas kernels: 12.3 us -> 13.2 us
    unnamed x40 -> x22, local copies, waits for them, and re-layouts: 8.81 us -> 4.01 us
    dynamic_slice x1, local copies, waits for them, and re-layouts: 0.01 us -> 0.84 us  [body(): lax.dynamic_slice_in_dim(probe_field, lax.axis_index('col') * depth, dept...]
    ppermute x3, waiting for transfers between devices: 4.06 us -> 3.23 us  [row_terms(): lax.ppermute(value, 'row', [(row, row ^ step) for row in range(rows)])]
    pallas_call x1, Pallas kernels: 0.05 us -> 0.85 us  [body(): pl.pallas_call(update_kernel, out_shape=f32(n_col, 2, depth, side), in_sp...]
  transfers between devices with their start and end apart: 12 -> 12, of which waited for: 7 -> 6; matrix products, arithmetic and copies ran while one was open for 0% -> 1% of each run, Pallas kernels for 4% -> 5%
where the time goes in v7:
time: 72.6 us; the launch traced here: 72 us
  starting transfers between devices  27 us (37%)
  waiting for transfers between devices  26.1 us (36%)
  Pallas kernels  13.2 us (18%)
  local copies, waits for them, and re-layouts  4.85 us (7%)
  between operations  0.86 us (1%)
    ppermute x6, starting transfers between devices, shifted(): lax.ppermute(value, axis, [(source, source + steps) for source in range(i...  12.9 us
    all_to_all x1, waiting for transfers between devices, body(): part = jnp.sum(lax.all_to_all(sums, 'col', 0, 0), 0)  9.22 us
    ppermute x1, waiting for transfers between devices, diagonal(): return lax.ppermute(value, ('row', 'col'), pairs)  8.4 us
    pallas_call x1, Pallas kernels, body(): pl.pallas_call(frame_kernel, out_shape=(f32(2, side, side), f32(2, wide,...  8.04 us
    ppermute x6, waiting for transfers between devices, shifted(): lax.ppermute(value, axis, [(source, source + steps) for source in range(i...  5.21 us
    ppermute x3, starting transfers between devices, row_terms(): lax.ppermute(value, 'row', [(row, row ^ step) for row in range(rows)])  4.39 us
    all_to_all x1, starting transfers between devices, body(): part = jnp.sum(lax.all_to_all(sums, 'col', 0, 0), 0)  4.33 us
    unnamed x22, local copies, waits for them, and re-layouts  4.01 us
  transfers between devices with their start and end apart: 12, of which 6 were waited for; matrix products, arithmetic and copies ran while one was open for 1% of the time, Pallas kernels for 5%

profile of v7, /device:TPU:20, one launch (start us, length us, event | category | flops | bytes accessed | tf_op | source)
XLA Modules:
  0.0 72.0 jit_solution(15575399344507917626)
XLA Ops:
  0.6 0.0 copy-start
  0.6 1.0 %copy-done = f32[2,256,256]{2,1,0:T(8,128)S(1)} copy-done((f32[2,256,256]{2,1,0:T(8,128)S(1)}, f32[2,256,256]{2,1,0:T(8,128)}, u32[]{:S(2)}) %copy-start) | copy-done | bytes 524312
  1.7 0.1 shard_map.113
  1.8 2.4 %collective-permute-start = (f32[2,200,128]{2,1,0:T(8,128)S(1)}, f32[2,200,128]{2,1,0:T(8,128)S(1)}, u32[]{:S(2)}, u32[]{:S(2)}) collective-permute-start(f32[2,200,128]{2,1,0:T(8,128)S(1)} %get-tuple-element.24), channel_id=1, source_target_pairs={{8,0},{16,8},{24,16},{9,1},{17,9},{25,17},{10,2},{18,10},{26,18},{... | collective-permute-start | bytes 614408 | tf_op jit(solution)/shard_map/ppermute | solution.py:21
  4.2 2.5 %collective-permute-start.1 = (f32[2,320,128]{2,1,0:T(8,128)S(1)}, f32[2,320,128]{2,1,0:T(8,128)S(1)}, u32[]{:S(2)}, u32[]{:S(2)}) collective-permute-start(f32[2,320,128]{2,1,0:T(8,128)S(1)} %get-tuple-element.29), channel_id=1, source_target_pairs={{1,0},{2,1},{3,2},{4,3},{5,4},{6,5},{7,6},{9,8},{10,9},{11,10},{12... | collective-permute-start | bytes 983048 | tf_op jit(solution)/shard_map/ppermute | solution.py:21
  6.7 2.4 %collective-permute-start.2 = (f32[2,160,128]{2,1,0:T(8,128)S(1)}, f32[2,160,128]{2,1,0:T(8,128)S(1)}, u32[]{:S(2)}, u32[]{:S(2)}) collective-permute-start(f32[2,160,128]{2,1,0:T(8,128)S(1)} %get-tuple-element.31), channel_id=1, source_target_pairs={{8,0},{16,8},{24,16},{9,1},{17,9},{25,17},{10,2},{18,10},{26,18},{... | collective-permute-start | bytes 491528 | tf_op jit(solution)/shard_map/ppermute | solution.py:21
  9.0 1.5 %collective-permute-done.near_ref = f32[2,200,128]{2,1,0:T(8,128)S(1)} collective-permute-done((f32[2,200,128]{2,1,0:T(8,128)S(1)}, f32[2,200,128]{2,1,0:T(8,128)S(1)}, u32[]{:S(2)}, u32[]{:S(2)}) %collective-permute-start) | collective-permute-done | bytes 204832 | tf_op jit(solution)/shard_map/ppermute | solution.py:21
  10.5 1.9 %collective-permute-start.3 = (f32[2,200,128]{2,1,0:T(8,128)S(1)}, f32[2,200,128]{2,1,0:T(8,128)S(1)}, u32[]{:S(2)}, u32[]{:S(2)}) collective-permute-start(f32[2,200,128]{2,1,0:T(8,128)S(1)} %collective-permute-done.near_ref), channel_id=1, source_target_pairs={{1,0},{2,1},{3,2},{4,3},{5,4},{6,5},{7,6},{9,8},{10,9},{11,10},{12... | collective-permute-start | bytes 614408 | tf_op jit(solution)/shard_map/ppermute | solution.py:21
  12.4 0.0 copy-start.2
  12.4 1.0 %copy-done.2 = f32[2,256,256]{2,1,0:T(8,128)S(1)} copy-done((f32[2,256,256]{2,1,0:T(8,128)S(1)}, f32[2,256,256]{2,1,0:T(8,128)}, u32[]{:S(2)}) %copy-start.2) | copy-done | bytes 524312
  13.5 0.2 shard_map.115.peak_ref
  13.6 0.0 copy-start.3
  13.6 1.2 %copy-done.3 = f32[4,256,256]{2,1,0:T(8,128)S(1)} copy-done((f32[4,256,256]{2,1,0:T(8,128)S(1)}, f32[4,256,256]{2,1,0:T(8,128)}, u32[]{:S(2)}) %copy-start.3) | copy-done | bytes 1048600
  14.9 0.0 copy-start.4
  14.9 0.7 copy-done.4
  15.5 0.0 copy-start.1
  15.5 0.0 copy-start.5
  15.5 0.0 copy-start.6
  15.5 0.0 copy-start.7
  15.5 0.0 copy-start.8
  15.6 0.0 copy-start.9
  15.6 0.0 copy-start.10
  15.6 2.8 %shard_map.114 = (f32[4,2,256,256]{3,2,1,0:T(8,128)S(1)}, f32[4,256,256]{2,1,0:T(8,128)S(1)}) custom-call(s32[2,4]{1,0:T(2,128)S(1)} %bitcast.1, f32[2,256,256]{2,1,0:T(8,128)S(1)} %copy-done.2, f32[4,256,256]{2,1,0:T(8,128)S(1)} %copy-done.3), custom_call_target="tpu_custom_call" | custom-call | flops 3000000000 | bytes 6000000 | tf_op jit(solution)/shard_map/pallas_call | solution.py:422
  18.4 0.0 collective-permute-done.2.far_ref
  18.4 0.0 collective-permute-done.1.right_ref
  18.4 0.0 collective-permute-done.3.corner_ref
  18.5 0.0 copy-done.1
  18.5 0.0 copy-done.5
  18.5 0.0 copy-done.6
  18.5 0.0 copy-done.7
  18.5 0.0 copy-done.8
  18.5 0.0 copy-done.9
  18.5 0.0 copy-done.10
  18.5 8.0 %shard_map.116 = (f32[2,256,256]{2,1,0:T(8,128)S(1)}, f32[2,320,128]{2,1,0:T(8,128)S(1)}, f32[2,320,128]{2,1,0:T(8,128)S(1)}, f32[2,200,128]{2,1,0:T(8,128)S(1)}, f32[8,3,32,256]{3,2,1,0:T(8,128)}) custom-call(s32[2,4]{1,0:T(2,128)S(1)} %bitcast.2, f32[2,256,256]{2,1,0:T(8,128)S(1)} %copy-done.1, f32[2,320,128]{2,1,0:T(8,128)S(1)} %collective-permute-done.1.right_ref, ...), custom_call_target="tpu_custom_call" | custom-call | flops 6000000000 | bytes 12000000 | tf_op jit(solution)/shard_map/pallas_call | solution.py:433
  26.6 4.3 %all-to-all-start = ((f32[8,3,32,256]{3,2,1,0:T(8,128)}), f32[8,3,32,256]{3,2,1,0:T(8,128)S(1)}, u32[]{:S(2)}, u32[]{:S(2)}) async-start(f32[8,3,32,256]{3,2,1,0:T(8,128)} %get-tuple-element.36), calls=%async_computation | async-start | bytes 1572864 | tf_op jit(solution)/shard_map/all_to_all | solution.py:461
  30.9 1.9 %collective-permute-start.4 = (f32[2,320,128]{2,1,0:T(8,128)S(1)}, f32[2,320,128]{2,1,0:T(8,128)S(1)}, u32[]{:S(2)}, u32[]{:S(2)}) collective-permute-start(f32[2,320,128]{2,1,0:T(8,128)S(1)} %get-tuple-element.37), channel_id=1, source_target_pairs={{0,8},{8,16},{16,24},{1,9},{9,17},{17,25},{2,10},{10,18},{18,26},{... | collective-permute-start | bytes 983048 | tf_op jit(solution)/shard_map/ppermute | solution.py:21
  32.8 9.2 %all-to-all-done = f32[8,3,32,256]{3,2,1,0:T(8,128)S(1)} async-done(((f32[8,3,32,256]{3,2,1,0:T(8,128)}), f32[8,3,32,256]{3,2,1,0:T(8,128)S(1)}, u32[]{:S(2)}, u32[]{:S(2)}) %all-to-all-start) | async-done | bytes 786464 | tf_op jit(solution)/shard_map/all_to_all | solution.py:461
  42.0 0.1 reduce_sum.9.refs_2_
  42.1 0.5 collective-permute-done.4.down_ref
  42.5 0.0 collective-permute-start.5
  42.5 1.8 %collective-permute-start.6 = (f32[3,32,256]{2,1,0:T(8,128)S(1)}, f32[3,32,256]{2,1,0:T(8,128)S(1)}, u32[]{:S(2)}, u32[]{:S(2)}) collective-permute-start(f32[3,32,256]{2,1,0:T(8,128)S(1)} %reduce_sum.9.refs_2_), channel_id=1, source_target_pairs={{0,24},{8,16},{16,8},{24,0},{1,25},{9,17},{17,9},{25,1},{2,26},{10... | collective-permute-start | bytes 294920 | tf_op jit(solution)/shard_map/ppermute | solution.py:37
  44.3 2.6 %collective-permute-start.7 = (f32[3,32,256]{2,1,0:T(8,128)S(1)}, f32[3,32,256]{2,1,0:T(8,128)S(1)}, u32[]{:S(2)}, u32[]{:S(2)}) collective-permute-start(f32[3,32,256]{2,1,0:T(8,128)S(1)} %reduce_sum.9.refs_2_), channel_id=1, source_target_pairs={{0,8},{8,0},{16,24},{24,16},{1,9},{9,1},{17,25},{25,17},{2,10},{10... | collective-permute-start | bytes 294920 | tf_op jit(solution)/shard_map/ppermute | solution.py:37
  46.9 0.8 %constant_dynamic-slice_fusion.old_ref = f32[2,32,256]{2,1,0:T(8,128)S(1)} fusion(f32[2,256,256]{2,1,0:T(8,128)} %probe_ref.1, s32[]{:T(128)S(6)} %select_n.3), kind=kLoop, calls=%fused_computation | loop fusion | bytes 131076 | tf_op jit(solution)/shard_map/dynamic_slice | solution.py:463
  47.8 1.9 %collective-permute-start.8 = (f32[2,320,128]{2,1,0:T(8,128)S(1)}, f32[2,320,128]{2,1,0:T(8,128)S(1)}, u32[]{:S(2)}, u32[]{:S(2)}) collective-permute-start(f32[2,320,128]{2,1,0:T(8,128)S(1)} %get-tuple-element.41), channel_id=1, source_target_pairs={{0,1},{1,2},{2,3},{3,4},{4,5},{5,6},{6,7},{8,9},{9,10},{10,11},{11... | collective-permute-start | bytes 983048 | tf_op jit(solution)/shard_map/ppermute | solution.py:21
  49.7 0.0 collective-permute-done.5.refs_0_
  49.7 3.2 %collective-permute-done.6.refs_1_ = f32[3,32,256]{2,1,0:T(8,128)S(1)} collective-permute-done((f32[3,32,256]{2,1,0:T(8,128)S(1)}, f32[3,32,256]{2,1,0:T(8,128)S(1)}, u32[]{:S(2)}, u32[]{:S(2)}) %collective-permute-start.6) | collective-permute-done | bytes 98336 | tf_op jit(solution)/shard_map/ppermute | solution.py:37
  52.9 0.0 collective-permute-done.7.refs_3_
  52.9 0.8 %shard_map.117 = f32[8,2,32,256]{3,2,1,0:T(8,128)} custom-call(f32[2,32,256]{2,1,0:T(8,128)S(1)} %constant_dynamic-slice_fusion.old_ref, f32[3,32,256]{2,1,0:T(8,128)S(1)} %collective-permute-done.5.refs_0_, f32[3,32,256]{2,1,0:T(8,128)S(1)} %collective-permute-done.6.refs_1_, f32[3,32,256]{2,1,0:T(8,128)S(1)} %reduce_sum.9.refs_2_, ...), custom_call_target="tpu_custom_call" | custom-call | flops 10000000000 | bytes 1000000 | tf_op jit(solution)/shard_map/pallas_call | solution.py:468
  53.8 3.3 %collective-permute-done.8.right_ref = f32[2,320,128]{2,1,0:T(8,128)S(1)} collective-permute-done((f32[2,320,128]{2,1,0:T(8,128)S(1)}, f32[2,320,128]{2,1,0:T(8,128)S(1)}, u32[]{:S(2)}, u32[]{:S(2)}) %collective-permute-start.8) | collective-permute-done | bytes 327712 | tf_op jit(solution)/shard_map/ppermute | solution.py:21
  57.1 3.4 %all-to-all-start.1 = ((f32[8,2,32,256]{3,2,1,0:T(8,128)}), f32[8,2,32,256]{3,2,1,0:T(8,128)S(1)}, u32[]{:S(2)}, u32[]{:S(2)}) async-start(f32[8,2,32,256]{3,2,1,0:T(8,128)} %shard_map.117), calls=%async_computation.1 | async-start | bytes 1048576 | tf_op jit(solution)/shard_map/all_to_all | solution.py:477
  60.5 1.9 %collective-permute-start.9 = (f32[2,200,128]{2,1,0:T(8,128)S(1)}, f32[2,200,128]{2,1,0:T(8,128)S(1)}, u32[]{:S(2)}, u32[]{:S(2)}) collective-permute-start(f32[2,200,128]{2,1,0:T(8,128)S(1)} %get-tuple-element.44), channel_id=1, source_target_pairs={{0,9},{1,10},{2,11},{3,12},{4,13},{5,14},{6,15},{8,17},{9,18},{10,... | collective-permute-start | bytes 614408 | tf_op jit(solution)/shard_map/ppermute | solution.py:29
  62.4 8.4 %collective-permute-done.9.corner_ref = f32[2,200,128]{2,1,0:T(8,128)S(1)} collective-permute-done((f32[2,200,128]{2,1,0:T(8,128)S(1)}, f32[2,200,128]{2,1,0:T(8,128)S(1)}, u32[]{:S(2)}, u32[]{:S(2)}) %collective-permute-start.9) | collective-permute-done | bytes 204832 | tf_op jit(solution)/shard_map/ppermute | solution.py:29
  70.8 0.0 all-to-all-done.1.new_ref
  70.8 1.2 %shard_map.118 = (f32[2,256,256]{2,1,0:T(8,128)}, f32[2,256,256]{2,1,0:T(8,128)}) custom-call(f32[8,128]{1,0:T(8,128)S(1)} %shard_map.115.peak_ref, f32[2,256,256]{2,1,0:T(8,128)S(1)} %copy-done.1, f32[2,256,256]{2,1,0:T(8,128)S(1)} %get-tuple-element.34.grad_ref, f32[2,320,128]{2,1,0:T(8,128)S(1)} %collective-permute-done.8.right_ref, ...), custom_call_target="tpu_custom_call" | custom-call | flops 1000000 | bytes 4000000 | tf_op jit(solution)/shard_map/pallas_call | solution.py:478
Async XLA Ops:
  0.6 1.0 %copy-start = (f32[2,256,256]{2,1,0:T(8,128)S(1)}, f32[2,256,256]{2,1,0:T(8,128)}, u32[]{:S(2)}) copy-start(f32[2,256,256]{2,1,0:T(8,128)} %tile_ref.5) | copy-start | bytes 1572868
  1.8 8.7 %collective-permute-start = (f32[2,200,128]{2,1,0:T(8,128)S(1)}, f32[2,200,128]{2,1,0:T(8,128)S(1)}, u32[]{:S(2)}, u32[]{:S(2)}) collective-permute-start(f32[2,200,128]{2,1,0:T(8,128)S(1)} %get-tuple-element.24), channel_id=1, source_target_pairs={{8,0},{16,8},{24,16},{9,1},{17,9},{25,17},{10,2},{18,10},{26,18},{... | collective-permute-start | bytes 614408 | tf_op jit(solution)/shard_map/ppermute | solution.py:21
  4.2 14.3 %collective-permute-start.1 = (f32[2,320,128]{2,1,0:T(8,128)S(1)}, f32[2,320,128]{2,1,0:T(8,128)S(1)}, u32[]{:S(2)}, u32[]{:S(2)}) collective-permute-start(f32[2,320,128]{2,1,0:T(8,128)S(1)} %get-tuple-element.29), channel_id=1, source_target_pairs={{1,0},{2,1},{3,2},{4,3},{5,4},{6,5},{7,6},{9,8},{10,9},{11,10},{12... | collective-permute-start | bytes 983048 | tf_op jit(solution)/shard_map/ppermute | solution.py:21
  6.7 11.8 %collective-permute-start.2 = (f32[2,160,128]{2,1,0:T(8,128)S(1)}, f32[2,160,128]{2,1,0:T(8,128)S(1)}, u32[]{:S(2)}, u32[]{:S(2)}) collective-permute-start(f32[2,160,128]{2,1,0:T(8,128)S(1)} %get-tuple-element.31), channel_id=1, source_target_pairs={{8,0},{16,8},{24,16},{9,1},{17,9},{25,17},{10,2},{18,10},{26,18},{... | collective-permute-start | bytes 491528 | tf_op jit(solution)/shard_map/ppermute | solution.py:21
  10.5 7.9 %collective-permute-start.3 = (f32[2,200,128]{2,1,0:T(8,128)S(1)}, f32[2,200,128]{2,1,0:T(8,128)S(1)}, u32[]{:S(2)}, u32[]{:S(2)}) collective-permute-start(f32[2,200,128]{2,1,0:T(8,128)S(1)} %collective-permute-done.near_ref), channel_id=1, source_target_pairs={{1,0},{2,1},{3,2},{4,3},{5,4},{6,5},{7,6},{9,8},{10,9},{11,10},{12... | collective-permute-start | bytes 614408 | tf_op jit(solution)/shard_map/ppermute | solution.py:21
  12.4 1.0 %copy-start.2 = (f32[2,256,256]{2,1,0:T(8,128)S(1)}, f32[2,256,256]{2,1,0:T(8,128)}, u32[]{:S(2)}) copy-start(f32[2,256,256]{2,1,0:T(8,128)} %probe_ref.1) | copy-start | bytes 1572868
  13.6 1.2 %copy-start.3 = (f32[4,256,256]{2,1,0:T(8,128)S(1)}, f32[4,256,256]{2,1,0:T(8,128)}, u32[]{:S(2)}) copy-start(f32[4,256,256]{2,1,0:T(8,128)} %meas_ref) | copy-start | bytes 3145732
  14.9 0.7 copy-start.4
  15.5 2.9 %copy-start.1 = (f32[2,256,256]{2,1,0:T(8,128)S(1)}, f32[2,256,256]{2,1,0:T(8,128)}, u32[]{:S(2)}) copy-start(f32[2,256,256]{2,1,0:T(8,128)} %tile_ref.5) | copy-start | bytes 1572868
  15.5 2.9 %copy-start.5 = (bf16[768,256]{1,0:T(8,128)(2,1)S(1)}, bf16[768,256]{1,0:T(8,128)(2,1)}, u32[]{:S(2)}) copy-start(bf16[768,256]{1,0:T(8,128)(2,1)} %constant.24.clone.fwd_right) | copy-start | bytes 1179652
  15.5 2.9 %copy-start.6 = (bf16[256,768]{1,0:T(8,128)(2,1)S(1)}, bf16[256,768]{1,0:T(8,128)(2,1)}, u32[]{:S(2)}) copy-start(bf16[256,768]{1,0:T(8,128)(2,1)} %constant.25.clone.fwd_left) | copy-start | bytes 1179652
  15.5 2.9 %copy-start.7 = (bf16[768,256]{1,0:T(8,128)(2,1)S(1)}, bf16[768,256]{1,0:T(8,128)(2,1)}, u32[]{:S(2)}) copy-start(bf16[768,256]{1,0:T(8,128)(2,1)} %constant.26.clone.inv_right) | copy-start | bytes 1179652
  15.5 2.9 %copy-start.8 = (bf16[256,768]{1,0:T(8,128)(2,1)S(1)}, bf16[256,768]{1,0:T(8,128)(2,1)}, u32[]{:S(2)}) copy-start(bf16[256,768]{1,0:T(8,128)(2,1)} %constant.27.clone.inv_left) | copy-start | bytes 1179652
  15.6 2.9 %copy-start.9 = (f32[2,128,128]{2,1,0:T(8,128)S(1)}, f32[2,128,128]{2,1,0:T(8,128)}, u32[]{:S(2)}) copy-start(f32[2,128,128]{2,1,0:T(8,128)} %constant.29.clone.row_ref) | copy-start | bytes 393220
  15.6 2.9 %copy-start.10 = (f32[2,8,128]{2,1,0:T(8,128)S(1)}, f32[2,8,128]{2,1,0:T(8,128)}, u32[]{:S(2)}) copy-start(f32[2,8,128]{2,1,0:T(8,128)} %constant.28.clone.lane_ref) | copy-start | bytes 24580
  26.6 15.5 %all-to-all-start = ((f32[8,3,32,256]{3,2,1,0:T(8,128)}), f32[8,3,32,256]{3,2,1,0:T(8,128)S(1)}, u32[]{:S(2)}, u32[]{:S(2)}) async-start(f32[8,3,32,256]{3,2,1,0:T(8,128)} %get-tuple-element.36), calls=%async_computation | async-start | bytes 1572864 | tf_op jit(solution)/shard_map/all_to_all | solution.py:461
  30.9 11.6 %collective-permute-start.4 = (f32[2,320,128]{2,1,0:T(8,128)S(1)}, f32[2,320,128]{2,1,0:T(8,128)S(1)}, u32[]{:S(2)}, u32[]{:S(2)}) collective-permute-start(f32[2,320,128]{2,1,0:T(8,128)S(1)} %get-tuple-element.37), channel_id=1, source_target_pairs={{0,8},{8,16},{16,24},{1,9},{9,17},{17,25},{2,10},{10,18},{18,26},{... | collective-permute-start | bytes 983048 | tf_op jit(solution)/shard_map/ppermute | solution.py:21
  42.5 7.2 %collective-permute-start.5 = (f32[3,32,256]{2,1,0:T(8,128)S(1)}, f32[3,32,256]{2,1,0:T(8,128)S(1)}, u32[]{:S(2)}, u32[]{:S(2)}) collective-permute-start(f32[3,32,256]{2,1,0:T(8,128)S(1)} %reduce_sum.9.refs_2_), channel_id=1, source_target_pairs={{0,16},{8,24},{16,0},{24,8},{1,17},{9,25},{17,1},{25,9},{2,18},{10... | collective-permute-start | bytes 294920 | tf_op jit(solution)/shard_map/ppermute | solution.py:37
  42.5 10.4 %collective-permute-start.6 = (f32[3,32,256]{2,1,0:T(8,128)S(1)}, f32[3,32,256]{2,1,0:T(8,128)S(1)}, u32[]{:S(2)}, u32[]{:S(2)}) collective-permute-start(f32[3,32,256]{2,1,0:T(8,128)S(1)} %reduce_sum.9.refs_2_), channel_id=1, source_target_pairs={{0,24},{8,16},{16,8},{24,0},{1,25},{9,17},{17,9},{25,1},{2,26},{10... | collective-permute-start | bytes 294920 | tf_op jit(solution)/shard_map/ppermute | solution.py:37
  44.3 8.6 %collective-permute-start.7 = (f32[3,32,256]{2,1,0:T(8,128)S(1)}, f32[3,32,256]{2,1,0:T(8,128)S(1)}, u32[]{:S(2)}, u32[]{:S(2)}) collective-permute-start(f32[3,32,256]{2,1,0:T(8,128)S(1)} %reduce_sum.9.refs_2_), channel_id=1, source_target_pairs={{0,8},{8,0},{16,24},{24,16},{1,9},{9,1},{17,25},{25,17},{2,10},{10... | collective-permute-start | bytes 294920 | tf_op jit(solution)/shard_map/ppermute | solution.py:37
  47.8 9.3 %collective-permute-start.8 = (f32[2,320,128]{2,1,0:T(8,128)S(1)}, f32[2,320,128]{2,1,0:T(8,128)S(1)}, u32[]{:S(2)}, u32[]{:S(2)}) collective-permute-start(f32[2,320,128]{2,1,0:T(8,128)S(1)} %get-tuple-element.41), channel_id=1, source_target_pairs={{0,1},{1,2},{2,3},{3,4},{4,5},{5,6},{6,7},{8,9},{9,10},{10,11},{11... | collective-permute-start | bytes 983048 | tf_op jit(solution)/shard_map/ppermute | solution.py:21
  57.1 13.8 %all-to-all-start.1 = ((f32[8,2,32,256]{3,2,1,0:T(8,128)}), f32[8,2,32,256]{3,2,1,0:T(8,128)S(1)}, u32[]{:S(2)}, u32[]{:S(2)}) async-start(f32[8,2,32,256]{3,2,1,0:T(8,128)} %shard_map.117), calls=%async_computation.1 | async-start | bytes 1048576 | tf_op jit(solution)/shard_map/all_to_all | solution.py:477
  60.5 10.3 %collective-permute-start.9 = (f32[2,200,128]{2,1,0:T(8,128)S(1)}, f32[2,200,128]{2,1,0:T(8,128)S(1)}, u32[]{:S(2)}, u32[]{:S(2)}) collective-permute-start(f32[2,200,128]{2,1,0:T(8,128)S(1)} %get-tuple-element.44), channel_id=1, source_target_pairs={{0,9},{1,10},{2,11},{3,12},{4,13},{5,14},{6,15},{8,17},{9,18},{10,... | collective-permute-start | bytes 614408 | tf_op jit(solution)/shard_map/ppermute | solution.py:29
